TPU v7x, 32 devices: a whole 2x2x4 slice. The times are simulated.
32 devices in a mesh: grp: 2 (over y), off: 4 (over x, core), tile: 4 (over z).
Axes of the slice: x: 2, y: 2, z: 4, core: 2. Of those that a mesh axis runs over, the one named last changes fastest.
Arguments:
- traces: bfloat16 [4096, 4096], P(('grp', 'off', 'tile')), parts along dimension 0, may hold values from -6 to 6
- class_map: int32 [4096, 1], P(('grp', 'off', 'tile')), parts along dimension 0, may hold values from 0 to 3; in each aligned block of 128 rows (0 to 127, 128 to 255, ...) at most 48 rows name the same one
- mid_bins: int32 [4096], P(('grp', 'off', 'tile')), parts along dimension 0, may hold values from 0 to 127
- fold_count: int32 [8], P(('grp', 'off')), parts along dimension 0, may hold values from 1 to 8
- weight_tiles: bfloat16 [4, 4, 128, 128], P('off'), may hold values from -0.09375 to 0.09375
- apertures: int32 [64, 32], P(('grp', 'off', 'tile')), parts along dimension 0, may hold values from 0 to 4
Outputs:
- image_tiles: float32 [64, 128, 128], P(('grp', 'off', 'tile')), parts along dimension 0
There are 2 independent parts, one for each index of `grp`. A program takes and returns all parts, laid end to end along the dimension named above; an argument that names none is the same for every part. Nothing has to cross between parts.
Inputs may be any that keep to these rules, and one draw needn't show every extreme that they name: `class_map`: in the rows of one device each class is named by at most 48 traces; some class is named by exactly 48 traces on some device.
All inputs are finite; a program needn't handle non-finite values.
Results may differ from a plain program's by a relative error of at most 0.0025.
Values may be sent and summed in bfloat16 or wider, within the bound.
No kernel may reach another device: no remote copies, remote signals or barrier semaphores. Data moves between devices by JAX's collectives and lax.ppermute only.
A program may use at most 64 MiB of HBM per device.

v0:
```python
import jax
import jax.numpy as jnp
from jax import lax
from jax.sharding import PartitionSpec as P

BANDS = 32
BAND = 128
PTS = 128
MB = 128


def shards(traces, class_map, mid_bins, fold_count, weight_tiles, apertures):
    n_off = lax.axis_size("off")
    tr_dev = traces.shape[0]
    width = traces.shape[1]
    capacity = tr_dev // n_off + max(2, tr_dev // (2 * n_off))
    classes = class_map[:, 0]
    member = (classes[:, None] == jnp.arange(n_off, dtype=jnp.int32)[None, :]).astype(jnp.int32)
    ranks = jnp.sum((jnp.cumsum(member, axis=0) - 1) * member, axis=1)
    slots = classes * capacity + ranks
    source = (
        jnp.zeros((n_off * capacity,), jnp.int32).at[slots].set(jnp.arange(tr_dev, dtype=jnp.int32))
    )
    filled = jnp.zeros((n_off * capacity,), jnp.int32).at[slots].set(1)
    outgoing = traces[source].reshape(n_off, capacity, width)
    out_bins = jnp.where(filled > 0, mid_bins[source], -1).reshape(n_off, capacity)
    arrived, arrived_bins = (
        lax.all_to_all(outgoing, "off", split_axis=0, concat_axis=0, tiled=True),
        lax.all_to_all(out_bins, "off", split_axis=0, concat_axis=0, tiled=True),
    )
    arrived = arrived.reshape(n_off * capacity, width)
    arrived_bins = arrived_bins.reshape(n_off * capacity)
    binning = (jnp.arange(MB, dtype=jnp.int32)[:, None] == arrived_bins[None, :]).astype(
        jnp.bfloat16
    )
    stack = jnp.dot(binning, arrived, preferred_element_type=jnp.float32).astype(jnp.bfloat16)
    pattern = lax.all_gather(apertures, "off", axis=0, tiled=True)
    inverse = 1.0 / fold_count[0].astype(jnp.float32)
    tiles = weight_tiles[0]
    padded = jnp.concatenate([jnp.zeros((1, BAND, PTS), jnp.bfloat16), tiles], axis=0)

    def one_tile(row):
        chosen = padded[row].reshape(BANDS * BAND, PTS)
        return jnp.dot(stack, chosen, preferred_element_type=jnp.float32)

    return lax.psum_scatter(
        lax.map(one_tile, pattern) * inverse, "off", scatter_dimension=0, tiled=True
    )


def solution(mesh):
    placed = (
        P(("grp", "off", "tile"), None),
        P(("grp", "off", "tile"), None),
        P(("grp", "off", "tile")),
        P(("grp", "off")),
        P("off", None, None, None),
        P(("grp", "off", "tile"), None),
    )
    return jax.shard_map(
        shards,
        mesh=mesh,
        in_specs=placed,
        out_specs=P(("grp", "off", "tile"), None, None),
        check_vma=False,
    )
```

profile of v0, /device:TPU:0, one launch (start us, length us, event | category | flops | bytes accessed | tf_op | source)
XLA Modules:
  0.0 97.5 jit_solution(16871703396276375048)
XLA Ops:
  6.5 0.8 fusion.2
  7.5 0.8 select_reduce_fusion
  8.4 0.7 fusion.3
  9.0 1.0 scatter_custom_fusion.1
  10.1 1.0 %scatter_custom_fusion = s32[192]{0:T(256)S(1)} fusion(s32[128]{0:T(128)S(1)} %fusion.3, s32[128]{0:T(128)S(1)} %broadcast.49, s32[]{:T(128)} %copy.23), kind=kCustom, calls=%fused_computation.25 | custom fusion | bytes 772 | tf_op jit(solution)/shard_map/scatter | solution.py:24
  11.0 1.9 %gather_fusion.1 = s32[192]{0:T(256)S(1)} fusion(s32[128]{0:T(128)} %param.10, s32[1024]{0:T(1024)S(1)} %pad_clamp_fusion.1), kind=kCustom, calls=%fused_computation.1 | custom fusion | bytes 2304 | tf_op jit(solution)/shard_map/gather | solution.py:26
  12.9 0.7 all_to_all.9
  13.6 4.2 %all-to-all-start = ((s32[4,1,48]{2,1,0:T(1,128)}), s32[4,1,48]{2,1,0:T(1,128)S(1)}, u32[]{:S(2)}, u32[]{:S(2)}) async-start(s32[4,1,48]{2,1,0:T(1,128)} %all_to_all.9), calls=%async_computation | async-start | bytes 4096 | tf_op jit(solution)/shard_map/all_to_all | solution.py:29
  17.8 2.7 %gather_fusion.2 = bf16[192,4096]{1,0:T(8,128)(2,1)} fusion(bf16[128,4096]{1,0:T(8,128)(2,1)S(1)} %copy-done, s32[1024]{0:T(1024)S(1)} %pad_clamp_fusion.1), kind=kCustom, calls=%fused_computation.2 | custom fusion | bytes 3146496 | tf_op jit(solution)/shard_map/gather | solution.py:25
  20.5 1.0 %all-to-all-done = s32[4,1,48]{2,1,0:T(1,128)S(1)} async-done(((s32[4,1,48]{2,1,0:T(1,128)}), s32[4,1,48]{2,1,0:T(1,128)S(1)}, u32[]{:S(2)}, u32[]{:S(2)}) %all-to-all-start) | async-done | bytes 800 | tf_op jit(solution)/shard_map/all_to_all | solution.py:29
  21.5 3.7 %all-to-all-start.1 = ((bf16[4,48,4096]{2,1,0:T(8,128)(2,1)}), bf16[4,48,4096]{2,1,0:T(8,128)(2,1)S(1)}, u32[]{:S(2)}, u32[]{:S(2)}) async-start(bf16[4,48,4096]{2,1,0:T(8,128)(2,1)} %bitcast.11), calls=%async_computation.1 | async-start | bytes 3145728 | tf_op jit(solution)/shard_map/all_to_all | solution.py:28
  26.0 20.1 %all-gather = s32[4,2,32]{2,1,0:T(2,128)S(1)} all-gather(s32[1,2,32]{2,1,0:T(2,128)S(1)} %bitcast.43), channel_id=1, replica_groups=mesh['grp'=2,'off'=4,'tile'=4] {'off'}, dimensions={0}, use_global_device_ids=true | all-gather | bytes 1280 | tf_op jit(solution)/shard_map/all_gather | solution.py:37
  46.6 0.7 reduce.3
  47.4 1.2 %copy-done.1 = bf16[4,48,4096]{2,1,0:T(8,128)(2,1)} copy-done((bf16[4,48,4096]{2,1,0:T(8,128)(2,1)}, bf16[4,48,4096]{2,1,0:T(8,128)(2,1)S(1)}, u32[]{:S(2)}) %copy-start.1) | copy-done | bytes 1572888
  48.6 1.8 %convolution_convert_fusion = bf16[128,4096]{1,0:T(8,128)(2,1)S(1)} fusion(bf16[192,4096]{1,0:T(8,128)(2,1)} %bitcast.38, s32[192]{0:T(256)S(1)} %eq.35), kind=kOutput, calls=%fused_computation.10 | convolution fusion | flops 201875456 | bytes 2622208 | tf_op jit(solution)/shard_map/dot_general | solution.py:36
  50.4 15.8 %while.10 = (s32[]{:T(128)}, f32[8,128,128]{2,1,0:T(8,128)}, s32[8,32]{1,0:T(8,128)S(1)}, bf16[5,128,128]{2,1,0:T(8,128)(2,1)S(1)}, bf16[128,4096]{1,0:T(8,128)(2,1)S(1)}, /*index=5*/s32[]{:T(128)}) while((s32[]{:T(128)}, f32[8,128,128]{2,1,0:T(8,128)}, s32[8,32]{1,0:T(8,128)S(1)}, bf16[5,128,128]{2,1,0:T(8,128)(2,1)S(1)}, ...), condition=%wide.region_5.6_spmd, body=%wide.region_4.5_spmd.sunk | while | flops 134218848 | bytes 4527177 | solution.py:47
  50.4 0.7 gather_fusion
  52.4 0.7 gather_fusion
  53.7 0.6 constant_dynamic-update-slice_fusion.2
  54.4 0.7 gather_fusion
  56.3 0.7 gather_fusion
  57.7 0.6 constant_dynamic-update-slice_fusion.2
  58.3 0.7 gather_fusion
  59.6 0.6 constant_dynamic-update-slice_fusion.2
  60.3 0.7 gather_fusion
  61.6 0.6 constant_dynamic-update-slice_fusion.2
  62.3 0.7 gather_fusion
  63.6 0.6 constant_dynamic-update-slice_fusion.2
  64.2 0.7 gather_fusion
  65.6 0.6 constant_dynamic-update-slice_fusion.2
  66.2 1.9 %broadcast_multiply_fusion = f32[8,128,128]{2,1,0:T(8,128)} fusion(f32[8,128,128]{2,1,0:T(8,128)} %get-tuple-element.32, f32[]{:T(128)} %bitcast.13), kind=kLoop, calls=%fused_computation.11 | loop fusion | flops 131072 | bytes 1048580 | tf_op jit(solution)/shard_map/mul | solution.py:47
  68.1 22.6 %reduce-scatter.2.cloned.1.call-done = f32[2,128,128]{2,1,0:T(8,128)} async-done(((f32[8,128,128]{2,1,0:T(8,128)}), f32[2,128,128]{2,1,0:T(8,128)}) %reduce-scatter.2.cloned.1.call-update) | async-done | bytes 131088 | tf_op jit(solution)/shard_map/reduce_scatter | solution.py:46
  (54 shorter events, 6.7 us)
Async XLA Ops:
  6.5 11.3 %copy-start = (bf16[128,4096]{1,0:T(8,128)(2,1)S(1)}, bf16[128,4096]{1,0:T(8,128)(2,1)}, u32[]{:S(2)}) copy-start(bf16[128,4096]{1,0:T(8,128)(2,1)} %param.8) | copy-start | bytes 3145732
  13.6 7.9 %all-to-all-start = ((s32[4,1,48]{2,1,0:T(1,128)}), s32[4,1,48]{2,1,0:T(1,128)S(1)}, u32[]{:S(2)}, u32[]{:S(2)}) async-start(s32[4,1,48]{2,1,0:T(1,128)} %all_to_all.9), calls=%async_computation | async-start | bytes 4096 | tf_op jit(solution)/shard_map/all_to_all | solution.py:29
  21.5 4.4 %copy-start.2 = (bf16[1,4,128,128]{3,2,1,0:T(8,128)(2,1)S(1)}, bf16[1,4,128,128]{3,2,1,0:T(8,128)(2,1)}, u32[]{:S(2)}) copy-start(bf16[1,4,128,128]{3,2,1,0:T(8,128)(2,1)} %param.12) | copy-start | bytes 393220
  21.5 4.5 %copy-start.3 = (s32[2,32]{1,0:T(2,128)S(1)}, s32[2,32]{1,0:T(2,128)}, u32[]{:S(2)}) copy-start(s32[2,32]{1,0:T(2,128)} %param.13) | copy-start | bytes 772
  21.5 25.9 %all-to-all-start.1 = ((bf16[4,48,4096]{2,1,0:T(8,128)(2,1)}), bf16[4,48,4096]{2,1,0:T(8,128)(2,1)S(1)}, u32[]{:S(2)}, u32[]{:S(2)}) async-start(bf16[4,48,4096]{2,1,0:T(8,128)(2,1)} %bitcast.11), calls=%async_computation.1 | async-start | bytes 3145728 | tf_op jit(solution)/shard_map/all_to_all | solution.py:28
  25.2 65.5 %reduce-scatter.2.cloned.1.call-start = ((), (), s32[]{:S(2)}) async-start(), calls=%async_computation.3 | async-start | bytes 655360 | tf_op jit(solution)/shard_map/reduce_scatter | solution.py:46
  47.4 1.2 %copy-start.1 = (bf16[4,48,4096]{2,1,0:T(8,128)(2,1)}, bf16[4,48,4096]{2,1,0:T(8,128)(2,1)S(1)}, u32[]{:S(2)}) copy-start(bf16[4,48,4096]{2,1,0:T(8,128)(2,1)S(1)} %all-to-all-done.1) | copy-start | bytes 4718596
Sparse Core Ops, SparseCore 0:
  68.2 22.4 reduce-scatter.1
where the time goes:
time: 97.9 us; the launch traced here: 97.5 us
  waiting for transfers between devices  23.6 us (24%)
  local copies, waits for them, and re-layouts  20.7 us (21%)
  blocking collectives  20.1 us (21%)
  between operations  14.2 us (15%)
  starting transfers between devices  7.94 us (8%)
  matrix products  5.56 us (6%)
  other arithmetic  5.16 us (5%)
    reduce_scatter x1, waiting for transfers between devices, shards(): lax.psum_scatter(lax.map(one_tile, pattern) * inverse, 'off', scatter_dim...  22.6 us
    all_gather x1, blocking collectives, shards(): pattern = lax.all_gather(apertures, 'off', axis=0, tiled=True)  20.1 us
    gather x8, local copies, waits for them, and re-layouts, one_tile(): chosen = padded[row].reshape(BANDS * BAND, PTS)  5.98 us
    dynamic_update_slice x16, local copies, waits for them, and re-layouts, shards(): lax.map(one_tile, pattern) * inverse  5.76 us
    all_to_all x1, starting transfers between devices, shards(): lax.all_to_all(out_bins, 'off', split_axis=0, concat_axis=0, tiled=True)  4.21 us
    dot_general x8, matrix products, one_tile(): return jnp.dot(stack, chosen, preferred_element_type=jnp.float32)  3.72 us
    all_to_all x1, starting transfers between devices, shards(): lax.all_to_all(outgoing, 'off', split_axis=0, concat_axis=0, tiled=True)  3.69 us
    gather x1, local copies, waits for them, and re-layouts, shards(): outgoing = traces[source].reshape(n_off, capacity, width)  2.68 us
  transfers between devices with their start and end apart: 3, of which 2 were waited for; matrix products, arithmetic and copies ran while one was open for 4% of the time, Pallas kernels for 0%

commit v1 on v0

v1 whole, which is shorter than its diff:
```python
import functools

import jax
import jax.numpy as jnp
from jax import lax
from jax.experimental import pallas as pl
from jax.experimental.pallas import tpu as pltpu
from jax.sharding import PartitionSpec as P

BANDS = 32
BAND = 128
PTS = 128
MB = 128
NPAT = 4
SUB = 16
INFO = NPAT * BAND
F32 = jnp.float32
BF16 = jnp.bfloat16
VMEM = pl.BlockSpec(memory_space=pltpu.VMEM)
SMEM = pl.BlockSpec(memory_space=pltpu.SMEM)


def call(kernel, out, scratch=(), flops=0, moved=0):
    return functools.partial(
        pl.pallas_call,
        kernel,
        out_shape=out,
        scratch_shapes=scratch,
        compiler_params=pltpu.CompilerParams(vmem_limit_bytes=24 * 1024 * 1024),
        cost_estimate=pl.CostEstimate(flops=flops, bytes_accessed=moved, transcendentals=0),
    )


def pack_kernel(weight_ref, pattern_ref, fold_ref, packet_ref, info):
    tiles = pattern_ref.shape[0]
    packet_ref[0:INFO] = weight_ref[0].reshape(INFO, PTS)
    info[...] = jnp.zeros_like(info)
    info[0:tiles, 0:BANDS] = pattern_ref[...].astype(F32)
    info[tiles : tiles + 1] = jnp.full((1, PTS), fold_ref[0], jnp.int32).astype(F32)
    info[tiles + 1 : tiles + 2] = jnp.full((1, PTS), lax.axis_index("off"), jnp.int32).astype(F32)
    packet_ref[INFO:] = info[...].astype(BF16)


def band_sums(packet_ref, own_ref, near_ref, hi_ref, lo_ref, tiles):
    depth = BANDS * SUB
    pattern = packet_ref[INFO : INFO + SUB]
    band = lax.broadcasted_iota(jnp.int32, (PTS, depth), 0)
    column = lax.broadcasted_iota(jnp.int32, (PTS, depth), 1)
    spread = jnp.where(column // SUB == band, 1.0, 0.0).astype(BF16)
    wide = jnp.dot(pattern, spread, preferred_element_type=F32)
    row = lax.broadcasted_iota(jnp.int32, (NPAT * SUB, depth), 0)
    col = lax.broadcasted_iota(jnp.int32, (NPAT * SUB, depth), 1)
    value = (row // SUB + 1).astype(F32)
    same = row % SUB == col % SUB
    chosen = jnp.concatenate(
        [
            jnp.where(same & (jnp.broadcast_to(wide[g : g + 1], (NPAT * SUB, depth)) == value), 1.0, 0.0)
            for g in range(tiles)
        ],
        axis=0,
    ).astype(BF16)
    traces = own_ref.shape[0]
    for half, ref in enumerate((own_ref, near_ref)):
        for pair in range(traces // (2 * SUB)):
            at = pair * 2 * SUB
            block = jnp.concatenate(
                [
                    jnp.concatenate(
                        [
                            ref[at + n * SUB : at + (n + 1) * SUB, b * BAND : (b + 1) * BAND]
                            for n in range(2)
                        ],
                        axis=1,
                    )
                    for b in range(BANDS)
                ],
                axis=0,
            )
            sums = jnp.dot(chosen, block, preferred_element_type=F32)
            for n in range(2):
                for g in range(tiles):
                    for a in range(NPAT):
                        top = (g * NPAT + a) * SUB
                        slab = sums[top : top + SUB, n * BAND : (n + 1) * BAND]
                        hi = slab.astype(BF16)
                        lo = (slab - hi.astype(F32)).astype(BF16)
                        to = (g * 2 + half) * traces + at + n * SUB
                        hi_ref[to : to + SUB, a * BAND : (a + 1) * BAND] = hi
                        lo_ref[to : to + SUB, a * BAND : (a + 1) * BAND] = lo


def weigh(hi_ref, lo_ref, named, packets, tiles):
    total = None
    hi, lo = hi_ref[...], lo_ref[...]
    named = jnp.concatenate([named] * tiles, axis=0)
    for at in range(0, len(packets), 2):
        some = packets[at : at + 2]
        weights = jnp.concatenate([p[0:INFO] for p in some], axis=1) if len(some) > 1 else some[0][0:INFO]
        product = jnp.dot(hi, weights, preferred_element_type=F32) + jnp.dot(
            lo, weights, preferred_element_type=F32
        )
        for n, p in enumerate(some):
            info = p[INFO : INFO + SUB].astype(F32)
            scale = 1.0 / info[tiles : tiles + 1]
            mine = named == info[tiles + 1 : tiles + 2]
            part = jnp.where(mine, product[:, n * PTS : (n + 1) * PTS] * scale, 0.0)
            total = part if total is None else total + part
    return total


def bin_rows(total, binning, tiles):
    rows = binning.shape[1]
    wide = jnp.concatenate([total[g * rows : (g + 1) * rows] for g in range(tiles)], axis=1)
    hi = wide.astype(BF16)
    lo = (wide - hi.astype(F32)).astype(BF16)
    return jnp.dot(binning, hi, preferred_element_type=F32) + jnp.dot(
        binning, lo, preferred_element_type=F32
    )


def prepare_kernel(own_ref, near_ref, bins_ref, near_bins_ref, class_ref, near_class_ref,
                   packet_ref, near_packet_ref, binning_ref, named_ref, total_ref, hi_ref, lo_ref):
    tiles = hi_ref.shape[0] // named_ref.shape[0]
    traces = own_ref.shape[0]
    for half, (bins, classes) in enumerate(((bins_ref, class_ref), (near_bins_ref, near_class_ref))):
        at = half * traces
        place = lax.broadcasted_iota(jnp.int32, (MB, traces), 0)
        binning_ref[:, at : at + traces] = jnp.where(place == bins[...], 1.0, 0.0).astype(BF16)
        named_ref[at : at + traces] = jnp.broadcast_to(classes[...], (traces, traces)).astype(F32).T
    band_sums(packet_ref, own_ref, near_ref, hi_ref, lo_ref, tiles)
    total_ref[...] = weigh(hi_ref, lo_ref, named_ref[...], [packet_ref, near_packet_ref], tiles)


def begin_kernel(own_ref, near_ref, named_ref, pattern_ref, *refs):
    packets, (total_ref, hi_ref, lo_ref) = refs[:-3], refs[-3:]
    tiles = hi_ref.shape[0] // named_ref.shape[0]
    band_sums(pattern_ref, own_ref, near_ref, hi_ref, lo_ref, tiles)
    total_ref[...] = weigh(hi_ref, lo_ref, named_ref[...], packets, tiles)


def finish_kernel(total_ref, hi_ref, lo_ref, named_ref, binning_ref, *refs):
    packets, out_ref = refs[:-1], refs[-1]
    tiles = out_ref.shape[0]
    total = total_ref[...] + weigh(hi_ref, lo_ref, named_ref[...], packets, tiles)
    image = bin_rows(total, binning_ref[...], tiles)
    for g in range(tiles):
        out_ref[g] = image[:, g * PTS : (g + 1) * PTS].astype(out_ref.dtype)


def shards(traces, class_map, mid_bins, fold_count, weight_tiles, apertures):
    n_off = lax.axis_size("off")
    chips = n_off // 2
    tr_dev = traces.shape[0]
    tiles = apertures.shape[0]
    shape = jax.ShapeDtypeStruct

    def near(x):
        return lax.ppermute(x, "off", [(i, i ^ 1) for i in range(n_off)])

    def far(x, j):
        return lax.ppermute(
            x, "off", [(i, (i // 2 + j) % chips * 2 + i % 2) for i in range(n_off)]
        )

    packet = call(
        pack_kernel, shape((INFO + SUB, PTS), BF16), [pltpu.VMEM((SUB, PTS), F32)], moved=300000
    )(in_specs=[VMEM, VMEM, SMEM], out_specs=VMEM)(weight_tiles, apertures, fold_count)
    far_packets = [far(packet, j) for j in range(1, chips)]
    near_traces = near(traces)
    near_packet = near(packet)
    bins = mid_bins.reshape(1, tr_dev)
    classes = class_map.reshape(1, tr_dev)
    near_bins, near_classes = near(bins), near(classes)

    rows = 2 * tr_dev
    sums = shape((tiles * rows, NPAT * BAND), BF16)
    total = shape((tiles * rows, PTS), F32)
    work = 2 * tiles * rows * (NPAT * BAND) * PTS
    binning, named, own_total, own_hi, own_lo = call(
        prepare_kernel, (shape((MB, rows), BF16), shape((rows, PTS), F32), total, sums, sums),
        flops=10 * work, moved=8 << 20,
    )(in_specs=[VMEM] * 8, out_specs=[VMEM] * 5)(
        traces, near_traces, bins, near_bins, classes, near_classes, packet, near_packet
    )
    relayed = [near(p) for p in far_packets]
    received = []
    for j, p in enumerate(far_packets, 1):
        others = [packet, near_packet] + far_packets
        begun = call(begin_kernel, (total, sums, sums), flops=10 * work, moved=8 << 20)(
            in_specs=[VMEM] * (4 + len(others)), out_specs=[VMEM] * 3
        )(traces, near_traces, named, p, *others)
        part = call(finish_kernel, shape((tiles, MB, PTS), BF16), flops=4 * work, moved=2 << 20)(
            in_specs=[VMEM] * (5 + len(relayed)), out_specs=VMEM
        )(*begun, named, binning, *relayed)
        received.append(far(part, chips - j))
    rest = far_packets + relayed
    image = call(finish_kernel, shape((tiles, MB, PTS), F32), flops=6 * work, moved=2 << 20)(
        in_specs=[VMEM] * (5 + len(rest)), out_specs=VMEM
    )(own_total, own_hi, own_lo, named, binning, *rest)
    for part in received:
        image = image + part.astype(F32)
    return image


def solution(mesh):
    placed = (
        P(("grp", "off", "tile"), None),
        P(("grp", "off", "tile"), None),
        P(("grp", "off", "tile")),
        P(("grp", "off")),
        P("off", None, None, None),
        P(("grp", "off", "tile"), None),
    )
    return jax.shard_map(
        shards,
        mesh=mesh,
        in_specs=placed,
        out_specs=P(("grp", "off", "tile"), None, None),
        check_vma=False,
    )
```

time: 97.9 us -> 20.2 us (0.21)
  blocking collectives: 20.1 us -> 0 us
  local copies, waits for them, and re-layouts: 20.7 us -> 2.28 us
  waiting for transfers between devices: 23.6 us -> 6.74 us
  between operations: 14.2 us -> 0.72 us
  matrix products: 5.56 us -> 0 us
  other arithmetic: 5.16 us -> 0.67 us
  Pallas kernels: 0 us -> 3.59 us
  starting transfers between devices: 7.94 us -> 6.05 us
    reduce_scatter x1 -> x0, waiting for transfers between devices: 22.6 us -> none  [shards(): lax.psum_scatter(lax.map(one_tile, pattern) * inverse, 'off', scatter_dim...]
    all_gather x1 -> x0, blocking collectives: 20.1 us -> none  [shards(): pattern = lax.all_gather(apertures, 'off', axis=0, tiled=True)]
    gather x10 -> x0, local copies, waits for them, and re-layouts: 10.6 us -> none  [the longest x8 5.98 us: one_tile(): chosen = padded[row].reshape(BANDS * BAND, PTS)]
    all_to_all x2 -> x0, starting transfers between devices: 7.9 us -> none  [the longest x1 4.21 us: shards(): lax.all_to_all(out_bins, 'off', split_axis=0, concat_axis=0, tiled=True)]
    ppermute x0 -> x7, waiting for transfers between devices: none -> 6.74 us  [the longest x2 5.92 us: far(): lax.ppermute(x, 'off', [(i, (i // 2 + j) % chips * 2 + i % 2) for i in ra...]
    ppermute x0 -> x7, starting transfers between devices: none -> 6.05 us  [the longest x2 4.37 us: far(): lax.ppermute(x, 'off', [(i, (i // 2 + j) % chips * 2 + i % 2) for i in ra...]
    dynamic_update_slice x16 -> x0, local copies, waits for them, and re-layouts: 5.76 us -> none  [shards(): lax.map(one_tile, pattern) * inverse]
    dot_general x9 -> x0, matrix products: 5.56 us -> none  [the longest x8 3.72 us: one_tile(): return jnp.dot(stack, chosen, preferred_element_type=jnp.float32)]
  transfers between devices with their start and end apart: 3 -> 7, of which waited for: 2 -> 4; matrix products, arithmetic and copies ran while one was open for 4% -> 0% of each run, Pallas kernels for 0% -> 15%
where the time goes in v1:
time: 20.2 us; the launch traced here: 20.1 us
  waiting for transfers between devices  6.74 us (33%)
  starting transfers between devices  6.05 us (30%)
  Pallas kernels  3.59 us (18%)
  local copies, waits for them, and re-layouts  2.28 us (11%)
  between operations  0.72 us (4%)
  other arithmetic  0.67 us (3%)
    ppermute x2, waiting for transfers between devices, far(): lax.ppermute(x, 'off', [(i, (i // 2 + j) % chips * 2 + i % 2) for i in ra...  5.92 us
    ppermute x2, starting transfers between devices, far(): lax.ppermute(x, 'off', [(i, (i // 2 + j) % chips * 2 + i % 2) for i in ra...  4.37 us
    unnamed x10, local copies, waits for them, and re-layouts  2.28 us
    ppermute x5, starting transfers between devices, near(): return lax.ppermute(x, 'off', [(i, i ^ 1) for i in range(n_off)])  1.68 us
    pallas_call x1, Pallas kernels, shards(): call(begin_kernel, (total, sums, sums), flops=10 * work, moved=8 << 20)  1.25 us
    pallas_call x1, Pallas kernels, shards(): call(prepare_kernel, (shape((MB, rows), BF16), shape((rows, PTS), F32), t...  0.99 us
    ppermute x5, waiting for transfers between devices, near(): return lax.ppermute(x, 'off', [(i, i ^ 1) for i in range(n_off)])  0.83 us
    add x1, other arithmetic, shards(): image = image + part.astype(F32)  0.67 us
  transfers between devices with their start and end apart: 7, of which 4 were waited for; matrix products, arithmetic and copies ran while one was open for 0% of the time, Pallas kernels for 15%

profile of v1, /device:TPU:0, one launch (start us, length us, event | category | flops | bytes accessed | tf_op | source)
XLA Modules:
  0.0 20.1 jit_solution(1774864871852894858)
XLA Ops:
  0.0 0.0 copy-start.2
  0.0 0.5 %collective-permute-start = (bf16[128,4096]{1,0:T(8,128)(2,1)}, bf16[128,4096]{1,0:T(8,128)(2,1)S(1)}, u32[]{:S(2)}, u32[]{:S(2)}) collective-permute-start(bf16[128,4096]{1,0:T(8,128)(2,1)} %own_ref.3), channel_id=1, source_target_pairs={{0,4},{4,0},{8,12},{12,8},{1,5},{5,1},{9,13},{13,9},{2,6},{6,2},{1... | collective-permute-start | bytes 3145736 | tf_op jit(solution)/shard_map/ppermute | solution.py:158
  1.1 0.0 copy-done.2
  1.1 0.0 copy-start.1
  1.1 0.9 %copy-done.1 = bf16[1,4,128,128]{3,2,1,0:T(8,128)(2,1)S(1)} copy-done((bf16[1,4,128,128]{3,2,1,0:T(8,128)(2,1)S(1)}, bf16[1,4,128,128]{3,2,1,0:T(8,128)(2,1)}, u32[]{:S(2)}) %copy-start.1) | copy-done | bytes 131096
  2.0 0.0 copy-start.3
  2.1 2.6 %collective-permute-start.4 = (bf16[528,128]{1,0:T(8,128)(2,1)S(1)}, bf16[528,128]{1,0:T(8,128)(2,1)S(1)}, u32[]{:S(2)}, u32[]{:S(2)}) collective-permute-start(bf16[528,128]{1,0:T(8,128)(2,1)S(1)} %shard_map.64.packet_ref.refs_0_), channel_id=1, source_target_pairs={{0,8},{4,12},{8,0},{12,4},{1,9},{5,13},{9,1},{13,5},{2,10},{6,14},... | collective-permute-start | bytes 405512 | tf_op jit(solution)/shard_map/ppermute | solution.py:161
  4.6 0.2 %collective-permute-start.3 = (bf16[528,128]{1,0:T(8,128)(2,1)S(1)}, bf16[528,128]{1,0:T(8,128)(2,1)S(1)}, u32[]{:S(2)}, u32[]{:S(2)}) collective-permute-start(bf16[528,128]{1,0:T(8,128)(2,1)S(1)} %shard_map.64.packet_ref.refs_0_), channel_id=1, source_target_pairs={{0,4},{4,0},{8,12},{12,8},{1,5},{5,1},{9,13},{13,9},{2,6},{6,2},{1... | collective-permute-start | bytes 405512 | tf_op jit(solution)/shard_map/ppermute | solution.py:158
  4.8 4.0 %collective-permute-done.4.refs_0_.pattern_ref.refs_2_ = bf16[528,128]{1,0:T(8,128)(2,1)S(1)} collective-permute-done((bf16[528,128]{1,0:T(8,128)(2,1)S(1)}, bf16[528,128]{1,0:T(8,128)(2,1)S(1)}, u32[]{:S(2)}, u32[]{:S(2)}) %collective-permute-start.4) | collective-permute-done | bytes 135200 | tf_op jit(solution)/shard_map/ppermute | solution.py:161
  8.9 0.0 collective-permute-start.5
  8.9 0.0 copy-done.3
  8.9 0.0 copy-start.4
  8.9 0.5 %collective-permute-start.1 = (s32[1,128]{1,0:T(1,128)S(1)}, s32[1,128]{1,0:T(1,128)S(1)}, u32[]{:S(2)}, u32[]{:S(2)}) collective-permute-start(s32[1,128]{1,0:T(1,128)S(1)} %bitcast.2), channel_id=1, source_target_pairs={{0,4},{4,0},{8,12},{12,8},{1,5},{5,1},{9,13},{13,9},{2,6},{6,2},{1... | collective-permute-start | bytes 1544 | tf_op jit(solution)/shard_map/ppermute | solution.py:158
  9.4 0.1 copy-done.4
  9.5 0.5 %collective-permute-start.2 = (s32[1,128]{1,0:T(1,128)S(1)}, s32[1,128]{1,0:T(1,128)S(1)}, u32[]{:S(2)}, u32[]{:S(2)}) collective-permute-start(s32[1,128]{1,0:T(1,128)S(1)} %bitcast.4), channel_id=1, source_target_pairs={{0,4},{4,0},{8,12},{12,8},{1,5},{5,1},{9,13},{13,9},{2,6},{6,2},{1... | collective-permute-start | bytes 1544 | tf_op jit(solution)/shard_map/ppermute | solution.py:158
  10.0 0.2 collective-permute-done.1.near_bins_ref
  10.2 0.6 %collective-permute-done.2.near_class_ref = s32[1,128]{1,0:T(1,128)S(1)} collective-permute-done((s32[1,128]{1,0:T(1,128)S(1)}, s32[1,128]{1,0:T(1,128)S(1)}, u32[]{:S(2)}, u32[]{:S(2)}) %collective-permute-start.2) | collective-permute-done | bytes 544 | tf_op jit(solution)/shard_map/ppermute | solution.py:158
  10.9 0.0 collective-permute-done.3.near_packet_ref.refs_1_
  10.9 0.0 collective-permute-done.near_ref
  10.9 0.0 copy-start
  10.9 1.2 %copy-done = bf16[128,4096]{1,0:T(8,128)(2,1)S(1)} copy-done((bf16[128,4096]{1,0:T(8,128)(2,1)S(1)}, bf16[128,4096]{1,0:T(8,128)(2,1)}, u32[]{:S(2)}) %copy-start) | copy-done | bytes 1048600
  12.1 1.0 %shard_map.65 = (bf16[128,256]{1,0:T(8,128)(2,1)S(1)}, f32[256,128]{1,0:T(8,128)S(1)}, f32[512,128]{1,0:T(8,128)S(1)}, bf16[512,512]{1,0:T(8,128)(2,1)S(1)}, bf16[512,512]{1,0:T(8,128)(2,1)S(1)}) custom-call(bf16[128,4096]{1,0:T(8,128)(2,1)S(1)} %copy-done, bf16[128,4096]{1,0:T(8,128)(2,1)S(1)} %collective-permute-done.near_ref, s32[1,128]{1,0:T(1,128)S(1)} %bitcast.3, ...), custom_call_target="tpu_custom_call" | custom-call | flops 671088640 | bytes 8388608 | tf_op jit(solution)/shard_map/pallas_call | solution.py:179
  13.1 1.3 %shard_map.67 = (f32[512,128]{1,0:T(8,128)S(1)}, bf16[512,512]{1,0:T(8,128)(2,1)S(1)}, bf16[512,512]{1,0:T(8,128)(2,1)S(1)}) custom-call(bf16[128,4096]{1,0:T(8,128)(2,1)S(1)} %copy-done, bf16[128,4096]{1,0:T(8,128)(2,1)S(1)} %collective-permute-done.near_ref, f32[256,128]{1,0:T(8,128)S(1)} %get-tuple-element.16.named_ref, ...), custom_call_target="tpu_custom_call" | custom-call | flops 671088640 | bytes 8388608 | tf_op jit(solution)/shard_map/pallas_call | solution.py:189
  14.3 0.0 collective-permute-done.5.refs_1_.refs_0_
  14.3 0.7 %shard_map.68 = bf16[2,128,128]{2,1,0:T(8,128)(2,1)S(1)} custom-call(f32[512,128]{1,0:T(8,128)S(1)} %get-tuple-element.18.total_ref, bf16[512,512]{1,0:T(8,128)(2,1)S(1)} %get-tuple-element.19.hi_ref, bf16[512,512]{1,0:T(8,128)(2,1)S(1)} %get-tuple-element.20.lo_ref, f32[256,128]{1,0:T(8,128)S(1)} %get-tuple-element.16.named_ref, ...), custom_call_target="tpu_custom_call" | custom-call | flops 268435456 | bytes 2097152 | tf_op jit(solution)/shard_map/pallas_call | solution.py:192
  15.0 1.8 %collective-permute-start.6 = (bf16[2,128,128]{2,1,0:T(8,128)(2,1)S(1)}, bf16[2,128,128]{2,1,0:T(8,128)(2,1)S(1)}, u32[]{:S(2)}, u32[]{:S(2)}) collective-permute-start(bf16[2,128,128]{2,1,0:T(8,128)(2,1)S(1)} %shard_map.68), channel_id=1, source_target_pairs={{0,8},{4,12},{8,0},{12,4},{1,9},{5,13},{9,1},{13,5},{2,10},{6,14},... | collective-permute-start | bytes 196616 | tf_op jit(solution)/shard_map/ppermute | solution.py:161
  16.8 0.7 %shard_map.66 = f32[2,128,128]{2,1,0:T(8,128)S(1)} custom-call(f32[512,128]{1,0:T(8,128)S(1)} %get-tuple-element.13.total_ref, bf16[512,512]{1,0:T(8,128)(2,1)S(1)} %get-tuple-element.14.hi_ref, bf16[512,512]{1,0:T(8,128)(2,1)S(1)} %get-tuple-element.15.lo_ref, f32[256,128]{1,0:T(8,128)S(1)} %get-tuple-element.16.named_ref, ...), custom_call_target="tpu_custom_call" | custom-call | flops 402653184 | bytes 2097152 | tf_op jit(solution)/shard_map/pallas_call | solution.py:197
  17.5 1.9 %collective-permute-done.6 = bf16[2,128,128]{2,1,0:T(8,128)(2,1)S(1)} collective-permute-done((bf16[2,128,128]{2,1,0:T(8,128)(2,1)S(1)}, bf16[2,128,128]{2,1,0:T(8,128)(2,1)S(1)}, u32[]{:S(2)}, u32[]{:S(2)}) %collective-permute-start.6) | collective-permute-done | bytes 65568 | tf_op jit(solution)/shard_map/ppermute | solution.py:161
  19.4 0.7 %convert_add_fusion = f32[2,128,128]{2,1,0:T(8,128)} fusion(f32[2,128,128]{2,1,0:T(8,128)S(1)} %shard_map.66, bf16[2,128,128]{2,1,0:T(8,128)(2,1)S(1)} %collective-permute-done.6), kind=kLoop, calls=%fused_computation | loop fusion | flops 65536 | bytes 327680 | tf_op jit(solution)/shard_map/add | solution.py:201
  (1 shorter events, 0.0 us)
Async XLA Ops:
  0.0 1.1 %copy-start.2 = (s32[2,32]{1,0:T(2,128)S(1)}, s32[2,32]{1,0:T(2,128)}, u32[]{:S(2)}) copy-start(s32[2,32]{1,0:T(2,128)} %pattern_ref.1) | copy-start | bytes 772
  0.0 10.9 %collective-permute-start = (bf16[128,4096]{1,0:T(8,128)(2,1)}, bf16[128,4096]{1,0:T(8,128)(2,1)S(1)}, u32[]{:S(2)}, u32[]{:S(2)}) collective-permute-start(bf16[128,4096]{1,0:T(8,128)(2,1)} %own_ref.3), channel_id=1, source_target_pairs={{0,4},{4,0},{8,12},{12,8},{1,5},{5,1},{9,13},{13,9},{2,6},{6,2},{1... | collective-permute-start | bytes 3145736 | tf_op jit(solution)/shard_map/ppermute | solution.py:158
  1.1 0.9 %copy-start.1 = (bf16[1,4,128,128]{3,2,1,0:T(8,128)(2,1)S(1)}, bf16[1,4,128,128]{3,2,1,0:T(8,128)(2,1)}, u32[]{:S(2)}) copy-start(bf16[1,4,128,128]{3,2,1,0:T(8,128)(2,1)} %weight_ref.1) | copy-start | bytes 393220
  2.0 6.8 %copy-start.3 = (s32[128]{0:T(128)S(1)}, s32[128]{0:T(128)}, u32[]{:S(2)}) copy-start(s32[128]{0:T(128)} %param.8) | copy-start | bytes 1540
  2.1 6.8 %collective-permute-start.4 = (bf16[528,128]{1,0:T(8,128)(2,1)S(1)}, bf16[528,128]{1,0:T(8,128)(2,1)S(1)}, u32[]{:S(2)}, u32[]{:S(2)}) collective-permute-start(bf16[528,128]{1,0:T(8,128)(2,1)S(1)} %shard_map.64.packet_ref.refs_0_), channel_id=1, source_target_pairs={{0,8},{4,12},{8,0},{12,4},{1,9},{5,13},{9,1},{13,5},{2,10},{6,14},... | collective-permute-start | bytes 405512 | tf_op jit(solution)/shard_map/ppermute | solution.py:161
  4.6 6.2 %collective-permute-start.3 = (bf16[528,128]{1,0:T(8,128)(2,1)S(1)}, bf16[528,128]{1,0:T(8,128)(2,1)S(1)}, u32[]{:S(2)}, u32[]{:S(2)}) collective-permute-start(bf16[528,128]{1,0:T(8,128)(2,1)S(1)} %shard_map.64.packet_ref.refs_0_), channel_id=1, source_target_pairs={{0,4},{4,0},{8,12},{12,8},{1,5},{5,1},{9,13},{13,9},{2,6},{6,2},{1... | collective-permute-start | bytes 405512 | tf_op jit(solution)/shard_map/ppermute | solution.py:158
  8.9 5.5 %collective-permute-start.5 = (bf16[528,128]{1,0:T(8,128)(2,1)S(1)}, bf16[528,128]{1,0:T(8,128)(2,1)S(1)}, u32[]{:S(2)}, u32[]{:S(2)}) collective-permute-start(bf16[528,128]{1,0:T(8,128)(2,1)S(1)} %collective-permute-done.4.refs_0_.pattern_ref.refs_2_), channel_id=1, source_target_pairs={{0,4},{4,0},{8,12},{12,8},{1,5},{5,1},{9,13},{13,9},{2,6},{6,2},{1... | collective-permute-start | bytes 405512 | tf_op jit(solution)/shard_map/ppermute | solution.py:158
  8.9 0.7 %copy-start.4 = (s32[128,1]{0,1:T(1,128)S(1)}, s32[128,1]{0,1:T(1,128)}, u32[]{:S(2)}) copy-start(s32[128,1]{0,1:T(1,128)} %param.7) | copy-start | bytes 1540
  8.9 1.3 %collective-permute-start.1 = (s32[1,128]{1,0:T(1,128)S(1)}, s32[1,128]{1,0:T(1,128)S(1)}, u32[]{:S(2)}, u32[]{:S(2)}) collective-permute-start(s32[1,128]{1,0:T(1,128)S(1)} %bitcast.2), channel_id=1, source_target_pairs={{0,4},{4,0},{8,12},{12,8},{1,5},{5,1},{9,13},{13,9},{2,6},{6,2},{1... | collective-permute-start | bytes 1544 | tf_op jit(solution)/shard_map/ppermute | solution.py:158
  9.5 1.3 %collective-permute-start.2 = (s32[1,128]{1,0:T(1,128)S(1)}, s32[1,128]{1,0:T(1,128)S(1)}, u32[]{:S(2)}, u32[]{:S(2)}) collective-permute-start(s32[1,128]{1,0:T(1,128)S(1)} %bitcast.4), channel_id=1, source_target_pairs={{0,4},{4,0},{8,12},{12,8},{1,5},{5,1},{9,13},{13,9},{2,6},{6,2},{1... | collective-permute-start | bytes 1544 | tf_op jit(solution)/shard_map/ppermute | solution.py:158
  10.9 1.2 %copy-start = (bf16[128,4096]{1,0:T(8,128)(2,1)S(1)}, bf16[128,4096]{1,0:T(8,128)(2,1)}, u32[]{:S(2)}) copy-start(bf16[128,4096]{1,0:T(8,128)(2,1)} %own_ref.3) | copy-start | bytes 3145732
  15.0 4.4 %collective-permute-start.6 = (bf16[2,128,128]{2,1,0:T(8,128)(2,1)S(1)}, bf16[2,128,128]{2,1,0:T(8,128)(2,1)S(1)}, u32[]{:S(2)}, u32[]{:S(2)}) collective-permute-start(bf16[2,128,128]{2,1,0:T(8,128)(2,1)S(1)} %shard_map.68), channel_id=1, source_target_pairs={{0,8},{4,12},{8,0},{12,4},{1,9},{5,13},{9,1},{13,5},{2,10},{6,14},... | collective-permute-start | bytes 196616 | tf_op jit(solution)/shard_map/ppermute | solution.py:161

commit v2 on v1

v2 whole, which is shorter than its diff:
```python
import functools

import jax
import jax.numpy as jnp
from jax import lax
from jax.experimental import pallas as pl
from jax.experimental.pallas import tpu as pltpu
from jax.sharding import PartitionSpec as P

BANDS = 32
BAND = 128
PTS = 128
MB = 128
NPAT = 4
SUB = 16
DEPTH = NPAT * BAND
F32 = jnp.float32
BF16 = jnp.bfloat16
VMEM = pl.BlockSpec(memory_space=pltpu.VMEM)
SMEM = pl.BlockSpec(memory_space=pltpu.SMEM)


def call(kernel, out, scratch=(), flops=0, moved=0, limit=24 << 20):
    return functools.partial(
        pl.pallas_call,
        kernel,
        out_shape=out,
        scratch_shapes=scratch,
        compiler_params=pltpu.CompilerParams(vmem_limit_bytes=limit),
        cost_estimate=pl.CostEstimate(flops=flops, bytes_accessed=moved, transcendentals=0),
    )


def zero_kernel(out_ref):
    out_ref[...] = jnp.zeros_like(out_ref)


def info_kernel(zero_ref, fold_ref, bins_ref, class_ref, pattern_ref, info_ref, info):
    info[...] = jnp.broadcast_to(zero_ref[0:1], info.shape)
    info[0:1] = jnp.full((1, PTS), fold_ref[0], jnp.int32).astype(F32)
    info[1:2] = bins_ref[...].astype(F32)
    info[2:3] = class_ref[...].astype(F32)
    info[8 : 8 + pattern_ref.shape[0], 0:BANDS] = pattern_ref[...].astype(F32)
    info_ref[...] = info[...].astype(BF16)


def owner(chips, j, turn):
    me = lax.axis_index("off")
    core = lax.rem(me, 2)
    chip = lax.rem(me // 2 + chips - j, chips)
    return chip * 2 + (1 - core if turn else core)


def choice(info, tiles):
    depth = BANDS * SUB
    band = lax.broadcasted_iota(jnp.int32, (PTS, depth), 0)
    column = lax.broadcasted_iota(jnp.int32, (PTS, depth), 1)
    spread = jnp.where(column // SUB == band, 1.0, 0.0).astype(BF16)
    wide = jnp.dot(info, spread, preferred_element_type=F32)[8:SUB]
    row = lax.broadcasted_iota(jnp.int32, (NPAT * SUB, depth), 0)
    col = lax.broadcasted_iota(jnp.int32, (NPAT * SUB, depth), 1)
    value = (row // SUB + 1).astype(F32)
    same = row % SUB == col % SUB
    return jnp.concatenate(
        [
            jnp.where(same & (jnp.broadcast_to(wide[g : g + 1], (NPAT * SUB, depth)) == value), 1.0, 0.0)
            for g in range(tiles)
        ],
        axis=0,
    ).astype(BF16)


def band_sums(chosen, own_ref, near_ref, hi_ref, lo_ref, tiles):
    traces = own_ref.shape[0]
    for half, ref in enumerate((own_ref, near_ref)):
        for pair in range(traces // (2 * SUB)):
            at = pair * 2 * SUB
            block = jnp.concatenate(
                [
                    jnp.concatenate(
                        [
                            ref[at + n * SUB : at + (n + 1) * SUB, b * BAND : (b + 1) * BAND]
                            for n in range(2)
                        ],
                        axis=1,
                    )
                    for b in range(BANDS)
                ],
                axis=0,
            )
            sums = jnp.dot(chosen, block, preferred_element_type=F32)
            for n in range(2):
                for g in range(tiles):
                    for a in range(NPAT):
                        top = (g * NPAT + a) * SUB
                        slab = sums[top : top + SUB, n * BAND : (n + 1) * BAND]
                        hi = slab.astype(BF16)
                        lo = (slab - hi.astype(F32)).astype(BF16)
                        to = (g * 2 + half) * traces + at + n * SUB
                        hi_ref[to : to + SUB, a * BAND : (a + 1) * BAND] = hi
                        lo_ref[to : to + SUB, a * BAND : (a + 1) * BAND] = lo


def weigh(hi_ref, lo_ref, named, weights, owners, tiles):
    total = None
    hi, lo = hi_ref[...], lo_ref[...]
    named = jnp.concatenate([named] * tiles, axis=0)
    for at in range(0, len(weights), 2):
        some = [w[...] for w in weights[at : at + 2]]
        wide = jnp.concatenate(some, axis=1) if len(some) > 1 else some[0]
        product = jnp.dot(hi, wide, preferred_element_type=F32) + jnp.dot(
            lo, wide, preferred_element_type=F32
        )
        for n in range(len(some)):
            mine = named == owners[at + n].astype(F32)
            part = jnp.where(mine, product[:, n * PTS : (n + 1) * PTS], 0.0)
            total = part if total is None else total + part
    return total


def over_fold(named, infos, owners):
    scale = jnp.zeros_like(named)
    for info, held in zip(infos, owners):
        scale = jnp.where(named == held.astype(F32), 1.0 / info[0:SUB].astype(F32)[0:1], scale)
    return scale


def bin_rows(total, binning, tiles):
    rows = binning.shape[1]
    wide = jnp.concatenate([total[g * rows : (g + 1) * rows] for g in range(tiles)], axis=1)
    hi = wide.astype(BF16)
    lo = (wide - hi.astype(F32)).astype(BF16)
    return jnp.dot(binning, hi, preferred_element_type=F32) + jnp.dot(
        binning, lo, preferred_element_type=F32
    )


def choice_kernel(info_ref, near_info_ref, *refs):
    infos, (chosen_ref, binning_ref, named_ref) = refs[:-3], refs[-3:]
    traces = named_ref.shape[0] // 2
    for half, ref in enumerate((info_ref, near_info_ref)):
        at = half * traces
        info = ref[...].astype(F32)
        place = lax.broadcasted_iota(jnp.int32, (MB, traces), 0).astype(F32)
        binning_ref[:, at : at + traces] = jnp.where(place == info[1:2], 1.0, 0.0).astype(BF16)
        named_ref[at : at + traces] = jnp.broadcast_to(info[2:3], (traces, traces)).T
    infos = (info_ref,) + infos
    size = chosen_ref.shape[0] // len(infos)
    for n, info in enumerate(infos):
        chosen_ref[n * size : (n + 1) * size] = choice(info[...], size // (NPAT * SUB))


def begin_kernel(chips, j, own_ref, near_ref, named_ref, chosen_ref, *refs):
    weights, (total_ref, hi_ref, lo_ref) = refs[:-3], refs[-3:]
    tiles = hi_ref.shape[0] // named_ref.shape[0]
    size = tiles * NPAT * SUB
    band_sums(chosen_ref[j * size : (j + 1) * size], own_ref, near_ref, hi_ref, lo_ref, tiles)
    owners = [owner(chips, 0, 0), owner(chips, 0, 1)] + [owner(chips, n, 0) for n in range(1, chips)]
    total_ref[...] = weigh(hi_ref, lo_ref, named_ref[...], weights, owners, tiles)


def image_of(total, named, binning, infos, owners, out_ref):
    tiles = out_ref.shape[0]
    total = total * jnp.concatenate([over_fold(named, infos, owners)] * tiles, axis=0)
    image = bin_rows(total, binning, tiles)
    for g in range(tiles):
        out_ref[g] = image[:, g * PTS : (g + 1) * PTS].astype(out_ref.dtype)


def all_owners(chips):
    return [owner(chips, n, turn) for turn in range(2) for n in range(chips)]


def finish_kernel(chips, hi_ref, lo_ref, total_ref, named_ref, binning_ref, *refs):
    infos, weights, out_ref = refs[: 2 * chips], refs[2 * chips : -1], refs[-1]
    named, owners = named_ref[...], all_owners(chips)
    total = total_ref[...] + weigh(
        hi_ref, lo_ref, named, weights, owners[chips + 1 :], out_ref.shape[0]
    )
    image_of(total, named, binning_ref[...], infos, owners, out_ref)


def own_kernel(chips, own_ref, near_ref, chosen_ref, named_ref, binning_ref, *refs):
    infos, weights, (out_ref, hi_ref, lo_ref) = refs[: 2 * chips], refs[2 * chips : -3], refs[-3:]
    named, owners, tiles = named_ref[...], all_owners(chips), out_ref.shape[0]
    band_sums(chosen_ref[0 : tiles * NPAT * SUB], own_ref, near_ref, hi_ref, lo_ref, tiles)
    total = weigh(hi_ref, lo_ref, named, weights, owners, tiles)
    image_of(total, named, binning_ref[...], infos, owners, out_ref)


def shards(traces, class_map, mid_bins, fold_count, weight_tiles, apertures):
    n_off = lax.axis_size("off")
    chips = n_off // 2
    tr_dev = traces.shape[0]
    tiles = apertures.shape[0]
    shape = jax.ShapeDtypeStruct

    def near(x):
        return lax.ppermute(x, "off", [(i, i ^ 1) for i in range(n_off)])

    def far(x, j, turn=0):
        return lax.ppermute(
            x, "off", [(i, (i // 2 + j) % chips * 2 + (i % 2 ^ turn)) for i in range(n_off)]
        )

    hops = range(1, chips)
    weights = weight_tiles.reshape(DEPTH, PTS)
    zero = call(zero_kernel, shape((8, PTS), F32), flops=5 * 10**9)(in_specs=[], out_specs=VMEM)()
    fold_count, zero = lax.optimization_barrier((fold_count, zero))
    info = call(info_kernel, shape((SUB, PTS), BF16), [pltpu.VMEM((SUB, PTS), F32)], flops=5 * 10**9)(
        in_specs=[VMEM, SMEM, VMEM, VMEM, VMEM], out_specs=VMEM
    )(zero, fold_count, mid_bins.reshape(1, tr_dev), class_map.reshape(1, tr_dev), apertures)
    far_weights = [far(weights, j) for j in hops]
    far_infos = [far(info, j) for j in hops]
    near_traces, near_weights, near_info = near(traces), near(weights), near(info)

    rows = 2 * tr_dev
    sums = shape((tiles * rows, NPAT * BAND), BF16)
    total = shape((tiles * rows, PTS), F32)
    work = 2 * tiles * rows * (NPAT * BAND) * PTS
    chosen, binning, named = call(
        choice_kernel,
        (shape((chips * tiles * NPAT * SUB, BANDS * SUB), BF16), shape((MB, rows), BF16),
         shape((rows, PTS), F32)),
    )(in_specs=[VMEM] * (1 + chips), out_specs=[VMEM] * 3)(info, near_info, *far_infos)
    far_weights, chosen = lax.optimization_barrier((far_weights, chosen))
    relayed = [near(w) for w in far_weights]
    infos = [info] + far_infos + [near_info] + [near(x) for x in far_infos]
    received = []
    for j in hops:
        others = [weights, near_weights] + far_weights
        begun, *its_sums = call(functools.partial(begin_kernel, chips, j), (total, sums, sums))(
            in_specs=[VMEM] * (4 + len(others)), out_specs=[VMEM] * 3
        )(traces, near_traces, named, chosen, *others)
        rest = [begun, named, binning] + infos + relayed
        part = call(functools.partial(finish_kernel, chips), shape((tiles, MB, PTS), BF16))(
            in_specs=[VMEM] * (2 + len(rest)), out_specs=VMEM
        )(*its_sums, *rest)
        received.append(far(part, chips - j))
    rest = infos + [weights] + far_weights + [near_weights] + relayed
    image = call(
        functools.partial(own_kernel, chips), shape((tiles, MB, PTS), F32),
        [pltpu.VMEM(sums.shape, BF16)] * 2, flops=15 * work,
    )(in_specs=[VMEM] * (5 + len(rest)), out_specs=VMEM)(
        traces, near_traces, chosen, named, binning, *rest
    )
    for part in received:
        image = image + part.astype(F32)
    return image


def solution(mesh):
    placed = (
        P(("grp", "off", "tile"), None),
        P(("grp", "off", "tile"), None),
        P(("grp", "off", "tile")),
        P(("grp", "off")),
        P("off", None, None, None),
        P(("grp", "off", "tile"), None),
    )
    return jax.shard_map(
        shards,
        mesh=mesh,
        in_specs=placed,
        out_specs=P(("grp", "off", "tile"), None, None),
        check_vma=False,
    )
```

time: 20.2 us -> 15.8 us (0.78)
  waiting for transfers between devices: 6.74 us -> 4.74 us
  local copies, waits for them, and re-layouts: 2.28 us -> 0.91 us
  starting transfers between devices: 6.05 us -> 5.21 us
  Pallas kernels: 3.59 us -> 3.34 us
    unnamed x10, local copies, waits for them, and re-layouts: 2.28 us -> 0.91 us
    ppermute x2 -> x3, waiting for transfers between devices: 5.92 us -> 4.73 us  [far(): lax.ppermute(x, 'off', [(i, (i // 2 + j) % chips * 2 + (i % 2 ^ turn)) fo...]
    ppermute x5, waiting for transfers between devices: 0.83 us -> 0.01 us  [near(): return lax.ppermute(x, 'off', [(i, i ^ 1) for i in range(n_off)])]
    ppermute x2 -> x3, starting transfers between devices: 4.37 us -> 3.56 us  [far(): lax.ppermute(x, 'off', [(i, (i // 2 + j) % chips * 2 + (i % 2 ^ turn)) fo...]
    pallas_call x5 -> x6, Pallas kernels: 3.59 us -> 3.34 us  [the longest x1 1.32 us: shards(): call(functools.partial(own_kernel, chips), shape((tiles, MB, PTS), F32),...]
  transfers between devices with their start and end apart: 7 -> 8, of which waited for: 4 -> 2; matrix products, arithmetic and copies ran while one was open for 0% -> 0% of each run, Pallas kernels for 15% -> 17%
where the time goes in v2:
time: 15.8 us; the launch traced here: 15.6 us
  starting transfers between devices  5.21 us (33%)
  waiting for transfers between devices  4.74 us (30%)
  Pallas kernels  3.34 us (21%)
  local copies, waits for them, and re-layouts  0.91 us (6%)
  between operations  0.77 us (5%)
  other arithmetic  0.67 us (4%)
    ppermute x3, waiting for transfers between devices, far(): lax.ppermute(x, 'off', [(i, (i // 2 + j) % chips * 2 + (i % 2 ^ turn)) fo...  4.73 us
    ppermute x3, starting transfers between devices, far(): lax.ppermute(x, 'off', [(i, (i // 2 + j) % chips * 2 + (i % 2 ^ turn)) fo...  3.56 us
    ppermute x5, starting transfers between devices, near(): return lax.ppermute(x, 'off', [(i, i ^ 1) for i in range(n_off)])  1.65 us
    pallas_call x1, Pallas kernels, shards(): call(functools.partial(own_kernel, chips), shape((tiles, MB, PTS), F32),...  1.32 us
    pallas_call x1, Pallas kernels, shards(): call(functools.partial(begin_kernel, chips, j), (total, sums, sums))  1.15 us
    unnamed x10, local copies, waits for them, and re-layouts  0.91 us
    add x1, other arithmetic, shards(): image = image + part.astype(F32)  0.67 us
    pallas_call x1, Pallas kernels, shards(): call(functools.partial(finish_kernel, chips), shape((tiles, MB, PTS), BF16))  0.67 us
  transfers between devices with their start and end apart: 8, of which 2 were waited for; matrix products, arithmetic and copies ran while one was open for 0% of the time, Pallas kernels for 17%

profile of v2, /device:TPU:0, one launch (start us, length us, event | category | flops | bytes accessed | tf_op | source)
XLA Modules:
  0.0 15.6 jit_solution(17526269812562825593)
XLA Ops:
  0.0 2.9 %collective-permute-start.1 = (bf16[512,128]{1,0:T(8,128)(2,1)}, bf16[512,128]{1,0:T(8,128)(2,1)S(1)}, u32[]{:S(2)}, u32[]{:S(2)}) collective-permute-start(bf16[512,128]{1,0:T(8,128)(2,1)} %bitcast.3), channel_id=1, source_target_pairs={{0,8},{4,12},{8,0},{12,4},{1,9},{5,13},{9,1},{13,5},{2,10},{6,14},... | collective-permute-start | bytes 393224 | tf_op jit(solution)/shard_map/ppermute | solution.py:202
  2.9 0.0 collective-permute-start
  3.6 0.0 copy-start.4
  3.6 0.0 copy-start.2
  3.6 0.0 copy-start.3
  3.6 0.6 %copy-done.4 = s32[128,1]{0,1:T(1,128)S(1)} copy-done((s32[128,1]{0,1:T(1,128)S(1)}, s32[128,1]{0,1:T(1,128)}, u32[]{:S(2)}) %copy-start.4) | copy-done | bytes 536
  4.3 0.0 copy-done.2
  4.3 0.0 copy-done.3
  4.3 0.0 copy-start.1
  4.3 0.0 copy-start
  4.3 0.1 collective-permute-start.3
  4.4 0.6 %collective-permute-start.2 = (bf16[16,128]{1,0:T(8,128)(2,1)S(1)}, bf16[16,128]{1,0:T(8,128)(2,1)S(1)}, u32[]{:S(2)}, u32[]{:S(2)}) collective-permute-start(bf16[16,128]{1,0:T(8,128)(2,1)S(1)} %shard_map.65.info_ref.refs_0_), channel_id=1, source_target_pairs={{0,4},{4,0},{8,12},{12,8},{1,5},{5,1},{9,13},{13,9},{2,6},{6,2},{1... | collective-permute-start | bytes 12296 | tf_op jit(solution)/shard_map/ppermute | solution.py:199
  5.0 0.2 %copy-done.1 = bf16[1,4,128,128]{3,2,1,0:T(8,128)(2,1)S(1)} copy-done((bf16[1,4,128,128]{3,2,1,0:T(8,128)(2,1)S(1)}, bf16[1,4,128,128]{3,2,1,0:T(8,128)(2,1)}, u32[]{:S(2)}) %copy-start.1) | copy-done | bytes 131096
  5.2 0.5 %collective-permute-start.5 = (bf16[512,128]{1,0:T(8,128)(2,1)S(1)}, bf16[512,128]{1,0:T(8,128)(2,1)S(1)}, u32[]{:S(2)}, u32[]{:S(2)}) collective-permute-start(bf16[512,128]{1,0:T(8,128)(2,1)S(1)} %bitcast.4), channel_id=1, source_target_pairs={{0,4},{4,0},{8,12},{12,8},{1,5},{5,1},{9,13},{13,9},{2,6},{6,2},{1... | collective-permute-start | bytes 393224 | tf_op jit(solution)/shard_map/ppermute | solution.py:199
  5.7 2.3 %collective-permute-done.3.refs_0_.refs_1_ = bf16[16,128]{1,0:T(8,128)(2,1)S(1)} collective-permute-done((bf16[16,128]{1,0:T(8,128)(2,1)S(1)}, bf16[16,128]{1,0:T(8,128)(2,1)S(1)}, u32[]{:S(2)}, u32[]{:S(2)}) %collective-permute-start.3) | collective-permute-done | bytes 4128 | tf_op jit(solution)/shard_map/ppermute | solution.py:202
  8.0 0.0 collective-permute-done.2.near_info_ref.refs_2_
  8.0 0.2 %shard_map.66 = (bf16[256,512]{1,0:T(8,128)(2,1)S(1)}, bf16[128,256]{1,0:T(8,128)(2,1)S(1)}, f32[256,128]{1,0:T(8,128)S(1)}) custom-call(bf16[16,128]{1,0:T(8,128)(2,1)S(1)} %shard_map.65.info_ref.refs_0_, bf16[16,128]{1,0:T(8,128)(2,1)S(1)} %collective-permute-done.2.near_info_ref.refs_2_, bf16[16,128]{1,0:T(8,128)(2,1)S(1)} %collective-permute-done.3.refs_0_.refs_1_), custom_call_target="tpu_custom_call" | custom-call | tf_op jit(solution)/shard_map/pallas_call | solution.py:221
  8.2 0.0 collective-permute-done.1.refs_5_.refs_2_
  8.2 0.1 collective-permute-start.6
  8.3 0.5 %collective-permute-start.4 = (bf16[16,128]{1,0:T(8,128)(2,1)S(1)}, bf16[16,128]{1,0:T(8,128)(2,1)S(1)}, u32[]{:S(2)}, u32[]{:S(2)}) collective-permute-start(bf16[16,128]{1,0:T(8,128)(2,1)S(1)} %collective-permute-done.3.refs_0_.refs_1_), channel_id=1, source_target_pairs={{0,4},{4,0},{8,12},{12,8},{1,5},{5,1},{9,13},{13,9},{2,6},{6,2},{1... | collective-permute-start | bytes 12296 | tf_op jit(solution)/shard_map/ppermute | solution.py:199
  8.8 0.0 collective-permute-done.5.refs_6_.refs_1_
  8.8 0.0 collective-permute-done.near_ref
  8.8 0.0 copy-done
  8.8 1.1 %shard_map.68 = (f32[512,128]{1,0:T(8,128)S(1)}, bf16[512,512]{1,0:T(8,128)(2,1)S(1)}, bf16[512,512]{1,0:T(8,128)(2,1)S(1)}) custom-call(bf16[128,4096]{1,0:T(8,128)(2,1)S(1)} %copy-done, bf16[128,4096]{1,0:T(8,128)(2,1)S(1)} %collective-permute-done.near_ref, f32[256,128]{1,0:T(8,128)S(1)} %get-tuple-element.19.named_ref, ...), custom_call_target="tpu_custom_call" | custom-call | tf_op jit(solution)/shard_map/pallas_call | solution.py:232
  9.9 0.0 collective-permute-done.4.refs_3_
  10.0 0.0 collective-permute-done.6.refs_7_.refs_4_
  10.0 0.7 %shard_map.69 = bf16[2,128,128]{2,1,0:T(8,128)(2,1)S(1)} custom-call(bf16[512,512]{1,0:T(8,128)(2,1)S(1)} %get-tuple-element.22.hi_ref, bf16[512,512]{1,0:T(8,128)(2,1)S(1)} %get-tuple-element.23.lo_ref, f32[512,128]{1,0:T(8,128)S(1)} %get-tuple-element.24.total_ref, f32[256,128]{1,0:T(8,128)S(1)} %get-tuple-element.19.named_ref, ...), custom_call_target="tpu_custom_call" | custom-call | tf_op jit(solution)/shard_map/pallas_call | solution.py:236
  10.6 0.6 %collective-permute-start.7 = (bf16[2,128,128]{2,1,0:T(8,128)(2,1)S(1)}, bf16[2,128,128]{2,1,0:T(8,128)(2,1)S(1)}, u32[]{:S(2)}, u32[]{:S(2)}) collective-permute-start(bf16[2,128,128]{2,1,0:T(8,128)(2,1)S(1)} %shard_map.69), channel_id=1, source_target_pairs={{0,8},{4,12},{8,0},{12,4},{1,9},{5,13},{9,1},{13,5},{2,10},{6,14},... | collective-permute-start | bytes 196616 | tf_op jit(solution)/shard_map/ppermute | solution.py:202
  11.2 1.3 %shard_map.67 = f32[2,128,128]{2,1,0:T(8,128)S(1)} custom-call(bf16[128,4096]{1,0:T(8,128)(2,1)S(1)} %copy-done, bf16[128,4096]{1,0:T(8,128)(2,1)S(1)} %collective-permute-done.near_ref, bf16[256,512]{1,0:T(8,128)(2,1)S(1)} %get-tuple-element.18.chosen_ref, f32[256,128]{1,0:T(8,128)S(1)} %get-tuple-element.19.named_ref, ...), custom_call_target="tpu_custom_call" | custom-call | flops 1006632960 | tf_op jit(solution)/shard_map/pallas_call | solution.py:241
  12.5 2.5 %collective-permute-done.7 = bf16[2,128,128]{2,1,0:T(8,128)(2,1)S(1)} collective-permute-done((bf16[2,128,128]{2,1,0:T(8,128)(2,1)S(1)}, bf16[2,128,128]{2,1,0:T(8,128)(2,1)S(1)}, u32[]{:S(2)}, u32[]{:S(2)}) %collective-permute-start.7) | collective-permute-done | bytes 65568 | tf_op jit(solution)/shard_map/ppermute | solution.py:202
  15.0 0.7 %convert_add_fusion = f32[2,128,128]{2,1,0:T(8,128)} fusion(f32[2,128,128]{2,1,0:T(8,128)S(1)} %shard_map.67, bf16[2,128,128]{2,1,0:T(8,128)(2,1)S(1)} %collective-permute-done.7), kind=kLoop, calls=%fused_computation | loop fusion | flops 65536 | bytes 327680 | tf_op jit(solution)/shard_map/add | solution.py:248
  (2 shorter events, 0.0 us)
Async XLA Ops:
  0.0 8.2 %collective-permute-start.1 = (bf16[512,128]{1,0:T(8,128)(2,1)}, bf16[512,128]{1,0:T(8,128)(2,1)S(1)}, u32[]{:S(2)}, u32[]{:S(2)}) collective-permute-start(bf16[512,128]{1,0:T(8,128)(2,1)} %bitcast.3), channel_id=1, source_target_pairs={{0,8},{4,12},{8,0},{12,4},{1,9},{5,13},{9,1},{13,5},{2,10},{6,14},... | collective-permute-start | bytes 393224 | tf_op jit(solution)/shard_map/ppermute | solution.py:202
  2.9 5.8 %collective-permute-start = (bf16[128,4096]{1,0:T(8,128)(2,1)}, bf16[128,4096]{1,0:T(8,128)(2,1)S(1)}, u32[]{:S(2)}, u32[]{:S(2)}) collective-permute-start(bf16[128,4096]{1,0:T(8,128)(2,1)} %own_ref.3), channel_id=1, source_target_pairs={{0,4},{4,0},{8,12},{12,8},{1,5},{5,1},{9,13},{13,9},{2,6},{6,2},{1... | collective-permute-start | bytes 3145736 | tf_op jit(solution)/shard_map/ppermute | solution.py:199
  3.6 0.7 %copy-start.4 = (s32[128,1]{0,1:T(1,128)S(1)}, s32[128,1]{0,1:T(1,128)}, u32[]{:S(2)}) copy-start(s32[128,1]{0,1:T(1,128)} %param.7) | copy-start | bytes 1540
  3.6 0.7 %copy-start.2 = (s32[2,32]{1,0:T(2,128)S(1)}, s32[2,32]{1,0:T(2,128)}, u32[]{:S(2)}) copy-start(s32[2,32]{1,0:T(2,128)} %pattern_ref.1) | copy-start | bytes 772
  3.6 0.7 %copy-start.3 = (s32[128]{0:T(128)S(1)}, s32[128]{0:T(128)}, u32[]{:S(2)}) copy-start(s32[128]{0:T(128)} %param.8) | copy-start | bytes 1540
  4.3 0.9 %copy-start.1 = (bf16[1,4,128,128]{3,2,1,0:T(8,128)(2,1)S(1)}, bf16[1,4,128,128]{3,2,1,0:T(8,128)(2,1)}, u32[]{:S(2)}) copy-start(bf16[1,4,128,128]{3,2,1,0:T(8,128)(2,1)} %param.10) | copy-start | bytes 393220
  4.3 4.5 %copy-start = (bf16[128,4096]{1,0:T(8,128)(2,1)S(1)}, bf16[128,4096]{1,0:T(8,128)(2,1)}, u32[]{:S(2)}) copy-start(bf16[128,4096]{1,0:T(8,128)(2,1)} %own_ref.3) | copy-start | bytes 3145732
  4.3 3.7 %collective-permute-start.3 = (bf16[16,128]{1,0:T(8,128)(2,1)S(1)}, bf16[16,128]{1,0:T(8,128)(2,1)S(1)}, u32[]{:S(2)}, u32[]{:S(2)}) collective-permute-start(bf16[16,128]{1,0:T(8,128)(2,1)S(1)} %shard_map.65.info_ref.refs_0_), channel_id=1, source_target_pairs={{0,8},{4,12},{8,0},{12,4},{1,9},{5,13},{9,1},{13,5},{2,10},{6,14},... | collective-permute-start | bytes 12296 | tf_op jit(solution)/shard_map/ppermute | solution.py:202
  4.4 3.6 %collective-permute-start.2 = (bf16[16,128]{1,0:T(8,128)(2,1)S(1)}, bf16[16,128]{1,0:T(8,128)(2,1)S(1)}, u32[]{:S(2)}, u32[]{:S(2)}) collective-permute-start(bf16[16,128]{1,0:T(8,128)(2,1)S(1)} %shard_map.65.info_ref.refs_0_), channel_id=1, source_target_pairs={{0,4},{4,0},{8,12},{12,8},{1,5},{5,1},{9,13},{13,9},{2,6},{6,2},{1... | collective-permute-start | bytes 12296 | tf_op jit(solution)/shard_map/ppermute | solution.py:199
  5.2 3.6 %collective-permute-start.5 = (bf16[512,128]{1,0:T(8,128)(2,1)S(1)}, bf16[512,128]{1,0:T(8,128)(2,1)S(1)}, u32[]{:S(2)}, u32[]{:S(2)}) collective-permute-start(bf16[512,128]{1,0:T(8,128)(2,1)S(1)} %bitcast.4), channel_id=1, source_target_pairs={{0,4},{4,0},{8,12},{12,8},{1,5},{5,1},{9,13},{13,9},{2,6},{6,2},{1... | collective-permute-start | bytes 393224 | tf_op jit(solution)/shard_map/ppermute | solution.py:199
  8.2 1.8 %collective-permute-start.6 = (bf16[512,128]{1,0:T(8,128)(2,1)S(1)}, bf16[512,128]{1,0:T(8,128)(2,1)S(1)}, u32[]{:S(2)}, u32[]{:S(2)}) collective-permute-start(bf16[512,128]{1,0:T(8,128)(2,1)S(1)} %collective-permute-done.1.refs_5_.refs_2_), channel_id=1, source_target_pairs={{0,4},{4,0},{8,12},{12,8},{1,5},{5,1},{9,13},{13,9},{2,6},{6,2},{1... | collective-permute-start | bytes 393224 | tf_op jit(solution)/shard_map/ppermute | solution.py:199
  8.3 1.7 %collective-permute-start.4 = (bf16[16,128]{1,0:T(8,128)(2,1)S(1)}, bf16[16,128]{1,0:T(8,128)(2,1)S(1)}, u32[]{:S(2)}, u32[]{:S(2)}) collective-permute-start(bf16[16,128]{1,0:T(8,128)(2,1)S(1)} %collective-permute-done.3.refs_0_.refs_1_), channel_id=1, source_target_pairs={{0,4},{4,0},{8,12},{12,8},{1,5},{5,1},{9,13},{13,9},{2,6},{6,2},{1... | collective-permute-start | bytes 12296 | tf_op jit(solution)/shard_map/ppermute | solution.py:199
  10.6 4.3 %collective-permute-start.7 = (bf16[2,128,128]{2,1,0:T(8,128)(2,1)S(1)}, bf16[2,128,128]{2,1,0:T(8,128)(2,1)S(1)}, u32[]{:S(2)}, u32[]{:S(2)}) collective-permute-start(bf16[2,128,128]{2,1,0:T(8,128)(2,1)S(1)} %shard_map.69), channel_id=1, source_target_pairs={{0,8},{4,12},{8,0},{12,4},{1,9},{5,13},{9,1},{13,5},{2,10},{6,14},... | collective-permute-start | bytes 196616 | tf_op jit(solution)/shard_map/ppermute | solution.py:202

commit v3 on v2

v3 whole, which is shorter than its diff:
```python
import functools

import jax
import jax.numpy as jnp
from jax import lax
from jax.experimental import pallas as pl
from jax.experimental.pallas import tpu as pltpu
from jax.sharding import PartitionSpec as P

BANDS = 32
BAND = 128
PTS = 128
MB = 128
NPAT = 4
SUB = 16
DEPTH = NPAT * BAND
INFO_COST = 5 * 10**8
BEGIN_COST = 11 * 10**8
SUMS_COST = 4 * 10**8
FACTS_COST = 10**9
F32 = jnp.float32
BF16 = jnp.bfloat16
VMEM = pl.BlockSpec(memory_space=pltpu.VMEM)
ANY = pl.BlockSpec(memory_space=pl.ANY)
SMEM = pl.BlockSpec(memory_space=pltpu.SMEM)


def call(kernel, out, scratch=(), flops=0, moved=0, limit=24 << 20):
    return functools.partial(
        pl.pallas_call,
        kernel,
        out_shape=out,
        scratch_shapes=scratch,
        compiler_params=pltpu.CompilerParams(vmem_limit_bytes=limit),
        cost_estimate=pl.CostEstimate(flops=flops, bytes_accessed=moved, transcendentals=0),
    )


def facts_kernel(fold_ref, pattern_ref, facts_ref, facts):
    facts[...] = jnp.zeros_like(facts)
    facts[0:1] = jnp.full((1, PTS), fold_ref[0], jnp.int32).astype(F32)
    facts[8 : 8 + pattern_ref.shape[0], 0:BANDS] = pattern_ref[...].astype(F32)
    facts_ref[...] = facts[...].astype(BF16)


def info_kernel(after_ref, facts_ref, bins_ref, class_ref, info_ref, info):
    info[...] = facts_ref[...].astype(F32)
    info[1:2] = bins_ref[...].astype(F32)
    info[2:3] = class_ref[...].astype(F32)
    info_ref[...] = info[...].astype(BF16)


def owner(chips, j, turn):
    me = lax.axis_index("off")
    core = lax.rem(me, 2)
    chip = lax.rem(me // 2 + chips - j, chips)
    return chip * 2 + (1 - core if turn else core)


def choice(pattern):
    depth = BANDS * SUB
    tiles = pattern.shape[0]
    band = lax.broadcasted_iota(jnp.int32, (BANDS, depth), 0)
    column = lax.broadcasted_iota(jnp.int32, (BANDS, depth), 1)
    spread = jnp.where(column // SUB == band, 1.0, 0.0).astype(BF16)
    padded = jnp.concatenate([pattern] * (8 // tiles), axis=0).astype(BF16)
    wide = jnp.dot(padded, spread, preferred_element_type=F32)
    row = lax.broadcasted_iota(jnp.int32, (NPAT * SUB, depth), 0)
    col = lax.broadcasted_iota(jnp.int32, (NPAT * SUB, depth), 1)
    value = (row // SUB + 1).astype(F32)
    same = row % SUB == col % SUB
    return jnp.concatenate(
        [
            jnp.where(same & (jnp.broadcast_to(wide[g : g + 1], (NPAT * SUB, depth)) == value), 1.0, 0.0)
            for g in range(tiles)
        ],
        axis=0,
    ).astype(BF16)


def band_sums(chosen, own_ref, near_ref, hi_ref, lo_ref, tiles):
    traces = own_ref.shape[0]
    for half, ref in enumerate((own_ref, near_ref)):
        for pair in range(traces // (2 * SUB)):
            at = pair * 2 * SUB
            block = jnp.concatenate(
                [
                    jnp.concatenate(
                        [
                            ref[at + n * SUB : at + (n + 1) * SUB, b * BAND : (b + 1) * BAND]
                            for n in range(2)
                        ],
                        axis=1,
                    )
                    for b in range(BANDS)
                ],
                axis=0,
            )
            sums = jnp.dot(chosen, block, preferred_element_type=F32)
            for n in range(2):
                for g in range(tiles):
                    for a in range(NPAT):
                        top = (g * NPAT + a) * SUB
                        slab = sums[top : top + SUB, n * BAND : (n + 1) * BAND]
                        hi = slab.astype(BF16)
                        lo = (slab - hi.astype(F32)).astype(BF16)
                        to = (g * 2 + half) * traces + at + n * SUB
                        hi_ref[to : to + SUB, a * BAND : (a + 1) * BAND] = hi
                        lo_ref[to : to + SUB, a * BAND : (a + 1) * BAND] = lo


def weigh(hi_ref, lo_ref, named, weights, owners, tiles):
    total = None
    hi, lo = hi_ref[...], lo_ref[...]
    named = jnp.concatenate([named] * tiles, axis=0)
    for at in range(0, len(weights), 2):
        some = [w[0:DEPTH] for w in weights[at : at + 2]]
        wide = jnp.concatenate(some, axis=1) if len(some) > 1 else some[0]
        product = jnp.dot(hi, wide, preferred_element_type=F32) + jnp.dot(
            lo, wide, preferred_element_type=F32
        )
        for n in range(len(some)):
            mine = named == owners[at + n].astype(F32)
            part = jnp.where(mine, product[:, n * PTS : (n + 1) * PTS], 0.0)
            total = part if total is None else total + part
    return total


def over_fold(named, infos, owners):
    scale = jnp.zeros_like(named)
    for info, held in zip(infos, owners):
        scale = jnp.where(named == held.astype(F32), 1.0 / info[...].astype(F32)[0:1], scale)
    return scale


def bin_rows(total, binning, tiles):
    rows = binning.shape[1]
    wide = jnp.concatenate([total[g * rows : (g + 1) * rows] for g in range(tiles)], axis=1)
    hi = wide.astype(BF16)
    lo = (wide - hi.astype(F32)).astype(BF16)
    return jnp.dot(binning, hi, preferred_element_type=F32) + jnp.dot(
        binning, lo, preferred_element_type=F32
    )


def sums_kernel(own_ref, near_ref, facts_ref, hi_ref, lo_ref):
    tiles = hi_ref.shape[0] // (2 * own_ref.shape[0])
    chosen = choice(facts_ref[...].astype(F32)[8 : 8 + tiles, 0:BANDS])
    band_sums(chosen, own_ref, near_ref, hi_ref, lo_ref, tiles)


def begin_kernel(chips, hi_ref, lo_ref, weight_ref, near_weight_ref, *refs):
    infos, (total_ref, scale_ref, named_ref, binning_ref) = refs[:-4], refs[-4:]
    traces = named_ref.shape[0] // 2
    for half in range(2):
        at = half * traces
        info = infos[half * chips][...].astype(F32)
        place = lax.broadcasted_iota(jnp.int32, (MB, traces), 0).astype(F32)
        binning_ref[:, at : at + traces] = jnp.where(place == info[1:2], 1.0, 0.0).astype(BF16)
        named_ref[at : at + traces] = jnp.broadcast_to(info[2:3], (traces, traces)).T
    named, tiles = named_ref[...], hi_ref.shape[0] // named_ref.shape[0]
    owners = [owner(chips, 0, 0), owner(chips, 0, 1)]
    total_ref[...] = weigh(hi_ref, lo_ref, named, [weight_ref, near_weight_ref], owners, tiles)
    scale_ref[...] = over_fold(named, infos, all_owners(chips))


def image_of(total, scale, binning, out_ref):
    tiles = out_ref.shape[0]
    total = total * jnp.concatenate([scale] * tiles, axis=0)
    image = bin_rows(total, binning, tiles)
    for g in range(tiles):
        out_ref[g] = image[:, g * PTS : (g + 1) * PTS].astype(out_ref.dtype)


def all_owners(chips):
    return [owner(chips, n, turn) for turn in range(2) for n in range(chips)]


def finish_kernel(chips, hi_ref, lo_ref, total_ref, named_ref, scale_ref, binning_ref, *refs):
    weights, out_ref = refs[:-1], refs[-1]
    owners = [owner(chips, n, turn) for turn in range(2) for n in range(1, chips)]
    total = total_ref[...] + weigh(hi_ref, lo_ref, named_ref[...], weights, owners, out_ref.shape[0])
    image_of(total, scale_ref[...], binning_ref[...], out_ref)


def own_kernel(chips, own_ref, near_ref, pattern_ref, named_ref, scale_ref, binning_ref, *refs):
    weights, (out_ref, hi_ref, lo_ref) = refs[:-3], refs[-3:]
    tiles = out_ref.shape[0]
    chosen = choice(pattern_ref[...].astype(F32))
    band_sums(chosen, own_ref, near_ref, hi_ref, lo_ref, tiles)
    total = weigh(hi_ref, lo_ref, named_ref[...], weights, all_owners(chips), tiles)
    image_of(total, scale_ref[...], binning_ref[...], out_ref)


def shards(traces, class_map, mid_bins, fold_count, weight_tiles, apertures):
    n_off = lax.axis_size("off")
    chips = n_off // 2
    tr_dev = traces.shape[0]
    tiles = apertures.shape[0]
    shape = jax.ShapeDtypeStruct

    def near(x):
        return lax.ppermute(x, "off", [(i, i ^ 1) for i in range(n_off)])

    def far(x, j, turn=0):
        return lax.ppermute(
            x, "off", [(i, (i // 2 + j) % chips * 2 + (i % 2 ^ turn)) for i in range(n_off)]
        )

    hops = range(1, chips)
    weights = weight_tiles.reshape(DEPTH, PTS)
    far_weights = [far(weights, j) for j in hops]
    block = shape((SUB, PTS), BF16)
    facts = call(facts_kernel, block, [pltpu.VMEM(block.shape, F32)], flops=FACTS_COST)(
        in_specs=[SMEM, VMEM], out_specs=VMEM
    )(fold_count, apertures)
    far_facts = [far(facts, j) for j in hops]
    cross_facts = [far(facts, j, 1) for j in hops]
    near_traces, near_weights = near(traces), near(weights)
    info = call(info_kernel, block, [pltpu.VMEM(block.shape, F32)], flops=INFO_COST)(
        in_specs=[ANY] + [VMEM] * 3, out_specs=VMEM
    )(near_traces, facts, mid_bins.reshape(1, tr_dev), class_map.reshape(1, tr_dev))
    near_info = near(info)

    rows = 2 * tr_dev
    sums = shape((tiles * rows, NPAT * BAND), BF16)
    total = shape((tiles * rows, PTS), F32)
    by_row = shape((rows, PTS), F32)
    work = 2 * tiles * rows * (NPAT * BAND) * PTS
    far_weights, info = lax.optimization_barrier((far_weights, info))
    relayed = [near(w) for w in far_weights]
    infos = [info] + far_facts + [near_info] + cross_facts
    all_begun = []
    for j in hops:
        its_sums = call(sums_kernel, (sums, sums), flops=SUMS_COST)(
            in_specs=[VMEM] * 3, out_specs=[VMEM] * 2
        )(traces, near_traces, far_facts[j - 1])
        begun, scale, named, binning = call(
            functools.partial(begin_kernel, chips),
            (total, by_row, by_row, shape((MB, rows), BF16)), flops=BEGIN_COST,
        )(in_specs=[VMEM] * (4 + len(infos)), out_specs=[VMEM] * 4)(
            *its_sums, weights, near_weights, *infos
        )
        all_begun.append((begun, *its_sums))
    received = []
    for j in hops:
        begun, *its_sums = all_begun[j - 1]
        rest = [begun, named, scale, binning] + far_weights + relayed
        part = call(functools.partial(finish_kernel, chips), shape((tiles, MB, PTS), BF16))(
            in_specs=[VMEM] * (2 + len(rest)), out_specs=VMEM
        )(*its_sums, *rest)
        received.append(far(part, chips - j))
    rest = [weights] + far_weights + [near_weights] + relayed
    image = call(
        functools.partial(own_kernel, chips), shape((tiles, MB, PTS), F32),
        [pltpu.VMEM(sums.shape, BF16)] * 2, flops=15 * work,
    )(in_specs=[VMEM] * (6 + len(rest)), out_specs=VMEM)(
        traces, near_traces, apertures, named, scale, binning, *rest
    )
    for part in received:
        image = image + part.astype(F32)
    return image


def solution(mesh):
    placed = (
        P(("grp", "off", "tile"), None),
        P(("grp", "off", "tile"), None),
        P(("grp", "off", "tile")),
        P(("grp", "off")),
        P("off", None, None, None),
        P(("grp", "off", "tile"), None),
    )
    return jax.shard_map(
        shards,
        mesh=mesh,
        in_specs=placed,
        out_specs=P(("grp", "off", "tile"), None, None),
        check_vma=False,
    )
```

time: 15.8 us -> 14.6 us (0.924)
  waiting for transfers between devices: 4.74 us -> 2.58 us
  starting transfers between devices: 5.21 us -> 7.25 us
  local copies, waits for them, and re-layouts: 0.91 us -> 0.02 us
    ppermute x3 -> x4, starting transfers between devices: 3.56 us -> 6.12 us  [far(): lax.ppermute(x, 'off', [(i, (i // 2 + j) % chips * 2 + (i % 2 ^ turn)) fo...]
    ppermute x3 -> x4, waiting for transfers between devices: 4.73 us -> 2.51 us  [far(): lax.ppermute(x, 'off', [(i, (i // 2 + j) % chips * 2 + (i % 2 ^ turn)) fo...]
    unnamed x10, local copies, waits for them, and re-layouts: 0.91 us -> 0.02 us
    ppermute x5 -> x4, starting transfers between devices: 1.65 us -> 1.13 us  [near(): return lax.ppermute(x, 'off', [(i, i ^ 1) for i in range(n_off)])]
    pallas_call x4, Pallas kernels: 1.36 us -> 1.1 us  [the longest x1 0.64 us: shards(): call(sums_kernel, (sums, sums), flops=SUMS_COST)]
  transfers between devices with their start and end apart: 8 -> 8, of which waited for: 2 -> 4; matrix products, arithmetic and copies ran while one was open for 0% -> 0% of each run, Pallas kernels for 17% -> 17%
where the time goes in v3:
time: 14.6 us; the launch traced here: 14.5 us
  starting transfers between devices  7.25 us (50%)
  Pallas kernels  3.2 us (22%)
  waiting for transfers between devices  2.58 us (18%)
  between operations  0.77 us (5%)
  other arithmetic  0.67 us (5%)
    ppermute x4, starting transfers between devices, far(): lax.ppermute(x, 'off', [(i, (i // 2 + j) % chips * 2 + (i % 2 ^ turn)) fo...  6.12 us
    ppermute x4, waiting for transfers between devices, far(): lax.ppermute(x, 'off', [(i, (i // 2 + j) % chips * 2 + (i % 2 ^ turn)) fo...  2.51 us
    pallas_call x1, Pallas kernels, shards(): call(functools.partial(own_kernel, chips), shape((tiles, MB, PTS), F32),...  1.42 us
    ppermute x4, starting transfers between devices, near(): return lax.ppermute(x, 'off', [(i, i ^ 1) for i in range(n_off)])  1.13 us
    pallas_call x1, Pallas kernels, shards(): call(functools.partial(finish_kernel, chips), shape((tiles, MB, PTS), BF16))  0.67 us
    add x1, other arithmetic, shards(): image = image + part.astype(F32)  0.67 us
    pallas_call x1, Pallas kernels, shards(): call(sums_kernel, (sums, sums), flops=SUMS_COST)  0.64 us
    pallas_call x1, Pallas kernels, shards(): call(functools.partial(begin_kernel, chips), (total, by_row, by_row, shap...  0.44 us
  transfers between devices with their start and end apart: 8, of which 4 were waited for; matrix products, arithmetic and copies ran while one was open for 0% of the time, Pallas kernels for 17%

profile of v3, /device:TPU:0, one launch (start us, length us, event | category | flops | bytes accessed | tf_op | source)
XLA Modules:
  0.0 14.5 jit_solution(5954364913086680170)
XLA Ops:
  0.0 0.5 %collective-permute-start = (bf16[128,4096]{1,0:T(8,128)(2,1)}, bf16[128,4096]{1,0:T(8,128)(2,1)S(1)}, u32[]{:S(2)}, u32[]{:S(2)}) collective-permute-start(bf16[128,4096]{1,0:T(8,128)(2,1)} %own_ref.3), channel_id=1, source_target_pairs={{0,4},{4,0},{8,12},{12,8},{1,5},{5,1},{9,13},{13,9},{2,6},{6,2},{1... | collective-permute-start | bytes 3145736 | tf_op jit(solution)/shard_map/ppermute | solution.py:203
  0.5 0.0 copy-start.2
  0.5 2.5 %collective-permute-start.3 = (bf16[512,128]{1,0:T(8,128)(2,1)}, bf16[512,128]{1,0:T(8,128)(2,1)S(1)}, u32[]{:S(2)}, u32[]{:S(2)}) collective-permute-start(bf16[512,128]{1,0:T(8,128)(2,1)} %bitcast.3), channel_id=1, source_target_pairs={{0,8},{4,12},{8,0},{12,4},{1,9},{5,13},{9,1},{13,5},{2,10},{6,14},... | collective-permute-start | bytes 393224 | tf_op jit(solution)/shard_map/ppermute | solution.py:206
  3.0 0.2 %collective-permute-start.2 = (bf16[512,128]{1,0:T(8,128)(2,1)}, bf16[512,128]{1,0:T(8,128)(2,1)S(1)}, u32[]{:S(2)}, u32[]{:S(2)}) collective-permute-start(bf16[512,128]{1,0:T(8,128)(2,1)} %bitcast.4), channel_id=1, source_target_pairs={{0,4},{4,0},{8,12},{12,8},{1,5},{5,1},{9,13},{13,9},{2,6},{6,2},{1... | collective-permute-start | bytes 393224 | tf_op jit(solution)/shard_map/ppermute | solution.py:203
  3.8 0.0 copy-done.2
  3.8 0.0 copy-start.3
  3.8 0.0 copy-start.4
  3.9 0.0 copy-start
  3.9 0.3 %collective-permute-start.1 = (bf16[16,128]{1,0:T(8,128)(2,1)S(1)}, bf16[16,128]{1,0:T(8,128)(2,1)S(1)}, u32[]{:S(2)}, u32[]{:S(2)}) collective-permute-start(bf16[16,128]{1,0:T(8,128)(2,1)S(1)} %shard_map.64.facts_ref), channel_id=1, source_target_pairs={{0,8},{4,12},{8,0},{12,4},{1,9},{5,13},{9,1},{13,5},{2,10},{6,14},... | collective-permute-start | bytes 12296 | tf_op jit(solution)/shard_map/ppermute | solution.py:206
  4.2 1.4 %collective-permute-start.5 = (bf16[16,128]{1,0:T(8,128)(2,1)S(1)}, bf16[16,128]{1,0:T(8,128)(2,1)S(1)}, u32[]{:S(2)}, u32[]{:S(2)}) collective-permute-start(bf16[16,128]{1,0:T(8,128)(2,1)S(1)} %shard_map.64.facts_ref), channel_id=1, source_target_pairs={{0,12},{4,8},{8,4},{12,0},{1,13},{5,9},{9,5},{13,1},{2,14},{6,10},... | collective-permute-start | bytes 12296 | tf_op jit(solution)/shard_map/ppermute | solution.py:206
  5.6 0.0 collective-permute-done.near_ref.after_ref
  5.6 0.0 copy-done.3
  5.6 0.0 copy-done.4
  5.7 0.0 copy-start.1
  5.7 0.5 %collective-permute-start.4 = (bf16[16,128]{1,0:T(8,128)(2,1)S(1)}, bf16[16,128]{1,0:T(8,128)(2,1)S(1)}, u32[]{:S(2)}, u32[]{:S(2)}) collective-permute-start(bf16[16,128]{1,0:T(8,128)(2,1)S(1)} %shard_map.66.refs_0_), channel_id=1, source_target_pairs={{0,4},{4,0},{8,12},{12,8},{1,5},{5,1},{9,13},{13,9},{2,6},{6,2},{1... | collective-permute-start | bytes 12296 | tf_op jit(solution)/shard_map/ppermute | solution.py:203
  6.2 1.2 %collective-permute-done.3.refs_1_.refs_0_ = bf16[512,128]{1,0:T(8,128)(2,1)S(1)} collective-permute-done((bf16[512,128]{1,0:T(8,128)(2,1)}, bf16[512,128]{1,0:T(8,128)(2,1)S(1)}, u32[]{:S(2)}, u32[]{:S(2)}) %collective-permute-start.3) | collective-permute-done | bytes 131104 | tf_op jit(solution)/shard_map/ppermute | solution.py:206
  7.4 0.0 collective-permute-start.6
  7.4 0.1 collective-permute-done.1.facts_ref.refs_1_
  7.6 0.0 copy-done
  7.6 0.6 %shard_map.65 = (bf16[512,512]{1,0:T(8,128)(2,1)S(1)}, bf16[512,512]{1,0:T(8,128)(2,1)S(1)}) custom-call(bf16[128,4096]{1,0:T(8,128)(2,1)S(1)} %copy-done, bf16[128,4096]{1,0:T(8,128)(2,1)S(1)} %collective-permute-done.near_ref.after_ref, bf16[16,128]{1,0:T(8,128)(2,1)S(1)} %collective-permute-done.1.facts_ref.refs_1_), custom_call_target="tpu_custom_call" | custom-call | flops 400000000 | tf_op jit(solution)/shard_map/pallas_call | solution.py:235
  8.2 0.0 collective-permute-done.5.refs_3_
  8.2 0.0 collective-permute-done.2.near_weight_ref.refs_2_
  8.2 0.0 collective-permute-done.4.refs_2_
  8.2 0.0 copy-done.1
  8.2 0.4 %shard_map.67 = (f32[512,128]{1,0:T(8,128)S(1)}, f32[256,128]{1,0:T(8,128)S(1)}, f32[256,128]{1,0:T(8,128)S(1)}, bf16[128,256]{1,0:T(8,128)(2,1)S(1)}) custom-call(bf16[512,512]{1,0:T(8,128)(2,1)S(1)} %get-tuple-element.13.hi_ref, bf16[512,512]{1,0:T(8,128)(2,1)S(1)} %get-tuple-element.14.lo_ref, bf16[512,128]{1,0:T(8,128)(2,1)S(1)} %bitcast.5, ...), custom_call_target="tpu_custom_call" | custom-call | flops 1100000000 | tf_op jit(solution)/shard_map/pallas_call | solution.py:238
  8.7 0.1 collective-permute-done.6.refs_3_.refs_1_
  8.8 0.7 %shard_map.69 = bf16[2,128,128]{2,1,0:T(8,128)(2,1)S(1)} custom-call(bf16[512,512]{1,0:T(8,128)(2,1)S(1)} %get-tuple-element.13.hi_ref, bf16[512,512]{1,0:T(8,128)(2,1)S(1)} %get-tuple-element.14.lo_ref, f32[512,128]{1,0:T(8,128)S(1)} %get-tuple-element.20.total_ref, f32[256,128]{1,0:T(8,128)S(1)} %get-tuple-element.16.named_ref, ...), custom_call_target="tpu_custom_call" | custom-call | tf_op jit(solution)/shard_map/pallas_call | solution.py:249
  9.4 1.8 %collective-permute-start.7 = (bf16[2,128,128]{2,1,0:T(8,128)(2,1)S(1)}, bf16[2,128,128]{2,1,0:T(8,128)(2,1)S(1)}, u32[]{:S(2)}, u32[]{:S(2)}) collective-permute-start(bf16[2,128,128]{2,1,0:T(8,128)(2,1)S(1)} %shard_map.69), channel_id=1, source_target_pairs={{0,8},{4,12},{8,0},{12,4},{1,9},{5,13},{9,1},{13,5},{2,10},{6,14},... | collective-permute-start | bytes 196616 | tf_op jit(solution)/shard_map/ppermute | solution.py:206
  11.2 1.4 %shard_map.68 = f32[2,128,128]{2,1,0:T(8,128)S(1)} custom-call(bf16[128,4096]{1,0:T(8,128)(2,1)S(1)} %copy-done, bf16[128,4096]{1,0:T(8,128)(2,1)S(1)} %collective-permute-done.near_ref.after_ref, s32[2,32]{1,0:T(2,128)S(1)} %copy-done.2, f32[256,128]{1,0:T(8,128)S(1)} %get-tuple-element.16.named_ref, f32[256,128]{1,0:T(8,128)S(1)} %get-tuple-element.17.scale_ref, ...), custom_call_target="tpu_custom_call" | custom-call | flops 1006632960 | tf_op jit(solution)/shard_map/pallas_call | solution.py:254
  12.7 1.1 %collective-permute-done.7 = bf16[2,128,128]{2,1,0:T(8,128)(2,1)S(1)} collective-permute-done((bf16[2,128,128]{2,1,0:T(8,128)(2,1)S(1)}, bf16[2,128,128]{2,1,0:T(8,128)(2,1)S(1)}, u32[]{:S(2)}, u32[]{:S(2)}) %collective-permute-start.7) | collective-permute-done | bytes 65568 | tf_op jit(solution)/shard_map/ppermute | solution.py:206
  13.8 0.7 %convert_add_fusion = f32[2,128,128]{2,1,0:T(8,128)} fusion(f32[2,128,128]{2,1,0:T(8,128)S(1)} %shard_map.68, bf16[2,128,128]{2,1,0:T(8,128)(2,1)S(1)} %collective-permute-done.7), kind=kLoop, calls=%fused_computation | loop fusion | flops 65536 | bytes 327680 | tf_op jit(solution)/shard_map/add | solution.py:261
  (2 shorter events, 0.0 us)
Async XLA Ops:
  0.0 5.6 %collective-permute-start = (bf16[128,4096]{1,0:T(8,128)(2,1)}, bf16[128,4096]{1,0:T(8,128)(2,1)S(1)}, u32[]{:S(2)}, u32[]{:S(2)}) collective-permute-start(bf16[128,4096]{1,0:T(8,128)(2,1)} %own_ref.3), channel_id=1, source_target_pairs={{0,4},{4,0},{8,12},{12,8},{1,5},{5,1},{9,13},{13,9},{2,6},{6,2},{1... | collective-permute-start | bytes 3145736 | tf_op jit(solution)/shard_map/ppermute | solution.py:203
  0.5 3.4 %copy-start.2 = (s32[2,32]{1,0:T(2,128)S(1)}, s32[2,32]{1,0:T(2,128)}, u32[]{:S(2)}) copy-start(s32[2,32]{1,0:T(2,128)} %pattern_ref.3) | copy-start | bytes 772
  0.5 7.0 %collective-permute-start.3 = (bf16[512,128]{1,0:T(8,128)(2,1)}, bf16[512,128]{1,0:T(8,128)(2,1)S(1)}, u32[]{:S(2)}, u32[]{:S(2)}) collective-permute-start(bf16[512,128]{1,0:T(8,128)(2,1)} %bitcast.3), channel_id=1, source_target_pairs={{0,8},{4,12},{8,0},{12,4},{1,9},{5,13},{9,1},{13,5},{2,10},{6,14},... | collective-permute-start | bytes 393224 | tf_op jit(solution)/shard_map/ppermute | solution.py:206
  3.0 5.2 %collective-permute-start.2 = (bf16[512,128]{1,0:T(8,128)(2,1)}, bf16[512,128]{1,0:T(8,128)(2,1)S(1)}, u32[]{:S(2)}, u32[]{:S(2)}) collective-permute-start(bf16[512,128]{1,0:T(8,128)(2,1)} %bitcast.4), channel_id=1, source_target_pairs={{0,4},{4,0},{8,12},{12,8},{1,5},{5,1},{9,13},{13,9},{2,6},{6,2},{1... | collective-permute-start | bytes 393224 | tf_op jit(solution)/shard_map/ppermute | solution.py:203
  3.8 1.8 %copy-start.3 = (s32[128]{0:T(128)S(1)}, s32[128]{0:T(128)}, u32[]{:S(2)}) copy-start(s32[128]{0:T(128)} %param.8) | copy-start | bytes 1540
  3.8 1.8 %copy-start.4 = (s32[128,1]{0,1:T(1,128)S(1)}, s32[128,1]{0,1:T(1,128)}, u32[]{:S(2)}) copy-start(s32[128,1]{0,1:T(1,128)} %param.7) | copy-start | bytes 1540
  3.9 3.7 %copy-start = (bf16[128,4096]{1,0:T(8,128)(2,1)S(1)}, bf16[128,4096]{1,0:T(8,128)(2,1)}, u32[]{:S(2)}) copy-start(bf16[128,4096]{1,0:T(8,128)(2,1)} %own_ref.3) | copy-start | bytes 3145732
  3.9 3.7 %collective-permute-start.1 = (bf16[16,128]{1,0:T(8,128)(2,1)S(1)}, bf16[16,128]{1,0:T(8,128)(2,1)S(1)}, u32[]{:S(2)}, u32[]{:S(2)}) collective-permute-start(bf16[16,128]{1,0:T(8,128)(2,1)S(1)} %shard_map.64.facts_ref), channel_id=1, source_target_pairs={{0,8},{4,12},{8,0},{12,4},{1,9},{5,13},{9,1},{13,5},{2,10},{6,14},... | collective-permute-start | bytes 12296 | tf_op jit(solution)/shard_map/ppermute | solution.py:206
  4.2 4.0 %collective-permute-start.5 = (bf16[16,128]{1,0:T(8,128)(2,1)S(1)}, bf16[16,128]{1,0:T(8,128)(2,1)S(1)}, u32[]{:S(2)}, u32[]{:S(2)}) collective-permute-start(bf16[16,128]{1,0:T(8,128)(2,1)S(1)} %shard_map.64.facts_ref), channel_id=1, source_target_pairs={{0,12},{4,8},{8,4},{12,0},{1,13},{5,9},{9,5},{13,1},{2,14},{6,10},... | collective-permute-start | bytes 12296 | tf_op jit(solution)/shard_map/ppermute | solution.py:206
  5.7 2.6 %copy-start.1 = (bf16[1,4,128,128]{3,2,1,0:T(8,128)(2,1)S(1)}, bf16[1,4,128,128]{3,2,1,0:T(8,128)(2,1)}, u32[]{:S(2)}) copy-start(bf16[1,4,128,128]{3,2,1,0:T(8,128)(2,1)} %param.10) | copy-start | bytes 393220
  5.7 2.5 %collective-permute-start.4 = (bf16[16,128]{1,0:T(8,128)(2,1)S(1)}, bf16[16,128]{1,0:T(8,128)(2,1)S(1)}, u32[]{:S(2)}, u32[]{:S(2)}) collective-permute-start(bf16[16,128]{1,0:T(8,128)(2,1)S(1)} %shard_map.66.refs_0_), channel_id=1, source_target_pairs={{0,4},{4,0},{8,12},{12,8},{1,5},{5,1},{9,13},{13,9},{2,6},{6,2},{1... | collective-permute-start | bytes 12296 | tf_op jit(solution)/shard_map/ppermute | solution.py:203
  7.4 1.3 %collective-permute-start.6 = (bf16[512,128]{1,0:T(8,128)(2,1)S(1)}, bf16[512,128]{1,0:T(8,128)(2,1)S(1)}, u32[]{:S(2)}, u32[]{:S(2)}) collective-permute-start(bf16[512,128]{1,0:T(8,128)(2,1)S(1)} %collective-permute-done.3.refs_1_.refs_0_), channel_id=1, source_target_pairs={{0,4},{4,0},{8,12},{12,8},{1,5},{5,1},{9,13},{13,9},{2,6},{6,2},{1... | collective-permute-start | bytes 393224 | tf_op jit(solution)/shard_map/ppermute | solution.py:203
  9.4 4.4 %collective-permute-start.7 = (bf16[2,128,128]{2,1,0:T(8,128)(2,1)S(1)}, bf16[2,128,128]{2,1,0:T(8,128)(2,1)S(1)}, u32[]{:S(2)}, u32[]{:S(2)}) collective-permute-start(bf16[2,128,128]{2,1,0:T(8,128)(2,1)S(1)} %shard_map.69), channel_id=1, source_target_pairs={{0,8},{4,12},{8,0},{12,4},{1,9},{5,13},{9,1},{13,5},{2,10},{6,14},... | collective-permute-start | bytes 196616 | tf_op jit(solution)/shard_map/ppermute | solution.py:206

commit v4 on v3

--- a/solution.py
+++ b/solution.py
@@ -14,10 +14,12 @@
 NPAT = 4
 SUB = 16
 DEPTH = NPAT * BAND
-INFO_COST = 5 * 10**8
+INFO_COST = 7 * 10**8
 BEGIN_COST = 11 * 10**8
-SUMS_COST = 4 * 10**8
-FACTS_COST = 10**9
+SUMS_COST = 0
+FACTS_COST = 15 * 10**7
+CHOICE_COST = 7 * 10**9
+RELAY_COST = 4 * 10**9
 F32 = jnp.float32
 BF16 = jnp.bfloat16
 VMEM = pl.BlockSpec(memory_space=pltpu.VMEM)
@@ -43,11 +45,13 @@
     facts_ref[...] = facts[...].astype(BF16)
 
 
-def info_kernel(after_ref, facts_ref, bins_ref, class_ref, info_ref, info):
+def packet_kernel(facts_ref, weight_ref, bins_ref, class_ref, packet_ref, again_ref, info):
+    packet_ref[0:DEPTH] = weight_ref[...]
     info[...] = facts_ref[...].astype(F32)
     info[1:2] = bins_ref[...].astype(F32)
     info[2:3] = class_ref[...].astype(F32)
-    info_ref[...] = info[...].astype(BF16)
+    packet_ref[DEPTH:] = info[...].astype(BF16)
+    again_ref[...] = facts_ref[...]
 
 
 def owner(chips, j, turn):
@@ -129,7 +133,7 @@
 def over_fold(named, infos, owners):
     scale = jnp.zeros_like(named)
     for info, held in zip(infos, owners):
-        scale = jnp.where(named == held.astype(F32), 1.0 / info[...].astype(F32)[0:1], scale)
+        scale = jnp.where(named == held.astype(F32), 1.0 / info[info.shape[0] - SUB :].astype(F32)[0:1], scale)
     return scale
 
 
@@ -143,24 +147,32 @@
     )
 
 
-def sums_kernel(own_ref, near_ref, facts_ref, hi_ref, lo_ref):
+def choice_kernel(after_ref, facts_ref, chosen_ref):
+    tiles = chosen_ref.shape[0] // (NPAT * SUB)
+    chosen_ref[...] = choice(facts_ref[...].astype(F32)[8 : 8 + tiles, 0:BANDS])
+
+
+def sums_kernel(own_ref, near_ref, chosen_ref, hi_ref, lo_ref):
     tiles = hi_ref.shape[0] // (2 * own_ref.shape[0])
-    chosen = choice(facts_ref[...].astype(F32)[8 : 8 + tiles, 0:BANDS])
-    band_sums(chosen, own_ref, near_ref, hi_ref, lo_ref, tiles)
-
-
-def begin_kernel(chips, hi_ref, lo_ref, weight_ref, near_weight_ref, *refs):
+    band_sums(chosen_ref[...], own_ref, near_ref, hi_ref, lo_ref, tiles)
+
+
+def relay_kernel(after_ref, also_ref, weight_ref, out_ref):
+    out_ref[...] = weight_ref[...]
+
+
+def begin_kernel(chips, hi_ref, lo_ref, *refs):
     infos, (total_ref, scale_ref, named_ref, binning_ref) = refs[:-4], refs[-4:]
     traces = named_ref.shape[0] // 2
     for half in range(2):
         at = half * traces
-        info = infos[half * chips][...].astype(F32)
+        info = infos[half * chips][DEPTH:].astype(F32)
         place = lax.broadcasted_iota(jnp.int32, (MB, traces), 0).astype(F32)
         binning_ref[:, at : at + traces] = jnp.where(place == info[1:2], 1.0, 0.0).astype(BF16)
         named_ref[at : at + traces] = jnp.broadcast_to(info[2:3], (traces, traces)).T
     named, tiles = named_ref[...], hi_ref.shape[0] // named_ref.shape[0]
     owners = [owner(chips, 0, 0), owner(chips, 0, 1)]
-    total_ref[...] = weigh(hi_ref, lo_ref, named, [weight_ref, near_weight_ref], owners, tiles)
+    total_ref[...] = weigh(hi_ref, lo_ref, named, [infos[0], infos[chips]], owners, tiles)
     scale_ref[...] = over_fold(named, infos, all_owners(chips))
 
 
@@ -215,32 +227,40 @@
         in_specs=[SMEM, VMEM], out_specs=VMEM
     )(fold_count, apertures)
     far_facts = [far(facts, j) for j in hops]
-    cross_facts = [far(facts, j, 1) for j in hops]
-    near_traces, near_weights = near(traces), near(weights)
-    info = call(info_kernel, block, [pltpu.VMEM(block.shape, F32)], flops=INFO_COST)(
-        in_specs=[ANY] + [VMEM] * 3, out_specs=VMEM
-    )(near_traces, facts, mid_bins.reshape(1, tr_dev), class_map.reshape(1, tr_dev))
-    near_info = near(info)
+    tied, _ = lax.optimization_barrier((traces, facts))
+    near_traces = near(tied)
+    packet, again = call(
+        packet_kernel, (shape((DEPTH + SUB, PTS), BF16), block), [pltpu.VMEM(block.shape, F32)], flops=INFO_COST
+    )(in_specs=[VMEM] * 4, out_specs=[VMEM] * 2)(
+        facts, weights, mid_bins.reshape(1, tr_dev), class_map.reshape(1, tr_dev)
+    )
+    near_packet = near(packet)
+    cross_facts = [far(again, j, 1) for j in hops]
 
     rows = 2 * tr_dev
     sums = shape((tiles * rows, NPAT * BAND), BF16)
     total = shape((tiles * rows, PTS), F32)
     by_row = shape((rows, PTS), F32)
     work = 2 * tiles * rows * (NPAT * BAND) * PTS
-    far_weights, info = lax.optimization_barrier((far_weights, info))
-    relayed = [near(w) for w in far_weights]
-    infos = [info] + far_facts + [near_info] + cross_facts
+    relayed = [
+        near(call(relay_kernel, shape(w.shape, BF16), flops=RELAY_COST)(
+            in_specs=[ANY, VMEM, VMEM], out_specs=VMEM
+        )(packet, traces, w))
+        for w in far_weights
+    ]
+    infos = [packet] + far_facts + [near_packet] + cross_facts
     all_begun = []
     for j in hops:
+        chosen = call(choice_kernel, shape((tiles * NPAT * SUB, BANDS * SUB), BF16), flops=CHOICE_COST)(
+            in_specs=[VMEM] * 2, out_specs=VMEM
+        )(traces, far_facts[j - 1])
         its_sums = call(sums_kernel, (sums, sums), flops=SUMS_COST)(
             in_specs=[VMEM] * 3, out_specs=[VMEM] * 2
-        )(traces, near_traces, far_facts[j - 1])
+        )(traces, near_traces, chosen)
         begun, scale, named, binning = call(
             functools.partial(begin_kernel, chips),
             (total, by_row, by_row, shape((MB, rows), BF16)), flops=BEGIN_COST,
-        )(in_specs=[VMEM] * (4 + len(infos)), out_specs=[VMEM] * 4)(
-            *its_sums, weights, near_weights, *infos
-        )
+        )(in_specs=[VMEM] * (2 + len(infos)), out_specs=[VMEM] * 4)(*its_sums, *infos)
         all_begun.append((begun, *its_sums))
     received = []
     for j in hops:
@@ -250,7 +270,7 @@
             in_specs=[VMEM] * (2 + len(rest)), out_specs=VMEM
         )(*its_sums, *rest)
         received.append(far(part, chips - j))
-    rest = [weights] + far_weights + [near_weights] + relayed
+    rest = [packet] + far_weights + [near_packet] + relayed
     image = call(
         functools.partial(own_kernel, chips), shape((tiles, MB, PTS), F32),
         [pltpu.VMEM(sums.shape, BF16)] * 2, flops=15 * work,

time: 14.6 us -> 14.3 us (0.979)
  waiting for transfers between devices: 2.58 us -> 1.59 us
  local copies, waits for them, and re-layouts: 0.02 us -> 0.72 us
    ppermute x4, waiting for transfers between devices: 2.51 us -> 1.59 us  [far(): lax.ppermute(x, 'off', [(i, (i // 2 + j) % chips * 2 + (i % 2 ^ turn)) fo...]
    unnamed x10, local copies, waits for them, and re-layouts: 0.02 us -> 0.72 us
    ppermute x4 -> x3, starting transfers between devices: 1.13 us -> 0.55 us  [near(): return lax.ppermute(x, 'off', [(i, i ^ 1) for i in range(n_off)])]
    ppermute x4, starting transfers between devices: 6.12 us -> 6.6 us  [far(): lax.ppermute(x, 'off', [(i, (i // 2 + j) % chips * 2 + (i % 2 ^ turn)) fo...]
    pallas_call x1 -> x3, Pallas kernels: 0.01 us -> 0.19 us  [the longest x1 0.16 us: shards(): call(choice_kernel, shape((tiles * NPAT * SUB, BANDS * SUB), BF16), flops...]
  transfers between devices with their start and end apart: 8 -> 7, of which waited for: 4 -> 3; matrix products, arithmetic and copies ran while one was open for 0% -> 0% of each run, Pallas kernels for 17% -> 18%
where the time goes in v4:
time: 14.3 us; the launch traced here: 14.2 us
  starting transfers between devices  7.15 us (50%)
  Pallas kernels  3.28 us (23%)
  waiting for transfers between devices  1.59 us (11%)
  between operations  0.77 us (5%)
  local copies, waits for them, and re-layouts  0.72 us (5%)
  other arithmetic  0.67 us (5%)
    ppermute x4, starting transfers between devices, far(): lax.ppermute(x, 'off', [(i, (i // 2 + j) % chips * 2 + (i % 2 ^ turn)) fo...  6.6 us
    ppermute x4, waiting for transfers between devices, far(): lax.ppermute(x, 'off', [(i, (i // 2 + j) % chips * 2 + (i % 2 ^ turn)) fo...  1.59 us
    pallas_call x1, Pallas kernels, shards(): call(functools.partial(own_kernel, chips), shape((tiles, MB, PTS), F32),...  1.42 us
    unnamed x10, local copies, waits for them, and re-layouts  0.72 us
    pallas_call x1, Pallas kernels, shards(): call(functools.partial(finish_kernel, chips), shape((tiles, MB, PTS), BF16))  0.67 us
    add x1, other arithmetic, shards(): image = image + part.astype(F32)  0.67 us
    ppermute x3, starting transfers between devices, near(): return lax.ppermute(x, 'off', [(i, i ^ 1) for i in range(n_off)])  0.55 us
    pallas_call x1, Pallas kernels, shards(): call(sums_kernel, (sums, sums), flops=SUMS_COST)  0.54 us
  transfers between devices with their start and end apart: 7, of which 3 were waited for; matrix products, arithmetic and copies ran while one was open for 0% of the time, Pallas kernels for 18%

profile of v4, /device:TPU:0, one launch (start us, length us, event | category | flops | bytes accessed | tf_op | source)
XLA Modules:
  0.0 14.2 jit_solution(239332818525335483)
XLA Ops:
  0.0 0.0 copy-start.2
  0.0 2.9 %collective-permute-start.4 = (bf16[512,128]{1,0:T(8,128)(2,1)}, bf16[512,128]{1,0:T(8,128)(2,1)S(1)}, u32[]{:S(2)}, u32[]{:S(2)}) collective-permute-start(bf16[512,128]{1,0:T(8,128)(2,1)} %bitcast.3), channel_id=1, source_target_pairs={{0,8},{4,12},{8,0},{12,4},{1,9},{5,13},{9,1},{13,5},{2,10},{6,14},... | collective-permute-start | bytes 393224 | tf_op jit(solution)/shard_map/ppermute | solution.py:218
  3.6 0.0 copy-done.2
  3.6 0.0 copy-start.1
  3.6 0.1 collective-permute-start.1
  3.7 0.1 collective-permute-start
  3.8 0.0 copy-start.3
  3.8 0.0 copy-start.4
  3.8 0.7 %copy-done.1 = bf16[1,4,128,128]{3,2,1,0:T(8,128)(2,1)S(1)} copy-done((bf16[1,4,128,128]{3,2,1,0:T(8,128)(2,1)S(1)}, bf16[1,4,128,128]{3,2,1,0:T(8,128)(2,1)}, u32[]{:S(2)}) %copy-start.1) | copy-done | bytes 131096
  4.5 0.0 copy-done.3
  4.5 0.0 copy-done.4
  4.5 0.0 copy-start
  4.5 2.1 %collective-permute-start.3 = (bf16[16,128]{1,0:T(8,128)(2,1)S(1)}, bf16[16,128]{1,0:T(8,128)(2,1)S(1)}, u32[]{:S(2)}, u32[]{:S(2)}) collective-permute-start(bf16[16,128]{1,0:T(8,128)(2,1)S(1)} %get-tuple-element.18), channel_id=1, source_target_pairs={{0,12},{4,8},{8,4},{12,0},{1,13},{5,9},{9,5},{13,1},{2,14},{6,10},... | collective-permute-start | bytes 12296 | tf_op jit(solution)/shard_map/ppermute | solution.py:218
  6.6 0.0 collective-permute-start.2
  6.6 0.1 collective-permute-done.4.weight_ref.refs_1_.refs_0_
  6.7 0.0 copy-done
  6.7 0.5 %collective-permute-start.5 = (bf16[512,128]{1,0:T(8,128)(2,1)S(1)}, bf16[512,128]{1,0:T(8,128)(2,1)S(1)}, u32[]{:S(2)}, u32[]{:S(2)}) collective-permute-start(bf16[512,128]{1,0:T(8,128)(2,1)S(1)} %shard_map.69), channel_id=1, source_target_pairs={{0,4},{4,0},{8,12},{12,8},{1,5},{5,1},{9,13},{13,9},{2,6},{6,2},{1... | collective-permute-start | bytes 393224 | tf_op jit(solution)/shard_map/ppermute | solution.py:215
  7.2 0.1 collective-permute-done.1.facts_ref.refs_1_
  7.3 0.2 %shard_map.65.chosen_ref = bf16[128,512]{1,0:T(8,128)(2,1)S(1)} custom-call(bf16[128,4096]{1,0:T(8,128)(2,1)S(1)} %copy-done, bf16[16,128]{1,0:T(8,128)(2,1)S(1)} %collective-permute-done.1.facts_ref.refs_1_), custom_call_target="tpu_custom_call" | custom-call | flops 7000000000 | tf_op jit(solution)/shard_map/pallas_call | solution.py:254
  7.5 0.0 collective-permute-done.near_ref
  7.5 0.5 %shard_map.66 = (bf16[512,512]{1,0:T(8,128)(2,1)S(1)}, bf16[512,512]{1,0:T(8,128)(2,1)S(1)}) custom-call(bf16[128,4096]{1,0:T(8,128)(2,1)S(1)} %copy-done, bf16[128,4096]{1,0:T(8,128)(2,1)S(1)} %collective-permute-done.near_ref, bf16[128,512]{1,0:T(8,128)(2,1)S(1)} %shard_map.65.chosen_ref), custom_call_target="tpu_custom_call" | custom-call | tf_op jit(solution)/shard_map/pallas_call | solution.py:257
  8.0 0.0 collective-permute-done.3.refs_3_
  8.0 0.0 collective-permute-done.2.refs_2_
  8.0 0.4 %shard_map.68 = (f32[512,128]{1,0:T(8,128)S(1)}, f32[256,128]{1,0:T(8,128)S(1)}, f32[256,128]{1,0:T(8,128)S(1)}, bf16[128,256]{1,0:T(8,128)(2,1)S(1)}) custom-call(bf16[512,512]{1,0:T(8,128)(2,1)S(1)} %get-tuple-element.15.hi_ref, bf16[512,512]{1,0:T(8,128)(2,1)S(1)} %get-tuple-element.16.lo_ref, bf16[528,128]{1,0:T(8,128)(2,1)S(1)} %get-tuple-element.17.refs_0_.after_ref, ...), custom_call_target="tpu_custom_call" | custom-call | flops 1100000000 | tf_op jit(solution)/shard_map/pallas_call | solution.py:260
  8.5 0.0 collective-permute-done.5.refs_3_.refs_1_
  8.5 0.7 %shard_map.71 = bf16[2,128,128]{2,1,0:T(8,128)(2,1)S(1)} custom-call(bf16[512,512]{1,0:T(8,128)(2,1)S(1)} %get-tuple-element.15.hi_ref, bf16[512,512]{1,0:T(8,128)(2,1)S(1)} %get-tuple-element.16.lo_ref, f32[512,128]{1,0:T(8,128)S(1)} %get-tuple-element.22.total_ref, f32[256,128]{1,0:T(8,128)S(1)} %get-tuple-element.19.named_ref, ...), custom_call_target="tpu_custom_call" | custom-call | tf_op jit(solution)/shard_map/pallas_call | solution.py:269
  9.2 1.5 %collective-permute-start.6 = (bf16[2,128,128]{2,1,0:T(8,128)(2,1)S(1)}, bf16[2,128,128]{2,1,0:T(8,128)(2,1)S(1)}, u32[]{:S(2)}, u32[]{:S(2)}) collective-permute-start(bf16[2,128,128]{2,1,0:T(8,128)(2,1)S(1)} %shard_map.71), channel_id=1, source_target_pairs={{0,8},{4,12},{8,0},{12,4},{1,9},{5,13},{9,1},{13,5},{2,10},{6,14},... | collective-permute-start | bytes 196616 | tf_op jit(solution)/shard_map/ppermute | solution.py:218
  10.7 1.4 %shard_map.70 = f32[2,128,128]{2,1,0:T(8,128)S(1)} custom-call(bf16[128,4096]{1,0:T(8,128)(2,1)S(1)} %copy-done, bf16[128,4096]{1,0:T(8,128)(2,1)S(1)} %collective-permute-done.near_ref, s32[2,32]{1,0:T(2,128)S(1)} %copy-done.2, f32[256,128]{1,0:T(8,128)S(1)} %get-tuple-element.19.named_ref, f32[256,128]{1,0:T(8,128)S(1)} %get-tuple-element.20.scale_ref, ...), custom_call_target="tpu_custom_call" | custom-call | flops 1006632960 | tf_op jit(solution)/shard_map/pallas_call | solution.py:274
  12.1 1.4 %collective-permute-done.6 = bf16[2,128,128]{2,1,0:T(8,128)(2,1)S(1)} collective-permute-done((bf16[2,128,128]{2,1,0:T(8,128)(2,1)S(1)}, bf16[2,128,128]{2,1,0:T(8,128)(2,1)S(1)}, u32[]{:S(2)}, u32[]{:S(2)}) %collective-permute-start.6) | collective-permute-done | bytes 65568 | tf_op jit(solution)/shard_map/ppermute | solution.py:218
  13.5 0.7 %convert_add_fusion = f32[2,128,128]{2,1,0:T(8,128)} fusion(f32[2,128,128]{2,1,0:T(8,128)S(1)} %shard_map.70, bf16[2,128,128]{2,1,0:T(8,128)(2,1)S(1)} %collective-permute-done.6), kind=kLoop, calls=%fused_computation | loop fusion | flops 65536 | bytes 327680 | tf_op jit(solution)/shard_map/add | solution.py:281
  (3 shorter events, 0.0 us)
Async XLA Ops:
  0.0 3.6 %copy-start.2 = (s32[2,32]{1,0:T(2,128)S(1)}, s32[2,32]{1,0:T(2,128)}, u32[]{:S(2)}) copy-start(s32[2,32]{1,0:T(2,128)} %pattern_ref.3) | copy-start | bytes 772
  0.0 6.7 %collective-permute-start.4 = (bf16[512,128]{1,0:T(8,128)(2,1)}, bf16[512,128]{1,0:T(8,128)(2,1)S(1)}, u32[]{:S(2)}, u32[]{:S(2)}) collective-permute-start(bf16[512,128]{1,0:T(8,128)(2,1)} %bitcast.3), channel_id=1, source_target_pairs={{0,8},{4,12},{8,0},{12,4},{1,9},{5,13},{9,1},{13,5},{2,10},{6,14},... | collective-permute-start | bytes 393224 | tf_op jit(solution)/shard_map/ppermute | solution.py:218
  3.6 0.9 %copy-start.1 = (bf16[1,4,128,128]{3,2,1,0:T(8,128)(2,1)S(1)}, bf16[1,4,128,128]{3,2,1,0:T(8,128)(2,1)}, u32[]{:S(2)}) copy-start(bf16[1,4,128,128]{3,2,1,0:T(8,128)(2,1)} %param.10) | copy-start | bytes 393220
  3.6 3.7 %collective-permute-start.1 = (bf16[16,128]{1,0:T(8,128)(2,1)S(1)}, bf16[16,128]{1,0:T(8,128)(2,1)S(1)}, u32[]{:S(2)}, u32[]{:S(2)}) collective-permute-start(bf16[16,128]{1,0:T(8,128)(2,1)S(1)} %shard_map.64.facts_ref), channel_id=1, source_target_pairs={{0,8},{4,12},{8,0},{12,4},{1,9},{5,13},{9,1},{13,5},{2,10},{6,14},... | collective-permute-start | bytes 12296 | tf_op jit(solution)/shard_map/ppermute | solution.py:218
  3.7 3.8 %collective-permute-start = (bf16[128,4096]{1,0:T(8,128)(2,1)}, bf16[128,4096]{1,0:T(8,128)(2,1)S(1)}, u32[]{:S(2)}, u32[]{:S(2)}) collective-permute-start(bf16[128,4096]{1,0:T(8,128)(2,1)} %own_ref.3), channel_id=1, source_target_pairs={{0,4},{4,0},{8,12},{12,8},{1,5},{5,1},{9,13},{13,9},{2,6},{6,2},{1... | collective-permute-start | bytes 3145736 | tf_op jit(solution)/shard_map/ppermute | solution.py:215
  3.8 0.7 %copy-start.3 = (s32[128]{0:T(128)S(1)}, s32[128]{0:T(128)}, u32[]{:S(2)}) copy-start(s32[128]{0:T(128)} %param.8) | copy-start | bytes 1540
  3.8 0.7 %copy-start.4 = (s32[128,1]{0,1:T(1,128)S(1)}, s32[128,1]{0,1:T(1,128)}, u32[]{:S(2)}) copy-start(s32[128,1]{0,1:T(1,128)} %param.7) | copy-start | bytes 1540
  4.5 2.2 %copy-start = (bf16[128,4096]{1,0:T(8,128)(2,1)S(1)}, bf16[128,4096]{1,0:T(8,128)(2,1)}, u32[]{:S(2)}) copy-start(bf16[128,4096]{1,0:T(8,128)(2,1)} %own_ref.3) | copy-start | bytes 3145732
  4.5 3.5 %collective-permute-start.3 = (bf16[16,128]{1,0:T(8,128)(2,1)S(1)}, bf16[16,128]{1,0:T(8,128)(2,1)S(1)}, u32[]{:S(2)}, u32[]{:S(2)}) collective-permute-start(bf16[16,128]{1,0:T(8,128)(2,1)S(1)} %get-tuple-element.18), channel_id=1, source_target_pairs={{0,12},{4,8},{8,4},{12,0},{1,13},{5,9},{9,5},{13,1},{2,14},{6,10},... | collective-permute-start | bytes 12296 | tf_op jit(solution)/shard_map/ppermute | solution.py:218
  6.6 1.5 %collective-permute-start.2 = (bf16[528,128]{1,0:T(8,128)(2,1)S(1)}, bf16[528,128]{1,0:T(8,128)(2,1)S(1)}, u32[]{:S(2)}, u32[]{:S(2)}) collective-permute-start(bf16[528,128]{1,0:T(8,128)(2,1)S(1)} %get-tuple-element.17.refs_0_.after_ref), channel_id=1, source_target_pairs={{0,4},{4,0},{8,12},{12,8},{1,5},{5,1},{9,13},{13,9},{2,6},{6,2},{1... | collective-permute-start | bytes 405512 | tf_op jit(solution)/shard_map/ppermute | solution.py:215
  6.7 1.8 %collective-permute-start.5 = (bf16[512,128]{1,0:T(8,128)(2,1)S(1)}, bf16[512,128]{1,0:T(8,128)(2,1)S(1)}, u32[]{:S(2)}, u32[]{:S(2)}) collective-permute-start(bf16[512,128]{1,0:T(8,128)(2,1)S(1)} %shard_map.69), channel_id=1, source_target_pairs={{0,4},{4,0},{8,12},{12,8},{1,5},{5,1},{9,13},{13,9},{2,6},{6,2},{1... | collective-permute-start | bytes 393224 | tf_op jit(solution)/shard_map/ppermute | solution.py:215
  9.2 4.3 %collective-permute-start.6 = (bf16[2,128,128]{2,1,0:T(8,128)(2,1)S(1)}, bf16[2,128,128]{2,1,0:T(8,128)(2,1)S(1)}, u32[]{:S(2)}, u32[]{:S(2)}) collective-permute-start(bf16[2,128,128]{2,1,0:T(8,128)(2,1)S(1)} %shard_map.71), channel_id=1, source_target_pairs={{0,8},{4,12},{8,0},{12,4},{1,9},{5,13},{9,1},{13,5},{2,10},{6,14},... | collective-permute-start | bytes 196616 | tf_op jit(solution)/shard_map/ppermute | solution.py:218

commit v5 on v4

--- a/solution.py
+++ b/solution.py
@@ -14,12 +14,11 @@
 NPAT = 4
 SUB = 16
 DEPTH = NPAT * BAND
-INFO_COST = 7 * 10**8
-BEGIN_COST = 11 * 10**8
-SUMS_COST = 0
-FACTS_COST = 15 * 10**7
-CHOICE_COST = 7 * 10**9
-RELAY_COST = 4 * 10**9
+INFO_COST = 55 * 10**7
+BEGIN_COST = 8 * 10**8
+FACTS_COST = 2 * 10**8
+CHOICE_COST = 6 * 10**9
+RELAY_COST = 5 * 10**9
 F32 = jnp.float32
 BF16 = jnp.bfloat16
 VMEM = pl.BlockSpec(memory_space=pltpu.VMEM)
@@ -130,10 +129,10 @@
     return total
 
 
-def over_fold(named, infos, owners):
+def over_fold(named, folds, owners):
     scale = jnp.zeros_like(named)
-    for info, held in zip(infos, owners):
-        scale = jnp.where(named == held.astype(F32), 1.0 / info[info.shape[0] - SUB :].astype(F32)[0:1], scale)
+    for fold, held in zip(folds, owners):
+        scale = jnp.where(named == held.astype(F32), 1.0 / fold, scale)
     return scale
 
 
@@ -147,33 +146,38 @@
     )
 
 
-def choice_kernel(after_ref, facts_ref, chosen_ref):
-    tiles = chosen_ref.shape[0] // (NPAT * SUB)
-    chosen_ref[...] = choice(facts_ref[...].astype(F32)[8 : 8 + tiles, 0:BANDS])
-
-
-def sums_kernel(own_ref, near_ref, chosen_ref, hi_ref, lo_ref):
-    tiles = hi_ref.shape[0] // (2 * own_ref.shape[0])
-    band_sums(chosen_ref[...], own_ref, near_ref, hi_ref, lo_ref, tiles)
+def facts_in_kernel(after_ref, facts_ref, out_ref):
+    out_ref[...] = facts_ref[...]
 
 
 def relay_kernel(after_ref, also_ref, weight_ref, out_ref):
     out_ref[...] = weight_ref[...]
 
 
-def begin_kernel(chips, hi_ref, lo_ref, *refs):
-    infos, (total_ref, scale_ref, named_ref, binning_ref) = refs[:-4], refs[-4:]
+def sums_kernel(own_ref, near_ref, facts_ref, hi_ref, lo_ref):
+    tiles = hi_ref.shape[0] // (2 * own_ref.shape[0])
+    chosen = choice(facts_ref[...].astype(F32)[8 : 8 + tiles, 0:BANDS])
+    band_sums(chosen, own_ref, near_ref, hi_ref, lo_ref, tiles)
+
+
+def begin_kernel(chips, hi_ref, lo_ref, packet_ref, near_packet_ref, *refs):
+    facts, (total_ref, scale_ref, named_ref, binning_ref) = refs[:-4], refs[-4:]
     traces = named_ref.shape[0] // 2
-    for half in range(2):
+    tiles = hi_ref.shape[0] // (2 * traces)
+    folds = []
+    for half, ref in enumerate((packet_ref, near_packet_ref)):
         at = half * traces
-        info = infos[half * chips][DEPTH:].astype(F32)
+        info = ref[DEPTH:].astype(F32)
         place = lax.broadcasted_iota(jnp.int32, (MB, traces), 0).astype(F32)
         binning_ref[:, at : at + traces] = jnp.where(place == info[1:2], 1.0, 0.0).astype(BF16)
         named_ref[at : at + traces] = jnp.broadcast_to(info[2:3], (traces, traces)).T
-    named, tiles = named_ref[...], hi_ref.shape[0] // named_ref.shape[0]
+        folds.append(info[0:1])
+        for n in range(half * (chips - 1), (half + 1) * (chips - 1)):
+            folds.append(facts[n][...].astype(F32)[0:1])
+    named = named_ref[...]
     owners = [owner(chips, 0, 0), owner(chips, 0, 1)]
-    total_ref[...] = weigh(hi_ref, lo_ref, named, [infos[0], infos[chips]], owners, tiles)
-    scale_ref[...] = over_fold(named, infos, all_owners(chips))
+    total_ref[...] = weigh(hi_ref, lo_ref, named, [packet_ref, near_packet_ref], owners, tiles)
+    scale_ref[...] = over_fold(named, folds, all_owners(chips))
 
 
 def image_of(total, scale, binning, out_ref):
@@ -248,19 +252,21 @@
         )(packet, traces, w))
         for w in far_weights
     ]
-    infos = [packet] + far_facts + [near_packet] + cross_facts
+    known = [
+        call(facts_in_kernel, block, flops=CHOICE_COST)(in_specs=[VMEM] * 2, out_specs=VMEM)(traces, x)
+        for x in far_facts
+    ] + cross_facts
     all_begun = []
     for j in hops:
-        chosen = call(choice_kernel, shape((tiles * NPAT * SUB, BANDS * SUB), BF16), flops=CHOICE_COST)(
-            in_specs=[VMEM] * 2, out_specs=VMEM
-        )(traces, far_facts[j - 1])
-        its_sums = call(sums_kernel, (sums, sums), flops=SUMS_COST)(
-            in_specs=[VMEM] * 3, out_specs=[VMEM] * 2
-        )(traces, near_traces, chosen)
+        its_sums = call(sums_kernel, (sums, sums))(in_specs=[VMEM] * 3, out_specs=[VMEM] * 2)(
+            traces, near_traces, known[j - 1]
+        )
         begun, scale, named, binning = call(
             functools.partial(begin_kernel, chips),
             (total, by_row, by_row, shape((MB, rows), BF16)), flops=BEGIN_COST,
-        )(in_specs=[VMEM] * (2 + len(infos)), out_specs=[VMEM] * 4)(*its_sums, *infos)
+        )(in_specs=[VMEM] * (4 + len(known)), out_specs=[VMEM] * 4)(
+            *its_sums, packet, near_packet, *known
+        )
         all_begun.append((begun, *its_sums))
     received = []
     for j in hops:

time: 14.3 us -> 14.3 us (level)
  waiting for transfers between devices: 1.59 us -> 2.72 us
  starting transfers between devices: 7.15 us -> 6.06 us
    ppermute x4, waiting for transfers between devices: 1.59 us -> 2.71 us  [far(): lax.ppermute(x, 'off', [(i, (i // 2 + j) % chips * 2 + (i % 2 ^ turn)) fo...]
    ppermute x4, starting transfers between devices: 6.6 us -> 5.9 us  [far(): lax.ppermute(x, 'off', [(i, (i // 2 + j) % chips * 2 + (i % 2 ^ turn)) fo...]
    ppermute x3, starting transfers between devices: 0.55 us -> 0.16 us  [near(): return lax.ppermute(x, 'off', [(i, i ^ 1) for i in range(n_off)])]
where the time goes in v5:
time: 14.3 us; the launch traced here: 14.2 us
  starting transfers between devices  6.06 us (42%)
  Pallas kernels  3.21 us (22%)
  waiting for transfers between devices  2.72 us (19%)
  between operations  0.78 us (5%)
  local copies, waits for them, and re-layouts  0.71 us (5%)
  other arithmetic  0.67 us (5%)
    ppermute x4, starting transfers between devices, far(): lax.ppermute(x, 'off', [(i, (i // 2 + j) % chips * 2 + (i % 2 ^ turn)) fo...  5.9 us
    ppermute x4, waiting for transfers between devices, far(): lax.ppermute(x, 'off', [(i, (i // 2 + j) % chips * 2 + (i % 2 ^ turn)) fo...  2.71 us
    pallas_call x1, Pallas kernels, shards(): call(functools.partial(own_kernel, chips), shape((tiles, MB, PTS), F32),...  1.42 us
    unnamed x10, local copies, waits for them, and re-layouts  0.71 us
    pallas_call x1, Pallas kernels, shards(): call(functools.partial(finish_kernel, chips), shape((tiles, MB, PTS), BF16))  0.67 us
    add x1, other arithmetic, shards(): image = image + part.astype(F32)  0.67 us
    pallas_call x1, Pallas kernels, shards(): call(sums_kernel, (sums, sums))(in_specs=[VMEM] * 3, out_specs=[VMEM] * 2)  0.64 us
    pallas_call x1, Pallas kernels, shards(): call(functools.partial(begin_kernel, chips), (total, by_row, by_row, shap...  0.44 us
  transfers between devices with their start and end apart: 7, of which 3 were waited for; matrix products, arithmetic and copies ran while one was open for 0% of the time, Pallas kernels for 18%

profile of v5, /device:TPU:0, one launch (start us, length us, event | category | flops | bytes accessed | tf_op | source)
XLA Modules:
  0.0 14.2 jit_solution(4515118816462537915)
XLA Ops:
  0.0 0.0 copy-start.2
  0.0 2.9 %collective-permute-start.4 = (bf16[512,128]{1,0:T(8,128)(2,1)}, bf16[512,128]{1,0:T(8,128)(2,1)S(1)}, u32[]{:S(2)}, u32[]{:S(2)}) collective-permute-start(bf16[512,128]{1,0:T(8,128)(2,1)} %bitcast.3), channel_id=1, source_target_pairs={{0,8},{4,12},{8,0},{12,4},{1,9},{5,13},{9,1},{13,5},{2,10},{6,14},... | collective-permute-start | bytes 393224 | tf_op jit(solution)/shard_map/ppermute | solution.py:222
  3.6 0.0 copy-done.2
  3.6 0.0 copy-start.1
  3.6 0.0 copy-start.3
  3.6 0.0 copy-start.4
  3.6 0.0 copy-start
  3.7 0.1 collective-permute-start.1
  3.7 0.1 collective-permute-start
  3.8 0.7 %copy-done.1 = bf16[1,4,128,128]{3,2,1,0:T(8,128)(2,1)S(1)} copy-done((bf16[1,4,128,128]{3,2,1,0:T(8,128)(2,1)S(1)}, bf16[1,4,128,128]{3,2,1,0:T(8,128)(2,1)}, u32[]{:S(2)}) %copy-start.1) | copy-done | bytes 131096
  4.5 0.0 copy-done.3
  4.5 0.0 copy-done.4
  4.5 1.4 %collective-permute-start.3 = (bf16[16,128]{1,0:T(8,128)(2,1)S(1)}, bf16[16,128]{1,0:T(8,128)(2,1)S(1)}, u32[]{:S(2)}, u32[]{:S(2)}) collective-permute-start(bf16[16,128]{1,0:T(8,128)(2,1)S(1)} %get-tuple-element.18), channel_id=1, source_target_pairs={{0,12},{4,8},{8,4},{12,0},{1,13},{5,9},{9,5},{13,1},{2,14},{6,10},... | collective-permute-start | bytes 12296 | tf_op jit(solution)/shard_map/ppermute | solution.py:222
  6.0 0.0 collective-permute-start.2
  6.0 0.7 %collective-permute-done.4.weight_ref.refs_1_.refs_0_ = bf16[512,128]{1,0:T(8,128)(2,1)S(1)} collective-permute-done((bf16[512,128]{1,0:T(8,128)(2,1)}, bf16[512,128]{1,0:T(8,128)(2,1)S(1)}, u32[]{:S(2)}, u32[]{:S(2)}) %collective-permute-start.4) | collective-permute-done | bytes 131104 | tf_op jit(solution)/shard_map/ppermute | solution.py:222
  6.7 0.0 copy-done
  6.7 0.1 collective-permute-start.5
  6.8 0.5 %collective-permute-done.1.facts_ref = bf16[16,128]{1,0:T(8,128)(2,1)S(1)} collective-permute-done((bf16[16,128]{1,0:T(8,128)(2,1)S(1)}, bf16[16,128]{1,0:T(8,128)(2,1)S(1)}, u32[]{:S(2)}, u32[]{:S(2)}) %collective-permute-start.1) | collective-permute-done | bytes 4128 | tf_op jit(solution)/shard_map/ppermute | solution.py:222
  7.3 0.0 collective-permute-done.near_ref
  7.3 0.6 %shard_map.66 = (bf16[512,512]{1,0:T(8,128)(2,1)S(1)}, bf16[512,512]{1,0:T(8,128)(2,1)S(1)}) custom-call(bf16[128,4096]{1,0:T(8,128)(2,1)S(1)} %copy-done, bf16[128,4096]{1,0:T(8,128)(2,1)S(1)} %collective-permute-done.near_ref, bf16[16,128]{1,0:T(8,128)(2,1)S(1)} %shard_map.65.facts_ref.refs_0_), custom_call_target="tpu_custom_call" | custom-call | tf_op jit(solution)/shard_map/pallas_call | solution.py:261
  8.0 0.0 collective-permute-done.3.refs_1_
  8.0 0.0 collective-permute-done.2.near_packet_ref.refs_2_
  8.0 0.4 %shard_map.68 = (f32[512,128]{1,0:T(8,128)S(1)}, f32[256,128]{1,0:T(8,128)S(1)}, f32[256,128]{1,0:T(8,128)S(1)}, bf16[128,256]{1,0:T(8,128)(2,1)S(1)}) custom-call(bf16[512,512]{1,0:T(8,128)(2,1)S(1)} %get-tuple-element.15.hi_ref, bf16[512,512]{1,0:T(8,128)(2,1)S(1)} %get-tuple-element.16.lo_ref, ...), custom_call_target="tpu_custom_call" | custom-call | flops 800000000 | tf_op jit(solution)/shard_map/pallas_call | solution.py:264
  8.5 0.0 collective-permute-done.5.refs_3_.refs_1_
  8.5 0.7 %shard_map.71 = bf16[2,128,128]{2,1,0:T(8,128)(2,1)S(1)} custom-call(bf16[512,512]{1,0:T(8,128)(2,1)S(1)} %get-tuple-element.15.hi_ref, bf16[512,512]{1,0:T(8,128)(2,1)S(1)} %get-tuple-element.16.lo_ref, f32[512,128]{1,0:T(8,128)S(1)} %get-tuple-element.22.total_ref, f32[256,128]{1,0:T(8,128)S(1)} %get-tuple-element.19.named_ref, ...), custom_call_target="tpu_custom_call" | custom-call | tf_op jit(solution)/shard_map/pallas_call | solution.py:275
  9.1 1.5 %collective-permute-start.6 = (bf16[2,128,128]{2,1,0:T(8,128)(2,1)S(1)}, bf16[2,128,128]{2,1,0:T(8,128)(2,1)S(1)}, u32[]{:S(2)}, u32[]{:S(2)}) collective-permute-start(bf16[2,128,128]{2,1,0:T(8,128)(2,1)S(1)} %shard_map.71), channel_id=1, source_target_pairs={{0,8},{4,12},{8,0},{12,4},{1,9},{5,13},{9,1},{13,5},{2,10},{6,14},... | collective-permute-start | bytes 196616 | tf_op jit(solution)/shard_map/ppermute | solution.py:222
  10.6 1.4 %shard_map.70 = f32[2,128,128]{2,1,0:T(8,128)S(1)} custom-call(bf16[128,4096]{1,0:T(8,128)(2,1)S(1)} %copy-done, bf16[128,4096]{1,0:T(8,128)(2,1)S(1)} %collective-permute-done.near_ref, s32[2,32]{1,0:T(2,128)S(1)} %copy-done.2, f32[256,128]{1,0:T(8,128)S(1)} %get-tuple-element.19.named_ref, f32[256,128]{1,0:T(8,128)S(1)} %get-tuple-element.20.scale_ref, ...), custom_call_target="tpu_custom_call" | custom-call | flops 1006632960 | tf_op jit(solution)/shard_map/pallas_call | solution.py:280
  12.0 1.4 %collective-permute-done.6 = bf16[2,128,128]{2,1,0:T(8,128)(2,1)S(1)} collective-permute-done((bf16[2,128,128]{2,1,0:T(8,128)(2,1)S(1)}, bf16[2,128,128]{2,1,0:T(8,128)(2,1)S(1)}, u32[]{:S(2)}, u32[]{:S(2)}) %collective-permute-start.6) | collective-permute-done | bytes 65568 | tf_op jit(solution)/shard_map/ppermute | solution.py:222
  13.5 0.7 %convert_add_fusion = f32[2,128,128]{2,1,0:T(8,128)} fusion(f32[2,128,128]{2,1,0:T(8,128)S(1)} %shard_map.70, bf16[2,128,128]{2,1,0:T(8,128)(2,1)S(1)} %collective-permute-done.6), kind=kLoop, calls=%fused_computation | loop fusion | flops 65536 | bytes 327680 | tf_op jit(solution)/shard_map/add | solution.py:287
  (4 shorter events, 0.0 us)
Async XLA Ops:
  0.0 3.6 %copy-start.2 = (s32[2,32]{1,0:T(2,128)S(1)}, s32[2,32]{1,0:T(2,128)}, u32[]{:S(2)}) copy-start(s32[2,32]{1,0:T(2,128)} %pattern_ref.3) | copy-start | bytes 772
  0.0 6.7 %collective-permute-start.4 = (bf16[512,128]{1,0:T(8,128)(2,1)}, bf16[512,128]{1,0:T(8,128)(2,1)S(1)}, u32[]{:S(2)}, u32[]{:S(2)}) collective-permute-start(bf16[512,128]{1,0:T(8,128)(2,1)} %bitcast.3), channel_id=1, source_target_pairs={{0,8},{4,12},{8,0},{12,4},{1,9},{5,13},{9,1},{13,5},{2,10},{6,14},... | collective-permute-start | bytes 393224 | tf_op jit(solution)/shard_map/ppermute | solution.py:222
  3.6 0.9 %copy-start.1 = (bf16[1,4,128,128]{3,2,1,0:T(8,128)(2,1)S(1)}, bf16[1,4,128,128]{3,2,1,0:T(8,128)(2,1)}, u32[]{:S(2)}) copy-start(bf16[1,4,128,128]{3,2,1,0:T(8,128)(2,1)} %param.10) | copy-start | bytes 393220
  3.6 0.9 %copy-start.3 = (s32[128]{0:T(128)S(1)}, s32[128]{0:T(128)}, u32[]{:S(2)}) copy-start(s32[128]{0:T(128)} %param.8) | copy-start | bytes 1540
  3.6 0.9 %copy-start.4 = (s32[128,1]{0,1:T(1,128)S(1)}, s32[128,1]{0,1:T(1,128)}, u32[]{:S(2)}) copy-start(s32[128,1]{0,1:T(1,128)} %param.7) | copy-start | bytes 1540
  3.6 3.0 %copy-start = (bf16[128,4096]{1,0:T(8,128)(2,1)S(1)}, bf16[128,4096]{1,0:T(8,128)(2,1)}, u32[]{:S(2)}) copy-start(bf16[128,4096]{1,0:T(8,128)(2,1)} %own_ref.3) | copy-start | bytes 3145732
  3.7 3.7 %collective-permute-start.1 = (bf16[16,128]{1,0:T(8,128)(2,1)S(1)}, bf16[16,128]{1,0:T(8,128)(2,1)S(1)}, u32[]{:S(2)}, u32[]{:S(2)}) collective-permute-start(bf16[16,128]{1,0:T(8,128)(2,1)S(1)} %shard_map.64.facts_ref), channel_id=1, source_target_pairs={{0,8},{4,12},{8,0},{12,4},{1,9},{5,13},{9,1},{13,5},{2,10},{6,14},... | collective-permute-start | bytes 12296 | tf_op jit(solution)/shard_map/ppermute | solution.py:222
  3.7 3.6 %collective-permute-start = (bf16[128,4096]{1,0:T(8,128)(2,1)}, bf16[128,4096]{1,0:T(8,128)(2,1)S(1)}, u32[]{:S(2)}, u32[]{:S(2)}) collective-permute-start(bf16[128,4096]{1,0:T(8,128)(2,1)} %own_ref.3), channel_id=1, source_target_pairs={{0,4},{4,0},{8,12},{12,8},{1,5},{5,1},{9,13},{13,9},{2,6},{6,2},{1... | collective-permute-start | bytes 3145736 | tf_op jit(solution)/shard_map/ppermute | solution.py:219
  4.5 3.5 %collective-permute-start.3 = (bf16[16,128]{1,0:T(8,128)(2,1)S(1)}, bf16[16,128]{1,0:T(8,128)(2,1)S(1)}, u32[]{:S(2)}, u32[]{:S(2)}) collective-permute-start(bf16[16,128]{1,0:T(8,128)(2,1)S(1)} %get-tuple-element.18), channel_id=1, source_target_pairs={{0,12},{4,8},{8,4},{12,0},{1,13},{5,9},{9,5},{13,1},{2,14},{6,10},... | collective-permute-start | bytes 12296 | tf_op jit(solution)/shard_map/ppermute | solution.py:222
  6.0 2.0 %collective-permute-start.2 = (bf16[528,128]{1,0:T(8,128)(2,1)S(1)}, bf16[528,128]{1,0:T(8,128)(2,1)S(1)}, u32[]{:S(2)}, u32[]{:S(2)}) collective-permute-start(bf16[528,128]{1,0:T(8,128)(2,1)S(1)} %get-tuple-element.17.packet_ref.after_ref.refs_0_), channel_id=1, source_target_pairs={{0,4},{4,0},{8,12},{12,8},{1,5},{5,1},{9,13},{13,9},{2,6},{6,2},{1... | collective-permute-start | bytes 405512 | tf_op jit(solution)/shard_map/ppermute | solution.py:219
  6.7 1.8 %collective-permute-start.5 = (bf16[512,128]{1,0:T(8,128)(2,1)S(1)}, bf16[512,128]{1,0:T(8,128)(2,1)S(1)}, u32[]{:S(2)}, u32[]{:S(2)}) collective-permute-start(bf16[512,128]{1,0:T(8,128)(2,1)S(1)} %shard_map.69), channel_id=1, source_target_pairs={{0,4},{4,0},{8,12},{12,8},{1,5},{5,1},{9,13},{13,9},{2,6},{6,2},{1... | collective-permute-start | bytes 393224 | tf_op jit(solution)/shard_map/ppermute | solution.py:219
  9.1 4.3 %collective-permute-start.6 = (bf16[2,128,128]{2,1,0:T(8,128)(2,1)S(1)}, bf16[2,128,128]{2,1,0:T(8,128)(2,1)S(1)}, u32[]{:S(2)}, u32[]{:S(2)}) collective-permute-start(bf16[2,128,128]{2,1,0:T(8,128)(2,1)S(1)} %shard_map.71), channel_id=1, source_target_pairs={{0,8},{4,12},{8,0},{12,4},{1,9},{5,13},{9,1},{13,5},{2,10},{6,14},... | collective-permute-start | bytes 196616 | tf_op jit(solution)/shard_map/ppermute | solution.py:222

commit v6 on v5

--- a/solution.py
+++ b/solution.py
@@ -15,9 +15,9 @@
 SUB = 16
 DEPTH = NPAT * BAND
 INFO_COST = 55 * 10**7
-BEGIN_COST = 8 * 10**8
+SCALE_COST = 8 * 10**8
 FACTS_COST = 2 * 10**8
-CHOICE_COST = 6 * 10**9
+NEWS_COST = 6 * 10**9
 RELAY_COST = 5 * 10**9
 F32 = jnp.float32
 BF16 = jnp.bfloat16
@@ -154,30 +154,31 @@
     out_ref[...] = weight_ref[...]
 
 
-def sums_kernel(own_ref, near_ref, facts_ref, hi_ref, lo_ref):
-    tiles = hi_ref.shape[0] // (2 * own_ref.shape[0])
+def begin_kernel(chips, own_ref, near_ref, facts_ref, packet_ref, near_packet_ref,
+                 total_ref, hi_ref, lo_ref, named_ref, binning_ref):
+    traces = own_ref.shape[0]
+    tiles = hi_ref.shape[0] // (2 * traces)
     chosen = choice(facts_ref[...].astype(F32)[8 : 8 + tiles, 0:BANDS])
     band_sums(chosen, own_ref, near_ref, hi_ref, lo_ref, tiles)
-
-
-def begin_kernel(chips, hi_ref, lo_ref, packet_ref, near_packet_ref, *refs):
-    facts, (total_ref, scale_ref, named_ref, binning_ref) = refs[:-4], refs[-4:]
-    traces = named_ref.shape[0] // 2
-    tiles = hi_ref.shape[0] // (2 * traces)
-    folds = []
     for half, ref in enumerate((packet_ref, near_packet_ref)):
         at = half * traces
         info = ref[DEPTH:].astype(F32)
         place = lax.broadcasted_iota(jnp.int32, (MB, traces), 0).astype(F32)
         binning_ref[:, at : at + traces] = jnp.where(place == info[1:2], 1.0, 0.0).astype(BF16)
         named_ref[at : at + traces] = jnp.broadcast_to(info[2:3], (traces, traces)).T
-        folds.append(info[0:1])
+    owners = [owner(chips, 0, 0), owner(chips, 0, 1)]
+    weights = [packet_ref, near_packet_ref]
+    total_ref[...] = weigh(hi_ref, lo_ref, named_ref[...], weights, owners, tiles)
+
+
+def scale_kernel(chips, named_ref, packet_ref, near_packet_ref, *refs):
+    facts, scale_ref = refs[:-1], refs[-1]
+    folds = []
+    for half, ref in enumerate((packet_ref, near_packet_ref)):
+        folds.append(ref[DEPTH:].astype(F32)[0:1])
         for n in range(half * (chips - 1), (half + 1) * (chips - 1)):
             folds.append(facts[n][...].astype(F32)[0:1])
-    named = named_ref[...]
-    owners = [owner(chips, 0, 0), owner(chips, 0, 1)]
-    total_ref[...] = weigh(hi_ref, lo_ref, named, [packet_ref, near_packet_ref], owners, tiles)
-    scale_ref[...] = over_fold(named, folds, all_owners(chips))
+    scale_ref[...] = over_fold(named_ref[...], folds, all_owners(chips))
 
 
 def image_of(total, scale, binning, out_ref):
@@ -253,21 +254,21 @@
         for w in far_weights
     ]
     known = [
-        call(facts_in_kernel, block, flops=CHOICE_COST)(in_specs=[VMEM] * 2, out_specs=VMEM)(traces, x)
+        call(facts_in_kernel, block, flops=NEWS_COST)(in_specs=[VMEM] * 2, out_specs=VMEM)(traces, x)
         for x in far_facts
     ] + cross_facts
     all_begun = []
     for j in hops:
-        its_sums = call(sums_kernel, (sums, sums))(in_specs=[VMEM] * 3, out_specs=[VMEM] * 2)(
-            traces, near_traces, known[j - 1]
-        )
-        begun, scale, named, binning = call(
+        begun, *its_sums, named, binning = call(
             functools.partial(begin_kernel, chips),
-            (total, by_row, by_row, shape((MB, rows), BF16)), flops=BEGIN_COST,
-        )(in_specs=[VMEM] * (4 + len(known)), out_specs=[VMEM] * 4)(
-            *its_sums, packet, near_packet, *known
+            (total, sums, sums, by_row, shape((MB, rows), BF16)),
+        )(in_specs=[VMEM] * 5, out_specs=[VMEM] * 5)(
+            traces, near_traces, known[j - 1], packet, near_packet
         )
         all_begun.append((begun, *its_sums))
+    scale = call(functools.partial(scale_kernel, chips), by_row, flops=SCALE_COST)(
+        in_specs=[VMEM] * (3 + len(known)), out_specs=VMEM
+    )(named, packet, near_packet, *known)
     received = []
     for j in hops:
         begun, *its_sums = all_begun[j - 1]

time: 14.3 us -> 14.3 us (level)
  no operation moved by 1% of the time
where the time goes in v6:
time: 14.3 us; the launch traced here: 14.1 us
  starting transfers between devices  6.09 us (43%)
  Pallas kernels  3.2 us (22%)
  waiting for transfers between devices  2.67 us (19%)
  between operations  0.77 us (5%)
  local copies, waits for them, and re-layouts  0.71 us (5%)
  other arithmetic  0.67 us (5%)
    ppermute x4, starting transfers between devices, far(): lax.ppermute(x, 'off', [(i, (i // 2 + j) % chips * 2 + (i % 2 ^ turn)) fo...  5.93 us
    ppermute x4, waiting for transfers between devices, far(): lax.ppermute(x, 'off', [(i, (i // 2 + j) % chips * 2 + (i % 2 ^ turn)) fo...  2.66 us
    pallas_call x1, Pallas kernels, shards(): call(functools.partial(own_kernel, chips), shape((tiles, MB, PTS), F32),...  1.43 us
    pallas_call x1, Pallas kernels, shards(): call(functools.partial(begin_kernel, chips), (total, sums, sums, by_row,...  1 us
    unnamed x10, local copies, waits for them, and re-layouts  0.71 us
    pallas_call x1, Pallas kernels, shards(): call(functools.partial(finish_kernel, chips), shape((tiles, MB, PTS), BF16))  0.67 us
    add x1, other arithmetic, shards(): image = image + part.astype(F32)  0.67 us
  transfers between devices with their start and end apart: 7, of which 3 were waited for; matrix products, arithmetic and copies ran while one was open for 0% of the time, Pallas kernels for 18%

profile of v6, /device:TPU:0, one launch (start us, length us, event | category | flops | bytes accessed | tf_op | source)
XLA Modules:
  0.0 14.1 jit_solution(16803771987666621424)
XLA Ops:
  0.0 0.0 copy-start.2
  0.0 2.9 %collective-permute-start.4 = (bf16[512,128]{1,0:T(8,128)(2,1)}, bf16[512,128]{1,0:T(8,128)(2,1)S(1)}, u32[]{:S(2)}, u32[]{:S(2)}) collective-permute-start(bf16[512,128]{1,0:T(8,128)(2,1)} %bitcast.3), channel_id=1, source_target_pairs={{0,8},{4,12},{8,0},{12,4},{1,9},{5,13},{9,1},{13,5},{2,10},{6,14},... | collective-permute-start | bytes 393224 | tf_op jit(solution)/shard_map/ppermute | solution.py:223
  3.6 0.0 copy-done.2
  3.6 0.0 copy-start.1
  3.6 0.0 copy-start.3
  3.6 0.0 copy-start.4
  3.6 0.0 copy-start
  3.7 0.1 collective-permute-start.1
  3.7 0.1 collective-permute-start
  3.8 0.7 %copy-done.1 = bf16[1,4,128,128]{3,2,1,0:T(8,128)(2,1)S(1)} copy-done((bf16[1,4,128,128]{3,2,1,0:T(8,128)(2,1)S(1)}, bf16[1,4,128,128]{3,2,1,0:T(8,128)(2,1)}, u32[]{:S(2)}) %copy-start.1) | copy-done | bytes 131096
  4.5 0.0 copy-done.3
  4.5 0.0 copy-done.4
  4.5 1.4 %collective-permute-start.3 = (bf16[16,128]{1,0:T(8,128)(2,1)S(1)}, bf16[16,128]{1,0:T(8,128)(2,1)S(1)}, u32[]{:S(2)}, u32[]{:S(2)}) collective-permute-start(bf16[16,128]{1,0:T(8,128)(2,1)S(1)} %get-tuple-element.16), channel_id=1, source_target_pairs={{0,12},{4,8},{8,4},{12,0},{1,13},{5,9},{9,5},{13,1},{2,14},{6,10},... | collective-permute-start | bytes 12296 | tf_op jit(solution)/shard_map/ppermute | solution.py:223
  6.0 0.0 collective-permute-start.2
  6.0 0.7 %collective-permute-done.4.weight_ref.refs_1_.refs_0_ = bf16[512,128]{1,0:T(8,128)(2,1)S(1)} collective-permute-done((bf16[512,128]{1,0:T(8,128)(2,1)}, bf16[512,128]{1,0:T(8,128)(2,1)S(1)}, u32[]{:S(2)}, u32[]{:S(2)}) %collective-permute-start.4) | collective-permute-done | bytes 131104 | tf_op jit(solution)/shard_map/ppermute | solution.py:223
  6.7 0.0 copy-done
  6.7 0.1 collective-permute-start.5
  6.8 0.5 %collective-permute-done.1.facts_ref = bf16[16,128]{1,0:T(8,128)(2,1)S(1)} collective-permute-done((bf16[16,128]{1,0:T(8,128)(2,1)S(1)}, bf16[16,128]{1,0:T(8,128)(2,1)S(1)}, u32[]{:S(2)}, u32[]{:S(2)}) %collective-permute-start.1) | collective-permute-done | bytes 4128 | tf_op jit(solution)/shard_map/ppermute | solution.py:223
  7.3 0.0 collective-permute-done.2.near_packet_ref.refs_2_
  7.3 0.0 collective-permute-done.near_ref
  7.3 1.0 %shard_map.67 = (f32[512,128]{1,0:T(8,128)S(1)}, bf16[512,512]{1,0:T(8,128)(2,1)S(1)}, bf16[512,512]{1,0:T(8,128)(2,1)S(1)}, f32[256,128]{1,0:T(8,128)S(1)}, bf16[128,256]{1,0:T(8,128)(2,1)S(1)}) custom-call(bf16[128,4096]{1,0:T(8,128)(2,1)S(1)} %copy-done, bf16[128,4096]{1,0:T(8,128)(2,1)S(1)} %collective-permute-done.near_ref, ...), custom_call_target="tpu_custom_call" | custom-call | tf_op jit(solution)/shard_map/pallas_call | solution.py:262
  8.3 0.0 collective-permute-done.3.refs_1_
  8.4 0.1 shard_map.68.scale_ref
  8.4 0.0 collective-permute-done.5.refs_3_.refs_1_
  8.4 0.7 %shard_map.71 = bf16[2,128,128]{2,1,0:T(8,128)(2,1)S(1)} custom-call(bf16[512,512]{1,0:T(8,128)(2,1)S(1)} %get-tuple-element.18.hi_ref, bf16[512,512]{1,0:T(8,128)(2,1)S(1)} %get-tuple-element.19.lo_ref, f32[512,128]{1,0:T(8,128)S(1)} %get-tuple-element.20.total_ref, f32[256,128]{1,0:T(8,128)S(1)} %get-tuple-element.15.named_ref, ...), custom_call_target="tpu_custom_call" | custom-call | tf_op jit(solution)/shard_map/pallas_call | solution.py:276
  9.1 1.5 %collective-permute-start.6 = (bf16[2,128,128]{2,1,0:T(8,128)(2,1)S(1)}, bf16[2,128,128]{2,1,0:T(8,128)(2,1)S(1)}, u32[]{:S(2)}, u32[]{:S(2)}) collective-permute-start(bf16[2,128,128]{2,1,0:T(8,128)(2,1)S(1)} %shard_map.71), channel_id=1, source_target_pairs={{0,8},{4,12},{8,0},{12,4},{1,9},{5,13},{9,1},{13,5},{2,10},{6,14},... | collective-permute-start | bytes 196616 | tf_op jit(solution)/shard_map/ppermute | solution.py:223
  10.6 1.4 %shard_map.70 = f32[2,128,128]{2,1,0:T(8,128)S(1)} custom-call(bf16[128,4096]{1,0:T(8,128)(2,1)S(1)} %copy-done, bf16[128,4096]{1,0:T(8,128)(2,1)S(1)} %collective-permute-done.near_ref, s32[2,32]{1,0:T(2,128)S(1)} %copy-done.2, f32[256,128]{1,0:T(8,128)S(1)} %get-tuple-element.15.named_ref, f32[256,128]{1,0:T(8,128)S(1)} %shard_map.68.scale_ref, ...), custom_call_target="tpu_custom_call" | custom-call | flops 1006632960 | tf_op jit(solution)/shard_map/pallas_call | solution.py:281
  12.0 1.4 %collective-permute-done.6 = bf16[2,128,128]{2,1,0:T(8,128)(2,1)S(1)} collective-permute-done((bf16[2,128,128]{2,1,0:T(8,128)(2,1)S(1)}, bf16[2,128,128]{2,1,0:T(8,128)(2,1)S(1)}, u32[]{:S(2)}, u32[]{:S(2)}) %collective-permute-start.6) | collective-permute-done | bytes 65568 | tf_op jit(solution)/shard_map/ppermute | solution.py:223
  13.4 0.7 %convert_add_fusion = f32[2,128,128]{2,1,0:T(8,128)} fusion(f32[2,128,128]{2,1,0:T(8,128)S(1)} %shard_map.70, bf16[2,128,128]{2,1,0:T(8,128)(2,1)S(1)} %collective-permute-done.6), kind=kLoop, calls=%fused_computation | loop fusion | flops 65536 | bytes 327680 | tf_op jit(solution)/shard_map/add | solution.py:288
  (4 shorter events, 0.0 us)
Async XLA Ops:
  0.0 3.6 %copy-start.2 = (s32[2,32]{1,0:T(2,128)S(1)}, s32[2,32]{1,0:T(2,128)}, u32[]{:S(2)}) copy-start(s32[2,32]{1,0:T(2,128)} %pattern_ref.3) | copy-start | bytes 772
  0.0 6.7 %collective-permute-start.4 = (bf16[512,128]{1,0:T(8,128)(2,1)}, bf16[512,128]{1,0:T(8,128)(2,1)S(1)}, u32[]{:S(2)}, u32[]{:S(2)}) collective-permute-start(bf16[512,128]{1,0:T(8,128)(2,1)} %bitcast.3), channel_id=1, source_target_pairs={{0,8},{4,12},{8,0},{12,4},{1,9},{5,13},{9,1},{13,5},{2,10},{6,14},... | collective-permute-start | bytes 393224 | tf_op jit(solution)/shard_map/ppermute | solution.py:223
  3.6 0.9 %copy-start.1 = (bf16[1,4,128,128]{3,2,1,0:T(8,128)(2,1)S(1)}, bf16[1,4,128,128]{3,2,1,0:T(8,128)(2,1)}, u32[]{:S(2)}) copy-start(bf16[1,4,128,128]{3,2,1,0:T(8,128)(2,1)} %param.10) | copy-start | bytes 393220
  3.6 0.9 %copy-start.3 = (s32[128]{0:T(128)S(1)}, s32[128]{0:T(128)}, u32[]{:S(2)}) copy-start(s32[128]{0:T(128)} %param.8) | copy-start | bytes 1540
  3.6 0.9 %copy-start.4 = (s32[128,1]{0,1:T(1,128)S(1)}, s32[128,1]{0,1:T(1,128)}, u32[]{:S(2)}) copy-start(s32[128,1]{0,1:T(1,128)} %param.7) | copy-start | bytes 1540
  3.6 3.0 %copy-start = (bf16[128,4096]{1,0:T(8,128)(2,1)S(1)}, bf16[128,4096]{1,0:T(8,128)(2,1)}, u32[]{:S(2)}) copy-start(bf16[128,4096]{1,0:T(8,128)(2,1)} %own_ref.3) | copy-start | bytes 3145732
  3.7 3.7 %collective-permute-start.1 = (bf16[16,128]{1,0:T(8,128)(2,1)S(1)}, bf16[16,128]{1,0:T(8,128)(2,1)S(1)}, u32[]{:S(2)}, u32[]{:S(2)}) collective-permute-start(bf16[16,128]{1,0:T(8,128)(2,1)S(1)} %shard_map.64.facts_ref), channel_id=1, source_target_pairs={{0,8},{4,12},{8,0},{12,4},{1,9},{5,13},{9,1},{13,5},{2,10},{6,14},... | collective-permute-start | bytes 12296 | tf_op jit(solution)/shard_map/ppermute | solution.py:223
  3.7 3.6 %collective-permute-start = (bf16[128,4096]{1,0:T(8,128)(2,1)}, bf16[128,4096]{1,0:T(8,128)(2,1)S(1)}, u32[]{:S(2)}, u32[]{:S(2)}) collective-permute-start(bf16[128,4096]{1,0:T(8,128)(2,1)} %own_ref.3), channel_id=1, source_target_pairs={{0,4},{4,0},{8,12},{12,8},{1,5},{5,1},{9,13},{13,9},{2,6},{6,2},{1... | collective-permute-start | bytes 3145736 | tf_op jit(solution)/shard_map/ppermute | solution.py:220
  4.5 3.8 %collective-permute-start.3 = (bf16[16,128]{1,0:T(8,128)(2,1)S(1)}, bf16[16,128]{1,0:T(8,128)(2,1)S(1)}, u32[]{:S(2)}, u32[]{:S(2)}) collective-permute-start(bf16[16,128]{1,0:T(8,128)(2,1)S(1)} %get-tuple-element.16), channel_id=1, source_target_pairs={{0,12},{4,8},{8,4},{12,0},{1,13},{5,9},{9,5},{13,1},{2,14},{6,10},... | collective-permute-start | bytes 12296 | tf_op jit(solution)/shard_map/ppermute | solution.py:223
  6.0 1.4 %collective-permute-start.2 = (bf16[528,128]{1,0:T(8,128)(2,1)S(1)}, bf16[528,128]{1,0:T(8,128)(2,1)S(1)}, u32[]{:S(2)}, u32[]{:S(2)}) collective-permute-start(bf16[528,128]{1,0:T(8,128)(2,1)S(1)} %get-tuple-element.14.packet_ref.after_ref.refs_0_), channel_id=1, source_target_pairs={{0,4},{4,0},{8,12},{12,8},{1,5},{5,1},{9,13},{13,9},{2,6},{6,2},{1... | collective-permute-start | bytes 405512 | tf_op jit(solution)/shard_map/ppermute | solution.py:220
  6.7 1.7 %collective-permute-start.5 = (bf16[512,128]{1,0:T(8,128)(2,1)S(1)}, bf16[512,128]{1,0:T(8,128)(2,1)S(1)}, u32[]{:S(2)}, u32[]{:S(2)}) collective-permute-start(bf16[512,128]{1,0:T(8,128)(2,1)S(1)} %shard_map.69), channel_id=1, source_target_pairs={{0,4},{4,0},{8,12},{12,8},{1,5},{5,1},{9,13},{13,9},{2,6},{6,2},{1... | collective-permute-start | bytes 393224 | tf_op jit(solution)/shard_map/ppermute | solution.py:220
  9.1 4.3 %collective-permute-start.6 = (bf16[2,128,128]{2,1,0:T(8,128)(2,1)S(1)}, bf16[2,128,128]{2,1,0:T(8,128)(2,1)S(1)}, u32[]{:S(2)}, u32[]{:S(2)}) collective-permute-start(bf16[2,128,128]{2,1,0:T(8,128)(2,1)S(1)} %shard_map.71), channel_id=1, source_target_pairs={{0,8},{4,12},{8,0},{12,4},{1,9},{5,13},{9,1},{13,5},{2,10},{6,14},... | collective-permute-start | bytes 196616 | tf_op jit(solution)/shard_map/ppermute | solution.py:223

commit v7 on v6

--- a/solution.py
+++ b/solution.py
@@ -44,13 +44,15 @@
     facts_ref[...] = facts[...].astype(BF16)
 
 
-def packet_kernel(facts_ref, weight_ref, bins_ref, class_ref, packet_ref, again_ref, info):
+def packet_kernel(facts_ref, weight_ref, bins_ref, class_ref,
+                  packet_ref, again_ref, spread_ref, code_ref, info):
     packet_ref[0:DEPTH] = weight_ref[...]
     info[...] = facts_ref[...].astype(F32)
     info[1:2] = bins_ref[...].astype(F32)
     info[2:3] = class_ref[...].astype(F32)
     packet_ref[DEPTH:] = info[...].astype(BF16)
     again_ref[...] = facts_ref[...]
+    masks(spread_ref, code_ref)
 
 
 def owner(chips, j, turn):
@@ -60,21 +62,23 @@
     return chip * 2 + (1 - core if turn else core)
 
 
-def choice(pattern):
-    depth = BANDS * SUB
+def masks(spread_ref, code_ref):
+    shape = spread_ref.shape
+    band = lax.broadcasted_iota(jnp.int32, shape, 0)
+    column = lax.broadcasted_iota(jnp.int32, shape, 1)
+    spread_ref[...] = jnp.where(column // SUB == band, 1.0, 0.0).astype(BF16)
+    row = lax.broadcasted_iota(jnp.int32, code_ref.shape, 0)
+    col = lax.broadcasted_iota(jnp.int32, code_ref.shape, 1)
+    code_ref[...] = jnp.where(row % SUB == col % SUB, (row // SUB + 1).astype(F32), -1.0)
+
+
+def choice(pattern, spread, code):
     tiles = pattern.shape[0]
-    band = lax.broadcasted_iota(jnp.int32, (BANDS, depth), 0)
-    column = lax.broadcasted_iota(jnp.int32, (BANDS, depth), 1)
-    spread = jnp.where(column // SUB == band, 1.0, 0.0).astype(BF16)
     padded = jnp.concatenate([pattern] * (8 // tiles), axis=0).astype(BF16)
     wide = jnp.dot(padded, spread, preferred_element_type=F32)
-    row = lax.broadcasted_iota(jnp.int32, (NPAT * SUB, depth), 0)
-    col = lax.broadcasted_iota(jnp.int32, (NPAT * SUB, depth), 1)
-    value = (row // SUB + 1).astype(F32)
-    same = row % SUB == col % SUB
     return jnp.concatenate(
         [
-            jnp.where(same & (jnp.broadcast_to(wide[g : g + 1], (NPAT * SUB, depth)) == value), 1.0, 0.0)
+            jnp.where(jnp.broadcast_to(wide[g : g + 1], code.shape) == code, 1.0, 0.0)
             for g in range(tiles)
         ],
         axis=0,
@@ -154,11 +158,11 @@
     out_ref[...] = weight_ref[...]
 
 
-def begin_kernel(chips, own_ref, near_ref, facts_ref, packet_ref, near_packet_ref,
+def begin_kernel(chips, own_ref, near_ref, facts_ref, packet_ref, near_packet_ref, spread_ref, code_ref,
                  total_ref, hi_ref, lo_ref, named_ref, binning_ref):
     traces = own_ref.shape[0]
     tiles = hi_ref.shape[0] // (2 * traces)
-    chosen = choice(facts_ref[...].astype(F32)[8 : 8 + tiles, 0:BANDS])
+    chosen = choice(facts_ref[...].astype(F32)[8 : 8 + tiles, 0:BANDS], spread_ref[...], code_ref[...])
     band_sums(chosen, own_ref, near_ref, hi_ref, lo_ref, tiles)
     for half, ref in enumerate((packet_ref, near_packet_ref)):
         at = half * traces
@@ -200,10 +204,10 @@
     image_of(total, scale_ref[...], binning_ref[...], out_ref)
 
 
-def own_kernel(chips, own_ref, near_ref, pattern_ref, named_ref, scale_ref, binning_ref, *refs):
+def own_kernel(chips, own_ref, near_ref, pattern_ref, spread_ref, code_ref, named_ref, scale_ref, binning_ref, *refs):
     weights, (out_ref, hi_ref, lo_ref) = refs[:-3], refs[-3:]
     tiles = out_ref.shape[0]
-    chosen = choice(pattern_ref[...].astype(F32))
+    chosen = choice(pattern_ref[...].astype(F32), spread_ref[...], code_ref[...])
     band_sums(chosen, own_ref, near_ref, hi_ref, lo_ref, tiles)
     total = weigh(hi_ref, lo_ref, named_ref[...], weights, all_owners(chips), tiles)
     image_of(total, scale_ref[...], binning_ref[...], out_ref)
@@ -234,9 +238,11 @@
     far_facts = [far(facts, j) for j in hops]
     tied, _ = lax.optimization_barrier((traces, facts))
     near_traces = near(tied)
-    packet, again = call(
-        packet_kernel, (shape((DEPTH + SUB, PTS), BF16), block), [pltpu.VMEM(block.shape, F32)], flops=INFO_COST
-    )(in_specs=[VMEM] * 4, out_specs=[VMEM] * 2)(
+    packet, again, *made = call(
+        packet_kernel,
+        (shape((DEPTH + SUB, PTS), BF16), block, shape((BANDS, BANDS * SUB), BF16),
+         shape((NPAT * SUB, BANDS * SUB), F32)), [pltpu.VMEM(block.shape, F32)], flops=INFO_COST
+    )(in_specs=[VMEM] * 4, out_specs=[VMEM] * 4)(
         facts, weights, mid_bins.reshape(1, tr_dev), class_map.reshape(1, tr_dev)
     )
     near_packet = near(packet)
@@ -262,8 +268,8 @@
         begun, *its_sums, named, binning = call(
             functools.partial(begin_kernel, chips),
             (total, sums, sums, by_row, shape((MB, rows), BF16)),
-        )(in_specs=[VMEM] * 5, out_specs=[VMEM] * 5)(
-            traces, near_traces, known[j - 1], packet, near_packet
+        )(in_specs=[VMEM] * 7, out_specs=[VMEM] * 5)(
+            traces, near_traces, known[j - 1], packet, near_packet, *made
         )
         all_begun.append((begun, *its_sums))
     scale = call(functools.partial(scale_kernel, chips), by_row, flops=SCALE_COST)(
@@ -281,8 +287,8 @@
     image = call(
         functools.partial(own_kernel, chips), shape((tiles, MB, PTS), F32),
         [pltpu.VMEM(sums.shape, BF16)] * 2, flops=15 * work,
-    )(in_specs=[VMEM] * (6 + len(rest)), out_specs=VMEM)(
-        traces, near_traces, apertures, named, scale, binning, *rest
+    )(in_specs=[VMEM] * (8 + len(rest)), out_specs=VMEM)(
+        traces, near_traces, apertures, *made, named, scale, binning, *rest
     )
     for part in received:
         image = image + part.astype(F32)

time: 14.3 us -> 14.2 us (level)
  no operation moved by 1% of the time
where the time goes in v7:
time: 14.2 us; the launch traced here: 14.1 us
  starting transfers between devices  6.12 us (43%)
  Pallas kernels  3.2 us (23%)
  waiting for transfers between devices  2.61 us (18%)
  between operations  0.77 us (5%)
  local copies, waits for them, and re-layouts  0.71 us (5%)
  other arithmetic  0.67 us (5%)
    ppermute x4, starting transfers between devices, far(): lax.ppermute(x, 'off', [(i, (i // 2 + j) % chips * 2 + (i % 2 ^ turn)) fo...  5.96 us
    ppermute x4, waiting for transfers between devices, far(): lax.ppermute(x, 'off', [(i, (i // 2 + j) % chips * 2 + (i % 2 ^ turn)) fo...  2.61 us
    pallas_call x1, Pallas kernels, shards(): call(functools.partial(own_kernel, chips), shape((tiles, MB, PTS), F32),...  1.45 us
    pallas_call x1, Pallas kernels, shards(): call(functools.partial(begin_kernel, chips), (total, sums, sums, by_row,...  0.97 us
    unnamed x10, local copies, waits for them, and re-layouts  0.71 us
    pallas_call x1, Pallas kernels, shards(): call(functools.partial(finish_kernel, chips), shape((tiles, MB, PTS), BF16))  0.68 us
    add x1, other arithmetic, shards(): image = image + part.astype(F32)  0.67 us
  transfers between devices with their start and end apart: 7, of which 3 were waited for; matrix products, arithmetic and copies ran while one was open for 0% of the time, Pallas kernels for 18%

profile of v7, /device:TPU:0, one launch (start us, length us, event | category | flops | bytes accessed | tf_op | source)
XLA Modules:
  0.0 14.1 jit_solution(2149812372470050842)
XLA Ops:
  0.0 0.0 copy-start.2
  0.0 2.9 %collective-permute-start.4 = (bf16[512,128]{1,0:T(8,128)(2,1)}, bf16[512,128]{1,0:T(8,128)(2,1)S(1)}, u32[]{:S(2)}, u32[]{:S(2)}) collective-permute-start(bf16[512,128]{1,0:T(8,128)(2,1)} %bitcast.3), channel_id=1, source_target_pairs={{0,8},{4,12},{8,0},{12,4},{1,9},{5,13},{9,1},{13,5},{2,10},{6,14},... | collective-permute-start | bytes 393224 | tf_op jit(solution)/shard_map/ppermute | solution.py:227
  3.6 0.0 copy-done.2
  3.6 0.0 copy-start.1
  3.6 0.0 copy-start.3
  3.6 0.0 copy-start.4
  3.6 0.0 copy-start
  3.7 0.1 collective-permute-start.1
  3.7 0.1 collective-permute-start
  3.8 0.7 %copy-done.1 = bf16[1,4,128,128]{3,2,1,0:T(8,128)(2,1)S(1)} copy-done((bf16[1,4,128,128]{3,2,1,0:T(8,128)(2,1)S(1)}, bf16[1,4,128,128]{3,2,1,0:T(8,128)(2,1)}, u32[]{:S(2)}) %copy-start.1) | copy-done | bytes 131096
  4.5 0.0 copy-done.3
  4.5 0.0 copy-done.4
  4.5 1.4 %collective-permute-start.3 = (bf16[16,128]{1,0:T(8,128)(2,1)S(1)}, bf16[16,128]{1,0:T(8,128)(2,1)S(1)}, u32[]{:S(2)}, u32[]{:S(2)}) collective-permute-start(bf16[16,128]{1,0:T(8,128)(2,1)S(1)} %get-tuple-element.20), channel_id=1, source_target_pairs={{0,12},{4,8},{8,4},{12,0},{1,13},{5,9},{9,5},{13,1},{2,14},{6,10},... | collective-permute-start | bytes 12296 | tf_op jit(solution)/shard_map/ppermute | solution.py:227
  6.0 0.0 collective-permute-start.2
  6.0 0.7 %collective-permute-done.4.weight_ref.refs_1_.refs_0_ = bf16[512,128]{1,0:T(8,128)(2,1)S(1)} collective-permute-done((bf16[512,128]{1,0:T(8,128)(2,1)}, bf16[512,128]{1,0:T(8,128)(2,1)S(1)}, u32[]{:S(2)}, u32[]{:S(2)}) %collective-permute-start.4) | collective-permute-done | bytes 131104 | tf_op jit(solution)/shard_map/ppermute | solution.py:227
  6.7 0.0 copy-done
  6.7 0.1 collective-permute-start.5
  6.8 0.5 %collective-permute-done.1.facts_ref = bf16[16,128]{1,0:T(8,128)(2,1)S(1)} collective-permute-done((bf16[16,128]{1,0:T(8,128)(2,1)S(1)}, bf16[16,128]{1,0:T(8,128)(2,1)S(1)}, u32[]{:S(2)}, u32[]{:S(2)}) %collective-permute-start.1) | collective-permute-done | bytes 4128 | tf_op jit(solution)/shard_map/ppermute | solution.py:227
  7.3 0.0 collective-permute-done.2.near_packet_ref.refs_2_
  7.3 0.0 collective-permute-done.near_ref
  7.3 1.0 %shard_map.67 = (f32[512,128]{1,0:T(8,128)S(1)}, bf16[512,512]{1,0:T(8,128)(2,1)S(1)}, bf16[512,512]{1,0:T(8,128)(2,1)S(1)}, f32[256,128]{1,0:T(8,128)S(1)}, bf16[128,256]{1,0:T(8,128)(2,1)S(1)}) custom-call(bf16[128,4096]{1,0:T(8,128)(2,1)S(1)} %copy-done, bf16[128,4096]{1,0:T(8,128)(2,1)S(1)} %collective-permute-done.near_ref, ...), custom_call_target="tpu_custom_call" | custom-call | tf_op jit(solution)/shard_map/pallas_call | solution.py:268
  8.3 0.0 collective-permute-done.3.refs_1_
  8.3 0.1 shard_map.68.scale_ref
  8.4 0.0 collective-permute-done.5.refs_3_.refs_1_
  8.4 0.7 %shard_map.71 = bf16[2,128,128]{2,1,0:T(8,128)(2,1)S(1)} custom-call(bf16[512,512]{1,0:T(8,128)(2,1)S(1)} %get-tuple-element.22.hi_ref, bf16[512,512]{1,0:T(8,128)(2,1)S(1)} %get-tuple-element.23.lo_ref, f32[512,128]{1,0:T(8,128)S(1)} %get-tuple-element.24.total_ref, f32[256,128]{1,0:T(8,128)S(1)} %get-tuple-element.19.named_ref, ...), custom_call_target="tpu_custom_call" | custom-call | tf_op jit(solution)/shard_map/pallas_call | solution.py:282
  9.1 1.5 %collective-permute-start.6 = (bf16[2,128,128]{2,1,0:T(8,128)(2,1)S(1)}, bf16[2,128,128]{2,1,0:T(8,128)(2,1)S(1)}, u32[]{:S(2)}, u32[]{:S(2)}) collective-permute-start(bf16[2,128,128]{2,1,0:T(8,128)(2,1)S(1)} %shard_map.71), channel_id=1, source_target_pairs={{0,8},{4,12},{8,0},{12,4},{1,9},{5,13},{9,1},{13,5},{2,10},{6,14},... | collective-permute-start | bytes 196616 | tf_op jit(solution)/shard_map/ppermute | solution.py:227
  10.6 1.4 %shard_map.70 = f32[2,128,128]{2,1,0:T(8,128)S(1)} custom-call(bf16[128,4096]{1,0:T(8,128)(2,1)S(1)} %copy-done, bf16[128,4096]{1,0:T(8,128)(2,1)S(1)} %collective-permute-done.near_ref, s32[2,32]{1,0:T(2,128)S(1)} %copy-done.2, bf16[32,512]{1,0:T(8,128)(2,1)S(1)} %get-tuple-element.16.spread_ref, f32[64,512]{1,0:T(8,128)S(1)} %get-tuple-element.17.code_ref, ...), custom_call_target="tpu_custom_call" | custom-call | flops 1006632960 | tf_op jit(solution)/shard_map/pallas_call | solution.py:287
  12.1 1.4 %collective-permute-done.6 = bf16[2,128,128]{2,1,0:T(8,128)(2,1)S(1)} collective-permute-done((bf16[2,128,128]{2,1,0:T(8,128)(2,1)S(1)}, bf16[2,128,128]{2,1,0:T(8,128)(2,1)S(1)}, u32[]{:S(2)}, u32[]{:S(2)}) %collective-permute-start.6) | collective-permute-done | bytes 65568 | tf_op jit(solution)/shard_map/ppermute | solution.py:227
  13.4 0.7 %convert_add_fusion = f32[2,128,128]{2,1,0:T(8,128)} fusion(f32[2,128,128]{2,1,0:T(8,128)S(1)} %shard_map.70, bf16[2,128,128]{2,1,0:T(8,128)(2,1)S(1)} %collective-permute-done.6), kind=kLoop, calls=%fused_computation | loop fusion | flops 65536 | bytes 327680 | tf_op jit(solution)/shard_map/add | solution.py:294
  (4 shorter events, 0.0 us)
Async XLA Ops:
  0.0 3.6 %copy-start.2 = (s32[2,32]{1,0:T(2,128)S(1)}, s32[2,32]{1,0:T(2,128)}, u32[]{:S(2)}) copy-start(s32[2,32]{1,0:T(2,128)} %pattern_ref.3) | copy-start | bytes 772
  0.0 6.7 %collective-permute-start.4 = (bf16[512,128]{1,0:T(8,128)(2,1)}, bf16[512,128]{1,0:T(8,128)(2,1)S(1)}, u32[]{:S(2)}, u32[]{:S(2)}) collective-permute-start(bf16[512,128]{1,0:T(8,128)(2,1)} %bitcast.3), channel_id=1, source_target_pairs={{0,8},{4,12},{8,0},{12,4},{1,9},{5,13},{9,1},{13,5},{2,10},{6,14},... | collective-permute-start | bytes 393224 | tf_op jit(solution)/shard_map/ppermute | solution.py:227
  3.6 0.9 %copy-start.1 = (bf16[1,4,128,128]{3,2,1,0:T(8,128)(2,1)S(1)}, bf16[1,4,128,128]{3,2,1,0:T(8,128)(2,1)}, u32[]{:S(2)}) copy-start(bf16[1,4,128,128]{3,2,1,0:T(8,128)(2,1)} %param.10) | copy-start | bytes 393220
  3.6 0.9 %copy-start.3 = (s32[128]{0:T(128)S(1)}, s32[128]{0:T(128)}, u32[]{:S(2)}) copy-start(s32[128]{0:T(128)} %param.8) | copy-start | bytes 1540
  3.6 0.9 %copy-start.4 = (s32[128,1]{0,1:T(1,128)S(1)}, s32[128,1]{0,1:T(1,128)}, u32[]{:S(2)}) copy-start(s32[128,1]{0,1:T(1,128)} %param.7) | copy-start | bytes 1540
  3.6 3.0 %copy-start = (bf16[128,4096]{1,0:T(8,128)(2,1)S(1)}, bf16[128,4096]{1,0:T(8,128)(2,1)}, u32[]{:S(2)}) copy-start(bf16[128,4096]{1,0:T(8,128)(2,1)} %own_ref.3) | copy-start | bytes 3145732
  3.7 3.7 %collective-permute-start.1 = (bf16[16,128]{1,0:T(8,128)(2,1)S(1)}, bf16[16,128]{1,0:T(8,128)(2,1)S(1)}, u32[]{:S(2)}, u32[]{:S(2)}) collective-permute-start(bf16[16,128]{1,0:T(8,128)(2,1)S(1)} %shard_map.64.facts_ref), channel_id=1, source_target_pairs={{0,8},{4,12},{8,0},{12,4},{1,9},{5,13},{9,1},{13,5},{2,10},{6,14},... | collective-permute-start | bytes 12296 | tf_op jit(solution)/shard_map/ppermute | solution.py:227
  3.7 3.6 %collective-permute-start = (bf16[128,4096]{1,0:T(8,128)(2,1)}, bf16[128,4096]{1,0:T(8,128)(2,1)S(1)}, u32[]{:S(2)}, u32[]{:S(2)}) collective-permute-start(bf16[128,4096]{1,0:T(8,128)(2,1)} %own_ref.3), channel_id=1, source_target_pairs={{0,4},{4,0},{8,12},{12,8},{1,5},{5,1},{9,13},{13,9},{2,6},{6,2},{1... | collective-permute-start | bytes 3145736 | tf_op jit(solution)/shard_map/ppermute | solution.py:224
  4.5 3.8 %collective-permute-start.3 = (bf16[16,128]{1,0:T(8,128)(2,1)S(1)}, bf16[16,128]{1,0:T(8,128)(2,1)S(1)}, u32[]{:S(2)}, u32[]{:S(2)}) collective-permute-start(bf16[16,128]{1,0:T(8,128)(2,1)S(1)} %get-tuple-element.20), channel_id=1, source_target_pairs={{0,12},{4,8},{8,4},{12,0},{1,13},{5,9},{9,5},{13,1},{2,14},{6,10},... | collective-permute-start | bytes 12296 | tf_op jit(solution)/shard_map/ppermute | solution.py:227
  6.0 1.4 %collective-permute-start.2 = (bf16[528,128]{1,0:T(8,128)(2,1)S(1)}, bf16[528,128]{1,0:T(8,128)(2,1)S(1)}, u32[]{:S(2)}, u32[]{:S(2)}) collective-permute-start(bf16[528,128]{1,0:T(8,128)(2,1)S(1)} %get-tuple-element.18.packet_ref.after_ref.refs_0_), channel_id=1, source_target_pairs={{0,4},{4,0},{8,12},{12,8},{1,5},{5,1},{9,13},{13,9},{2,6},{6,2},{1... | collective-permute-start | bytes 405512 | tf_op jit(solution)/shard_map/ppermute | solution.py:224
  6.7 1.7 %collective-permute-start.5 = (bf16[512,128]{1,0:T(8,128)(2,1)S(1)}, bf16[512,128]{1,0:T(8,128)(2,1)S(1)}, u32[]{:S(2)}, u32[]{:S(2)}) collective-permute-start(bf16[512,128]{1,0:T(8,128)(2,1)S(1)} %shard_map.69), channel_id=1, source_target_pairs={{0,4},{4,0},{8,12},{12,8},{1,5},{5,1},{9,13},{13,9},{2,6},{6,2},{1... | collective-permute-start | bytes 393224 | tf_op jit(solution)/shard_map/ppermute | solution.py:224
  9.1 4.3 %collective-permute-start.6 = (bf16[2,128,128]{2,1,0:T(8,128)(2,1)S(1)}, bf16[2,128,128]{2,1,0:T(8,128)(2,1)S(1)}, u32[]{:S(2)}, u32[]{:S(2)}) collective-permute-start(bf16[2,128,128]{2,1,0:T(8,128)(2,1)S(1)} %shard_map.71), channel_id=1, source_target_pairs={{0,8},{4,12},{8,0},{12,4},{1,9},{5,13},{9,1},{13,5},{2,10},{6,14},... | collective-permute-start | bytes 196616 | tf_op jit(solution)/shard_map/ppermute | solution.py:227

commit v8 on v7

--- a/solution.py
+++ b/solution.py
@@ -175,14 +175,13 @@
     total_ref[...] = weigh(hi_ref, lo_ref, named_ref[...], weights, owners, tiles)
 
 
-def scale_kernel(chips, named_ref, packet_ref, near_packet_ref, *refs):
-    facts, scale_ref = refs[:-1], refs[-1]
+def fold_scale(chips, named, packets, facts):
     folds = []
-    for half, ref in enumerate((packet_ref, near_packet_ref)):
+    for half, ref in enumerate(packets):
         folds.append(ref[DEPTH:].astype(F32)[0:1])
         for n in range(half * (chips - 1), (half + 1) * (chips - 1)):
             folds.append(facts[n][...].astype(F32)[0:1])
-    scale_ref[...] = over_fold(named_ref[...], folds, all_owners(chips))
+    return over_fold(named, folds, all_owners(chips))
 
 
 def image_of(total, scale, binning, out_ref):
@@ -197,20 +196,25 @@
     return [owner(chips, n, turn) for turn in range(2) for n in range(chips)]
 
 
-def finish_kernel(chips, hi_ref, lo_ref, total_ref, named_ref, scale_ref, binning_ref, *refs):
-    weights, out_ref = refs[:-1], refs[-1]
+def finish_kernel(chips, hi_ref, lo_ref, total_ref, named_ref, binning_ref, *refs):
+    packets, refs, out_ref = refs[:2], refs[2:-1], refs[-1]
+    facts, weights = refs[: 2 * (chips - 1)], refs[2 * (chips - 1) :]
+    named = named_ref[...]
     owners = [owner(chips, n, turn) for turn in range(2) for n in range(1, chips)]
-    total = total_ref[...] + weigh(hi_ref, lo_ref, named_ref[...], weights, owners, out_ref.shape[0])
-    image_of(total, scale_ref[...], binning_ref[...], out_ref)
-
-
-def own_kernel(chips, own_ref, near_ref, pattern_ref, spread_ref, code_ref, named_ref, scale_ref, binning_ref, *refs):
+    scale = fold_scale(chips, named, packets, facts)
+    total = total_ref[...] + weigh(hi_ref, lo_ref, named, weights, owners, out_ref.shape[0])
+    image_of(total, scale, binning_ref[...], out_ref)
+
+
+def own_kernel(chips, own_ref, near_ref, pattern_ref, spread_ref, code_ref, named_ref, binning_ref, *refs):
+    facts, refs = refs[: 2 * (chips - 1)], refs[2 * (chips - 1) :]
     weights, (out_ref, hi_ref, lo_ref) = refs[:-3], refs[-3:]
     tiles = out_ref.shape[0]
     chosen = choice(pattern_ref[...].astype(F32), spread_ref[...], code_ref[...])
     band_sums(chosen, own_ref, near_ref, hi_ref, lo_ref, tiles)
     total = weigh(hi_ref, lo_ref, named_ref[...], weights, all_owners(chips), tiles)
-    image_of(total, scale_ref[...], binning_ref[...], out_ref)
+    scale = fold_scale(chips, named_ref[...], (weights[0], weights[chips]), facts)
+    image_of(total, scale, binning_ref[...], out_ref)
 
 
 def shards(traces, class_map, mid_bins, fold_count, weight_tiles, apertures):
@@ -262,7 +266,7 @@
     known = [
         call(facts_in_kernel, block, flops=NEWS_COST)(in_specs=[VMEM] * 2, out_specs=VMEM)(traces, x)
         for x in far_facts
-    ] + cross_facts
+    ]
     all_begun = []
     for j in hops:
         begun, *its_sums, named, binning = call(
@@ -272,23 +276,26 @@
             traces, near_traces, known[j - 1], packet, near_packet, *made
         )
         all_begun.append((begun, *its_sums))
-    scale = call(functools.partial(scale_kernel, chips), by_row, flops=SCALE_COST)(
-        in_specs=[VMEM] * (3 + len(known)), out_specs=VMEM
-    )(named, packet, near_packet, *known)
+    known += [
+        call(facts_in_kernel, block, flops=SCALE_COST)(in_specs=[ANY, VMEM], out_specs=VMEM)(
+            all_begun[0][0], x
+        )
+        for x in cross_facts
+    ]
     received = []
     for j in hops:
         begun, *its_sums = all_begun[j - 1]
-        rest = [begun, named, scale, binning] + far_weights + relayed
+        rest = [begun, named, binning, packet, near_packet] + known + far_weights + relayed
         part = call(functools.partial(finish_kernel, chips), shape((tiles, MB, PTS), BF16))(
             in_specs=[VMEM] * (2 + len(rest)), out_specs=VMEM
         )(*its_sums, *rest)
         received.append(far(part, chips - j))
-    rest = [packet] + far_weights + [near_packet] + relayed
+    rest = known + [packet] + far_weights + [near_packet] + relayed
     image = call(
         functools.partial(own_kernel, chips), shape((tiles, MB, PTS), F32),
         [pltpu.VMEM(sums.shape, BF16)] * 2, flops=15 * work,
-    )(in_specs=[VMEM] * (8 + len(rest)), out_specs=VMEM)(
-        traces, near_traces, apertures, *made, named, scale, binning, *rest
+    )(in_specs=[VMEM] * (7 + len(rest)), out_specs=VMEM)(
+        traces, near_traces, apertures, *made, named, binning, *rest
     )
     for part in received:
         image = image + part.astype(F32)

time: 14.2 us -> 14.2 us (level)
  no operation moved by 1% of the time
where the time goes in v8:
time: 14.2 us; the launch traced here: 14 us
  starting transfers between devices  6.17 us (43%)
  Pallas kernels  3.15 us (22%)
  waiting for transfers between devices  2.56 us (18%)
  between operations  0.77 us (5%)
  local copies, waits for them, and re-layouts  0.71 us (5%)
  other arithmetic  0.67 us (5%)
    ppermute x4, starting transfers between devices, far(): lax.ppermute(x, 'off', [(i, (i // 2 + j) % chips * 2 + (i % 2 ^ turn)) fo...  6.01 us
    ppermute x4, waiting for transfers between devices, far(): lax.ppermute(x, 'off', [(i, (i // 2 + j) % chips * 2 + (i % 2 ^ turn)) fo...  2.55 us
    pallas_call x1, Pallas kernels, shards(): call(functools.partial(own_kernel, chips), shape((tiles, MB, PTS), F32),...  1.45 us
    pallas_call x1, Pallas kernels, shards(): call(functools.partial(begin_kernel, chips), (total, sums, sums, by_row,...  0.97 us
    unnamed x10, local copies, waits for them, and re-layouts  0.71 us
    pallas_call x1, Pallas kernels, shards(): call(functools.partial(finish_kernel, chips), shape((tiles, MB, PTS), BF16))  0.68 us
    add x1, other arithmetic, shards(): image = image + part.astype(F32)  0.67 us
  transfers between devices with their start and end apart: 7, of which 3 were waited for; matrix products, arithmetic and copies ran while one was open for 0% of the time, Pallas kernels for 18%

profile of v8, /device:TPU:0, one launch (start us, length us, event | category | flops | bytes accessed | tf_op | source)
XLA Modules:
  0.0 14.0 jit_solution(15354410022171930624)
XLA Ops:
  0.0 0.0 copy-start.2
  0.0 2.9 %collective-permute-start.4 = (bf16[512,128]{1,0:T(8,128)(2,1)}, bf16[512,128]{1,0:T(8,128)(2,1)S(1)}, u32[]{:S(2)}, u32[]{:S(2)}) collective-permute-start(bf16[512,128]{1,0:T(8,128)(2,1)} %bitcast.3), channel_id=1, source_target_pairs={{0,8},{4,12},{8,0},{12,4},{1,9},{5,13},{9,1},{13,5},{2,10},{6,14},... | collective-permute-start | bytes 393224 | tf_op jit(solution)/shard_map/ppermute | solution.py:231
  3.6 0.0 copy-done.2
  3.6 0.0 copy-start.1
  3.6 0.0 copy-start.3
  3.6 0.0 copy-start.4
  3.6 0.0 copy-start
  3.7 0.1 collective-permute-start.1
  3.7 0.1 collective-permute-start
  3.8 0.7 %copy-done.1 = bf16[1,4,128,128]{3,2,1,0:T(8,128)(2,1)S(1)} copy-done((bf16[1,4,128,128]{3,2,1,0:T(8,128)(2,1)S(1)}, bf16[1,4,128,128]{3,2,1,0:T(8,128)(2,1)}, u32[]{:S(2)}) %copy-start.1) | copy-done | bytes 131096
  4.5 0.0 copy-done.3
  4.5 0.0 copy-done.4
  4.5 1.4 %collective-permute-start.3 = (bf16[16,128]{1,0:T(8,128)(2,1)S(1)}, bf16[16,128]{1,0:T(8,128)(2,1)S(1)}, u32[]{:S(2)}, u32[]{:S(2)}) collective-permute-start(bf16[16,128]{1,0:T(8,128)(2,1)S(1)} %get-tuple-element.22), channel_id=1, source_target_pairs={{0,12},{4,8},{8,4},{12,0},{1,13},{5,9},{9,5},{13,1},{2,14},{6,10},... | collective-permute-start | bytes 12296 | tf_op jit(solution)/shard_map/ppermute | solution.py:231
  6.0 0.0 collective-permute-start.2
  6.0 0.7 %collective-permute-done.4.weight_ref.refs_3_.refs_4_ = bf16[512,128]{1,0:T(8,128)(2,1)S(1)} collective-permute-done((bf16[512,128]{1,0:T(8,128)(2,1)}, bf16[512,128]{1,0:T(8,128)(2,1)S(1)}, u32[]{:S(2)}, u32[]{:S(2)}) %collective-permute-start.4) | collective-permute-done | bytes 131104 | tf_op jit(solution)/shard_map/ppermute | solution.py:231
  6.7 0.0 copy-done
  6.7 0.1 collective-permute-start.5
  6.8 0.5 %collective-permute-done.1.facts_ref = bf16[16,128]{1,0:T(8,128)(2,1)S(1)} collective-permute-done((bf16[16,128]{1,0:T(8,128)(2,1)S(1)}, bf16[16,128]{1,0:T(8,128)(2,1)S(1)}, u32[]{:S(2)}, u32[]{:S(2)}) %collective-permute-start.1) | collective-permute-done | bytes 4128 | tf_op jit(solution)/shard_map/ppermute | solution.py:231
  7.3 0.0 collective-permute-done.2.near_packet_ref.refs_4_.refs_1_
  7.3 0.0 collective-permute-done.near_ref
  7.3 1.0 %shard_map.67 = (f32[512,128]{1,0:T(8,128)S(1)}, bf16[512,512]{1,0:T(8,128)(2,1)S(1)}, bf16[512,512]{1,0:T(8,128)(2,1)S(1)}, f32[256,128]{1,0:T(8,128)S(1)}, bf16[128,256]{1,0:T(8,128)(2,1)S(1)}) custom-call(bf16[128,4096]{1,0:T(8,128)(2,1)S(1)} %copy-done, bf16[128,4096]{1,0:T(8,128)(2,1)S(1)} %collective-permute-done.near_ref, ...), custom_call_target="tpu_custom_call" | custom-call | tf_op jit(solution)/shard_map/pallas_call | solution.py:272
  8.3 0.0 collective-permute-done.3.facts_ref
  8.3 0.0 collective-permute-done.5.refs_5_
  8.4 0.7 %shard_map.71 = bf16[2,128,128]{2,1,0:T(8,128)(2,1)S(1)} custom-call(bf16[512,512]{1,0:T(8,128)(2,1)S(1)} %get-tuple-element.23.hi_ref, bf16[512,512]{1,0:T(8,128)(2,1)S(1)} %get-tuple-element.24.lo_ref, f32[512,128]{1,0:T(8,128)S(1)} %get-tuple-element.21.after_ref.total_ref, f32[256,128]{1,0:T(8,128)S(1)} %get-tuple-element.19.named_ref, ...), custom_call_target="tpu_custom_call" | custom-call | tf_op jit(solution)/shard_map/pallas_call | solution.py:289
  9.0 1.6 %collective-permute-start.6 = (bf16[2,128,128]{2,1,0:T(8,128)(2,1)S(1)}, bf16[2,128,128]{2,1,0:T(8,128)(2,1)S(1)}, u32[]{:S(2)}, u32[]{:S(2)}) collective-permute-start(bf16[2,128,128]{2,1,0:T(8,128)(2,1)S(1)} %shard_map.71), channel_id=1, source_target_pairs={{0,8},{4,12},{8,0},{12,4},{1,9},{5,13},{9,1},{13,5},{2,10},{6,14},... | collective-permute-start | bytes 196616 | tf_op jit(solution)/shard_map/ppermute | solution.py:231
  10.6 1.4 %shard_map.70 = f32[2,128,128]{2,1,0:T(8,128)S(1)} custom-call(bf16[128,4096]{1,0:T(8,128)(2,1)S(1)} %copy-done, bf16[128,4096]{1,0:T(8,128)(2,1)S(1)} %collective-permute-done.near_ref, s32[2,32]{1,0:T(2,128)S(1)} %copy-done.2, bf16[32,512]{1,0:T(8,128)(2,1)S(1)} %get-tuple-element.16.spread_ref, f32[64,512]{1,0:T(8,128)S(1)} %get-tuple-element.17.code_ref, ...), custom_call_target="tpu_custom_call" | custom-call | flops 1006632960 | tf_op jit(solution)/shard_map/pallas_call | solution.py:294
  12.1 1.3 %collective-permute-done.6 = bf16[2,128,128]{2,1,0:T(8,128)(2,1)S(1)} collective-permute-done((bf16[2,128,128]{2,1,0:T(8,128)(2,1)S(1)}, bf16[2,128,128]{2,1,0:T(8,128)(2,1)S(1)}, u32[]{:S(2)}, u32[]{:S(2)}) %collective-permute-start.6) | collective-permute-done | bytes 65568 | tf_op jit(solution)/shard_map/ppermute | solution.py:231
  13.4 0.7 %convert_add_fusion = f32[2,128,128]{2,1,0:T(8,128)} fusion(f32[2,128,128]{2,1,0:T(8,128)S(1)} %shard_map.70, bf16[2,128,128]{2,1,0:T(8,128)(2,1)S(1)} %collective-permute-done.6), kind=kLoop, calls=%fused_computation | loop fusion | flops 65536 | bytes 327680 | tf_op jit(solution)/shard_map/add | solution.py:301
  (5 shorter events, 0.1 us)
Async XLA Ops:
  0.0 3.6 %copy-start.2 = (s32[2,32]{1,0:T(2,128)S(1)}, s32[2,32]{1,0:T(2,128)}, u32[]{:S(2)}) copy-start(s32[2,32]{1,0:T(2,128)} %pattern_ref.3) | copy-start | bytes 772
  0.0 6.7 %collective-permute-start.4 = (bf16[512,128]{1,0:T(8,128)(2,1)}, bf16[512,128]{1,0:T(8,128)(2,1)S(1)}, u32[]{:S(2)}, u32[]{:S(2)}) collective-permute-start(bf16[512,128]{1,0:T(8,128)(2,1)} %bitcast.3), channel_id=1, source_target_pairs={{0,8},{4,12},{8,0},{12,4},{1,9},{5,13},{9,1},{13,5},{2,10},{6,14},... | collective-permute-start | bytes 393224 | tf_op jit(solution)/shard_map/ppermute | solution.py:231
  3.6 0.9 %copy-start.1 = (bf16[1,4,128,128]{3,2,1,0:T(8,128)(2,1)S(1)}, bf16[1,4,128,128]{3,2,1,0:T(8,128)(2,1)}, u32[]{:S(2)}) copy-start(bf16[1,4,128,128]{3,2,1,0:T(8,128)(2,1)} %param.10) | copy-start | bytes 393220
  3.6 0.9 %copy-start.3 = (s32[128]{0:T(128)S(1)}, s32[128]{0:T(128)}, u32[]{:S(2)}) copy-start(s32[128]{0:T(128)} %param.8) | copy-start | bytes 1540
  3.6 0.9 %copy-start.4 = (s32[128,1]{0,1:T(1,128)S(1)}, s32[128,1]{0,1:T(1,128)}, u32[]{:S(2)}) copy-start(s32[128,1]{0,1:T(1,128)} %param.7) | copy-start | bytes 1540
  3.6 3.0 %copy-start = (bf16[128,4096]{1,0:T(8,128)(2,1)S(1)}, bf16[128,4096]{1,0:T(8,128)(2,1)}, u32[]{:S(2)}) copy-start(bf16[128,4096]{1,0:T(8,128)(2,1)} %own_ref.3) | copy-start | bytes 3145732
  3.7 3.7 %collective-permute-start.1 = (bf16[16,128]{1,0:T(8,128)(2,1)S(1)}, bf16[16,128]{1,0:T(8,128)(2,1)S(1)}, u32[]{:S(2)}, u32[]{:S(2)}) collective-permute-start(bf16[16,128]{1,0:T(8,128)(2,1)S(1)} %shard_map.64.facts_ref), channel_id=1, source_target_pairs={{0,8},{4,12},{8,0},{12,4},{1,9},{5,13},{9,1},{13,5},{2,10},{6,14},... | collective-permute-start | bytes 12296 | tf_op jit(solution)/shard_map/ppermute | solution.py:231
  3.7 3.6 %collective-permute-start = (bf16[128,4096]{1,0:T(8,128)(2,1)}, bf16[128,4096]{1,0:T(8,128)(2,1)S(1)}, u32[]{:S(2)}, u32[]{:S(2)}) collective-permute-start(bf16[128,4096]{1,0:T(8,128)(2,1)} %own_ref.3), channel_id=1, source_target_pairs={{0,4},{4,0},{8,12},{12,8},{1,5},{5,1},{9,13},{13,9},{2,6},{6,2},{1... | collective-permute-start | bytes 3145736 | tf_op jit(solution)/shard_map/ppermute | solution.py:228
  4.5 3.8 %collective-permute-start.3 = (bf16[16,128]{1,0:T(8,128)(2,1)S(1)}, bf16[16,128]{1,0:T(8,128)(2,1)S(1)}, u32[]{:S(2)}, u32[]{:S(2)}) collective-permute-start(bf16[16,128]{1,0:T(8,128)(2,1)S(1)} %get-tuple-element.22), channel_id=1, source_target_pairs={{0,12},{4,8},{8,4},{12,0},{1,13},{5,9},{9,5},{13,1},{2,14},{6,10},... | collective-permute-start | bytes 12296 | tf_op jit(solution)/shard_map/ppermute | solution.py:231
  6.0 1.4 %collective-permute-start.2 = (bf16[528,128]{1,0:T(8,128)(2,1)S(1)}, bf16[528,128]{1,0:T(8,128)(2,1)S(1)}, u32[]{:S(2)}, u32[]{:S(2)}) collective-permute-start(bf16[528,128]{1,0:T(8,128)(2,1)S(1)} %get-tuple-element.18.packet_ref.after_ref.refs_2_.refs_0_), channel_id=1, source_target_pairs={{0,4},{4,0},{8,12},{12,8},{1,5},{5,1},{9,13},{13,9},{2,6},{6,2},{1... | collective-permute-start | bytes 405512 | tf_op jit(solution)/shard_map/ppermute | solution.py:228
  6.7 1.6 %collective-permute-start.5 = (bf16[512,128]{1,0:T(8,128)(2,1)S(1)}, bf16[512,128]{1,0:T(8,128)(2,1)S(1)}, u32[]{:S(2)}, u32[]{:S(2)}) collective-permute-start(bf16[512,128]{1,0:T(8,128)(2,1)S(1)} %shard_map.69), channel_id=1, source_target_pairs={{0,4},{4,0},{8,12},{12,8},{1,5},{5,1},{9,13},{13,9},{2,6},{6,2},{1... | collective-permute-start | bytes 393224 | tf_op jit(solution)/shard_map/ppermute | solution.py:228
  9.0 4.3 %collective-permute-start.6 = (bf16[2,128,128]{2,1,0:T(8,128)(2,1)S(1)}, bf16[2,128,128]{2,1,0:T(8,128)(2,1)S(1)}, u32[]{:S(2)}, u32[]{:S(2)}) collective-permute-start(bf16[2,128,128]{2,1,0:T(8,128)(2,1)S(1)} %shard_map.71), channel_id=1, source_target_pairs={{0,8},{4,12},{8,0},{12,4},{1,9},{5,13},{9,1},{13,5},{2,10},{6,14},... | collective-permute-start | bytes 196616 | tf_op jit(solution)/shard_map/ppermute | solution.py:231
